TPU v7x, 32 devices: a whole 2x2x4 slice. The times are simulated.
32 devices in a mesh: narrow: 4 (over y, x), wide: 8 (over z, core).
Axes of the slice: x: 2, y: 2, z: 4, core: 2. Of those that a mesh axis runs over, the one named last changes fastest.
Arguments:
- tokens: bfloat16 [32768, 1024], P(('narrow', 'wide')), may hold values from -6 to 6
- norm_gains: float32 [2, 1024], replicated, may hold values from 0.25 to 1.75
- norm_biases: float32 [2, 1024], replicated, may hold values from -2 to 2
- w_qkv: bfloat16 [1024, 3072], replicated, may hold values from -0.25 to 0.25
- w_attn_out: bfloat16 [1024, 1024], replicated, may hold values from -0.75 to 0.75
- w_in: bfloat16 [8, 1024, 4096], P('wide'), may hold values from -0.1875 to 0.1875
- w_out: bfloat16 [8, 4096, 1024], P('wide'), may hold values from -0.09375 to 0.09375
- segment_ids: int32 [32, 1024], P(('narrow', 'wide')), may hold values from 0 to 3, never falling along the last dimension, each value on 1 to 512 neighbouring positions
- expert_ids: int32 [32768], P(('narrow', 'wide')), may hold values from 0 to 7, as said below
- slots: int32 [32768], P(('narrow', 'wide')), may hold values from 0 to 144, as said below
- cotangent: bfloat16 [32768, 1024], P(('narrow', 'wide')), may hold values from -6 to 6
Outputs:
- mixed: bfloat16 [32768, 1024], P(('narrow', 'wide'))
- d_tokens: float32 [32768, 1024], P(('narrow', 'wide'))
- d_norm_gains: float32 [2, 1024], P(None, ('narrow', 'wide'))
- d_norm_biases: float32 [2, 1024], P(None, ('narrow', 'wide'))
- d_w_qkv: float32 [1024, 3072], P(None, ('narrow', 'wide'))
- d_w_attn_out: float32 [1024, 1024], P(None, ('narrow', 'wide'))
- d_w_in: float32 [8, 1024, 4096], P('wide', None, 'narrow')
- d_w_out: float32 [8, 4096, 1024], P('wide', 'narrow')
Inputs may be any that keep to these rules, and one draw needn't show every extreme that they name: `expert_ids`: each token's expert, from a hash of the token. The number of earlier tokens of the same device that have the same expert, or 144 where that number is 144 or more (the token is dropped); so the retained tokens of one device and expert hold slots 0, 1, 2, ... without gaps, and on every device some expert fills all 144 slots.
All inputs are finite; a program needn't handle non-finite values.
Results may differ from a plain program's by a relative error of at most 0.012.
The roundings to bfloat16 on the way count: a program that leaves them out, or rounds other values in their place, can miss the bound.
Values may be sent and summed in bfloat16 or wider, within the bound.
No kernel may reach another device: no remote copies, remote signals or barrier semaphores. Data moves between devices by JAX's collectives and lax.ppermute only.
A program may use at most 320 MiB of HBM per device.

v0:
```python
import jax
import jax.numpy as jnp
from jax import lax
from jax.sharding import PartitionSpec as P

HEADS = 16


EPSILON = 1e-05
NEGATIVE = -1e30


def layer_norm(stream, norm_gain, norm_bias):
    average = jnp.mean(stream, axis=-1, keepdims=True)
    centered = stream - average
    inverse = lax.rsqrt(jnp.mean(centered * centered, axis=-1, keepdims=True) + EPSILON)
    return centered * inverse * norm_gain + norm_bias


def contract_rows(first_mat, second_mat):
    return lax.dot_general(
        first_mat, second_mat, (((0,), (0,)), ((), ())), preferred_element_type=jnp.float32
    )


def contract_cols(first_mat, second_mat):
    return lax.dot_general(
        first_mat, second_mat, (((1,), (1,)), ((), ())), preferred_element_type=jnp.float32
    )


def on_device(
    tokens,
    norm_gains,
    norm_biases,
    w_qkv,
    w_attn_out,
    w_in,
    w_out,
    segment_ids,
    expert_ids,
    slots,
    cotangent,
):
    tok_count, model_width = tokens.shape
    seq_count, seq_len = segment_ids.shape
    head_dim = model_width // HEADS
    score_scale = head_dim ** (-0.5)
    block_rows = min(512, seq_len)
    seq_blocks = seq_len // block_rows
    block_count = seq_count * seq_blocks
    wide_size = lax.axis_size("wide")
    local_experts = w_in.shape[0]
    experts_all = local_experts * wide_size
    capacity = tok_count * 9 // (8 * experts_all)
    stream = tokens.astype(jnp.float32)
    normed, first_back = jax.vjp(layer_norm, stream, norm_gains[0], norm_biases[0])
    normed_low = normed.astype(jnp.bfloat16)
    projected = jnp.dot(normed_low, w_qkv, preferred_element_type=jnp.float32).astype(jnp.bfloat16)
    query_rows, key_rows, value_rows = [
        part_rows.reshape(seq_count, seq_len, HEADS, head_dim)
        for part_rows in jnp.split(projected, 3, axis=1)
    ]
    positions = jnp.arange(seq_len, dtype=jnp.int32)

    def block_scores(block_index):
        seq_index = block_index // seq_blocks
        row_first = block_index % seq_blocks * block_rows
        query_seq = lax.dynamic_index_in_dim(query_rows, seq_index, 0, keepdims=False)
        query_block = lax.dynamic_slice_in_dim(query_seq, row_first, block_rows, 0)
        key_seq = lax.dynamic_index_in_dim(key_rows, seq_index, 0, keepdims=False)
        value_seq = lax.dynamic_index_in_dim(value_rows, seq_index, 0, keepdims=False)
        doc_ids = lax.dynamic_index_in_dim(segment_ids, seq_index, 0, keepdims=False)
        query_pos = row_first + positions[:block_rows]
        query_docs = lax.dynamic_slice_in_dim(doc_ids, row_first, block_rows, 0)
        allowed = (positions[None, :] <= query_pos[:, None]) & (
            doc_ids[None, :] == query_docs[:, None]
        )
        scores = (
            jnp.einsum("qhd,khd->hqk", query_block, key_seq, preferred_element_type=jnp.float32)
            * score_scale
        )
        scores = jnp.where(allowed[None], scores, NEGATIVE)
        return (scores, query_block, key_seq, value_seq)

    def attend_forward(block_index):
        scores, query_block, key_seq, value_seq = block_scores(block_index)
        row_max = jnp.max(scores, axis=-1, keepdims=True)
        exponent = jnp.exp(scores - row_max)
        row_total = jnp.sum(exponent, axis=-1, keepdims=True)
        attn_prob = (exponent / row_total).astype(jnp.bfloat16)
        head_out = jnp.einsum(
            "hqk,khd->qhd", attn_prob, value_seq, preferred_element_type=jnp.float32
        )
        return (head_out.astype(jnp.bfloat16), (row_max + jnp.log(row_total))[..., 0])

    head_blocks, log_totals = lax.map(attend_forward, jnp.arange(block_count, dtype=jnp.int32))
    mixed_heads = head_blocks.reshape(tok_count, model_width)
    middle = stream + jnp.dot(mixed_heads, w_attn_out, preferred_element_type=jnp.float32)
    second, second_back = jax.vjp(layer_norm, middle, norm_gains[1], norm_biases[1])
    sent_rows = second.astype(jnp.bfloat16)
    retained = slots < capacity
    flat_slot = jnp.where(retained, expert_ids * capacity + slots, experts_all * capacity)
    dispatch = (
        jnp.zeros((experts_all * capacity, model_width), jnp.bfloat16)
        .at[flat_slot]
        .set(sent_rows, mode="drop")
    )
    dispatch = dispatch.reshape(experts_all, capacity, model_width)
    received = lax.all_to_all(dispatch, "wide", split_axis=0, concat_axis=0, tiled=True)
    slot_count = received.shape[1]
    grouped = received.reshape(wide_size, local_experts, slot_count, model_width)
    expert_index = 0
    rows_flat = grouped[:, expert_index].reshape(wide_size * slot_count, model_width)
    preact = jnp.dot(rows_flat, w_in[expert_index], preferred_element_type=jnp.float32)
    hidden = jax.nn.gelu(preact).astype(jnp.bfloat16)
    produced = jnp.dot(hidden, w_out[expert_index], preferred_element_type=jnp.float32).astype(
        jnp.bfloat16
    )
    outputs = produced.reshape(wide_size, 1, slot_count, model_width)
    produced_all = outputs.reshape(experts_all, slot_count, model_width)
    returned, received = (
        lax.all_to_all(produced_all, "wide", split_axis=0, concat_axis=0, tiled=True),
        received,
    )
    expert_part = jnp.take(
        returned.reshape(experts_all * capacity, model_width),
        flat_slot,
        axis=0,
        mode="fill",
        fill_value=0,
    ).astype(jnp.float32)
    mixed = (middle + expert_part).astype(jnp.bfloat16)
    grad_out = cotangent.astype(jnp.float32)
    grad_dispatch = (
        jnp.zeros((experts_all * capacity, model_width), jnp.bfloat16)
        .at[flat_slot]
        .set(cotangent, mode="drop")
    )
    grad_recv = lax.all_to_all(
        grad_dispatch.reshape(experts_all, capacity, model_width),
        "wide",
        split_axis=0,
        concat_axis=0,
        tiled=True,
    )
    rows_in = lax.all_to_all(dispatch, "wide", split_axis=0, concat_axis=0, tiled=True)

    def by_expert(packed):
        return (
            packed.reshape(wide_size, local_experts, capacity, -1)
            .transpose(1, 0, 2, 3)
            .reshape(local_experts, wide_size * capacity, -1)
        )

    expert_rows = by_expert(rows_in)
    expert_grads = by_expert(grad_recv)
    expert_index = 0
    rows_one = expert_rows[expert_index]
    preact_one = jnp.dot(rows_one, w_in[expert_index], preferred_element_type=jnp.float32)
    hidden_one, gelu_one = jax.vjp(jax.nn.gelu, preact_one)
    grad_hidden_one = contract_cols(expert_grads[expert_index], w_out[expert_index])
    grad_preact_one = gelu_one(grad_hidden_one)[0].astype(jnp.bfloat16)
    hidden_list = [hidden_one.astype(jnp.bfloat16)]
    preact_list = [grad_preact_one]
    row_list = [contract_cols(grad_preact_one, w_in[expert_index]).astype(jnp.bfloat16)]
    hidden_low = jnp.stack(hidden_list)
    grad_preact = jnp.stack(preact_list)
    grad_rows = jnp.stack(row_list)
    hidden_cols, preact_cols = (
        lax.all_to_all(hidden_low, "narrow", split_axis=2, concat_axis=1, tiled=True),
        lax.all_to_all(grad_preact, "narrow", split_axis=2, concat_axis=1, tiled=True),
    )
    rows_part = lax.all_gather(expert_rows, "narrow", axis=1, tiled=True)
    grads_part = lax.all_gather(expert_grads, "narrow", axis=1, tiled=True)
    in_new = jnp.stack([contract_rows(rows_part[0], preact_cols[0])])
    out_new = jnp.stack([contract_rows(hidden_cols[0], grads_part[0])])
    grad_rows = (
        grad_rows.reshape(local_experts, wide_size, capacity, model_width)
        .transpose(1, 0, 2, 3)
        .reshape(experts_all, capacity, model_width)
    )
    grad_back = lax.all_to_all(grad_rows, "wide", split_axis=0, concat_axis=0, tiled=True)
    grad_sent = jnp.take(
        grad_back.reshape(experts_all * capacity, model_width),
        flat_slot,
        axis=0,
        mode="fill",
        fill_value=0,
    ).astype(jnp.float32)
    grad_middle_norm, grad_gain_two, grad_bias_two = second_back(grad_sent)
    grad_middle = grad_out + grad_middle_norm
    grad_attn = grad_middle.astype(jnp.bfloat16)
    grad_out_proj = contract_rows(mixed_heads, grad_attn)
    grad_heads = (
        contract_cols(grad_attn, w_attn_out)
        .astype(jnp.bfloat16)
        .reshape(block_count, block_rows, HEADS, head_dim)
    )

    def seq_back(seq_index):

        def attend_back(running, inner):
            key_grad, value_grad = running
            block_index = seq_index * seq_blocks + inner
            scores, query_block, key_seq, value_seq = block_scores(block_index)
            prob_full = jnp.exp(scores - log_totals[block_index][..., None])
            prob_low = prob_full.astype(jnp.bfloat16)
            head_grad = grad_heads[block_index]
            value_part = jnp.einsum(
                "hqk,qhd->khd", prob_low, head_grad, preferred_element_type=jnp.float32
            )
            prob_grad = jnp.einsum(
                "qhd,khd->hqk", head_grad, value_seq, preferred_element_type=jnp.float32
            )
            score_grad = (
                prob_full * (prob_grad - jnp.sum(prob_full * prob_grad, axis=-1, keepdims=True))
            ).astype(jnp.bfloat16)
            query_part = (
                jnp.einsum("hqk,khd->qhd", score_grad, key_seq, preferred_element_type=jnp.float32)
                * score_scale
            )
            key_part = (
                jnp.einsum(
                    "hqk,qhd->khd", score_grad, query_block, preferred_element_type=jnp.float32
                )
                * score_scale
            )
            return ((key_grad + key_part, value_grad + value_part), query_part)

        zero_one = jnp.zeros((seq_len, HEADS, head_dim), jnp.float32)
        (key_one, value_one), query_one = lax.scan(
            attend_back, (zero_one, zero_one), jnp.arange(seq_blocks, dtype=jnp.int32)
        )
        return (
            query_one.reshape(seq_len, model_width),
            key_one.reshape(seq_len, model_width),
            value_one.reshape(seq_len, model_width),
        )

    query_grad, key_grad, value_grad = lax.map(seq_back, jnp.arange(seq_count, dtype=jnp.int32))
    grad_projected = jnp.concatenate(
        [
            query_grad.reshape(tok_count, model_width),
            key_grad.reshape(tok_count, model_width),
            value_grad.reshape(tok_count, model_width),
        ],
        axis=1,
    ).astype(jnp.bfloat16)
    grad_qkv_w = contract_rows(normed_low, grad_projected)
    grad_normed = contract_cols(grad_projected, w_qkv)
    grad_stream_norm, grad_gain_one, grad_bias_one = first_back(grad_normed)
    grad_tokens = grad_middle + grad_stream_norm
    gain_grads = jnp.stack([grad_gain_one, grad_gain_two])
    bias_grads = jnp.stack([grad_bias_one, grad_bias_two])
    grad_qkv_w, grad_out_proj, gain_grads, bias_grads = (
        lax.psum_scatter(grad_qkv_w, ("narrow", "wide"), scatter_dimension=1, tiled=True),
        lax.psum_scatter(grad_out_proj, ("narrow", "wide"), scatter_dimension=1, tiled=True),
        lax.psum_scatter(gain_grads, ("narrow", "wide"), scatter_dimension=1, tiled=True),
        lax.psum_scatter(bias_grads, ("narrow", "wide"), scatter_dimension=1, tiled=True),
    )
    return (mixed, grad_tokens, gain_grads, bias_grads, grad_qkv_w, grad_out_proj, in_new, out_new)


def solution(mesh):
    placed = (
        P(("narrow", "wide"), None),
        P(),
        P(),
        P(),
        P(),
        P("wide", None, None),
        P("wide", None, None),
        P(("narrow", "wide"), None),
        P(("narrow", "wide")),
        P(("narrow", "wide")),
        P(("narrow", "wide"), None),
    )
    return jax.shard_map(
        on_device,
        mesh=mesh,
        in_specs=placed,
        out_specs=(
            P(("narrow", "wide"), None),
            P(("narrow", "wide"), None),
            P(None, ("narrow", "wide")),
            P(None, ("narrow", "wide")),
            P(None, ("narrow", "wide")),
            P(None, ("narrow", "wide")),
            P("wide", None, "narrow"),
            P("wide", "narrow", None),
        ),
        check_vma=False,
    )
```

profile of v0, /device:TPU:0, one launch (start us, length us, event | category | flops | bytes accessed | tf_op | source)
XLA Modules:
  0.0 1462.9 jit_solution(10887689991200647148)
XLA Ops:
  8.1 4.1 copy.70
  18.3 10.3 convolution_convert_fusion
  43.3 102.5 %while.45 = (s32[]{:T(128)}, bf16[2,512,16,64]{1,3,2,0:T(8,128)(2,1)}, f32[2,16,512]{2,1,0:T(8,128)}, s32[1024]{0:T(1024)S(1)}, s32[2]{0:T(128)S(1)}, /*index=5*...) while((s32[]{:T(128)}, ...), condition=%wide.region_5.6_spmd.clone, body=%wide.region_2.5_spmd.clone.sunk | while | flops 2250236416 | bytes 117724504 | solution.py:97
  48.0 15.6 %fusion.147 = (f32[16,512]{1,0:T(8,128)S(1)}, f32[16,512,1024]{2,1,0:T(8,128)}) fusion(pred[512,1024]{1,0:T(8,128)(4,1)S(1)} %compare_and_fusion.5, bf16[1,1024,16,64]{1,3,2,0:T(8,128)(2,1)} %get-tuple-element.778, bf16[1,1024,16,64]{1,3,2,0:T(8,128)(2,1)} %get-tuple-element.777, s32[]{:T(128)S(6)} %select_n.167), kind=kOutput, calls=%fused_computation.7.clone.1 | convolution fusion | flops 1098899456 | bytes 37257220 | tf_op jit(solution)/shard_map/while/body/eval_jaxpr/qhd,khd->hqk/dot_general | solution.py:80
  63.6 15.1 %fusion.148 = f32[16,512]{1,0:T(8,128)S(1)} fusion(f32[16,512,1024]{2,1,0:T(8,128)} %get-tuple-element.727, f32[16,512]{1,0:T(8,128)S(1)} %get-tuple-element.728, pred[512,1024]{1,0:T(8,128)(4,1)S(1)} %compare_and_fusion.5), kind=kLoop, calls=%fused_computation.8.clone.1 | loop fusion | flops 33546240 | bytes 34144256 | tf_op jit(solution)/shard_map/while/body/eval_jaxpr/reduce_sum | solution.py:90
  79.3 15.2 %fusion.149 = bf16[2,512,16,64]{1,3,2,0:T(8,128)(2,1)} fusion(bf16[2,512,16,64]{1,3,2,0:T(8,128)(2,1)} %get-tuple-element.758, s32[]{:T(128)} %get-tuple-element.757, bf16[1,1024,16,64]{1,3,2,0:T(8,128)(2,1)S(1)} %copy-done.4, f32[16,512,1024]{2,1,0:T(8,128)} %get-tuple-element.727, f32[16,512]{1,0:T(8,128)S(1)} %fusion.148, ...), kind=kOutput, calls=%fused_computation.16.clone.1 | convolution fusion | flops 1116209152 | bytes 37290496 | tf_op jit(solution)/shard_map/while/body/eval_jaxpr/hqk,khd->qhd/dot_general | solution.py:92
  98.9 15.6 %fusion.147 = (f32[16,512]{1,0:T(8,128)S(1)}, f32[16,512,1024]{2,1,0:T(8,128)}) fusion(pred[512,1024]{1,0:T(8,128)(4,1)S(1)} %compare_and_fusion.5, bf16[1,1024,16,64]{1,3,2,0:T(8,128)(2,1)} %get-tuple-element.778, bf16[1,1024,16,64]{1,3,2,0:T(8,128)(2,1)} %get-tuple-element.777, s32[]{:T(128)S(6)} %select_n.167), kind=kOutput, calls=%fused_computation.7.clone.1 | convolution fusion | flops 1098899456 | bytes 37257220 | tf_op jit(solution)/shard_map/while/body/eval_jaxpr/qhd,khd->hqk/dot_general | solution.py:80
  114.5 15.1 %fusion.148 = f32[16,512]{1,0:T(8,128)S(1)} fusion(f32[16,512,1024]{2,1,0:T(8,128)} %get-tuple-element.727, f32[16,512]{1,0:T(8,128)S(1)} %get-tuple-element.728, pred[512,1024]{1,0:T(8,128)(4,1)S(1)} %compare_and_fusion.5), kind=kLoop, calls=%fused_computation.8.clone.1 | loop fusion | flops 33546240 | bytes 34144256 | tf_op jit(solution)/shard_map/while/body/eval_jaxpr/reduce_sum | solution.py:90
  130.2 15.2 %fusion.149 = bf16[2,512,16,64]{1,3,2,0:T(8,128)(2,1)} fusion(bf16[2,512,16,64]{1,3,2,0:T(8,128)(2,1)} %get-tuple-element.758, s32[]{:T(128)} %get-tuple-element.757, bf16[1,1024,16,64]{1,3,2,0:T(8,128)(2,1)S(1)} %copy-done.4, f32[16,512,1024]{2,1,0:T(8,128)} %get-tuple-element.727, f32[16,512]{1,0:T(8,128)S(1)} %fusion.148, ...), kind=kOutput, calls=%fused_computation.16.clone.1 | convolution fusion | flops 1116209152 | bytes 37290496 | tf_op jit(solution)/shard_map/while/body/eval_jaxpr/hqk,khd->qhd/dot_general | solution.py:92
  160.9 7.6 scatter_custom_fusion
  168.5 6.6 all-to-all-start
  175.1 7.6 scatter_custom_fusion.1
  182.7 47.1 %all-to-all-done = bf16[8,144,1024]{2,1,0:T(8,128)(2,1)} async-done(((bf16[8,144,1024]{2,1,0:T(8,128)(2,1)}), bf16[8,144,1024]{2,1,0:T(8,128)(2,1)}, u32[]{:S(2)}, u32[]{:S(2)}) %all-to-all-start) | async-done | bytes 2359328 | tf_op jit(solution)/shard_map/all_to_all | solution.py:110
  229.8 4.4 all-to-all-start.2
  234.2 16.8 %fusion.67 = f32[1152,4096]{1,0:T(8,128)} fusion(bf16[1152,1024]{1,0:T(8,128)(2,1)} %bitcast.8, bf16[1,1024,4096]{2,1,0:T(8,128)(2,1)} %param.22), kind=kOutput, calls=%fused_computation.78 | convolution fusion | flops 9663676416 | bytes 29622272 | tf_op jit(solution)/shard_map/dot_general | solution.py:115
  251.0 37.9 %all-to-all-done.2 = bf16[8,144,1024]{2,1,0:T(8,128)(2,1)} async-done(((bf16[8,144,1024]{2,1,0:T(8,128)(2,1)}), bf16[8,144,1024]{2,1,0:T(8,128)(2,1)}, u32[]{:S(2)}, u32[]{:S(2)}) %all-to-all-start.2) | async-done | bytes 2359328 | tf_op jit(solution)/shard_map/all_to_all | solution.py:140
  288.9 27.0 %fusion.54 = bf16[1152,4096]{1,0:T(8,128)(2,1)} fusion(f32[1152,4096]{1,0:T(8,128)} %fusion.67, bf16[1152,1024]{1,0:T(8,128)(2,1)} %bitcast.14, bf16[1,4096,1024]{2,1,0:T(8,128)(2,1)} %param.23), kind=kOutput, calls=%fused_computation.66 | convolution fusion | flops 9758048256 | bytes 39059456 | tf_op jit(solution)/shard_map/dot_general | solution.py:27
  315.9 16.4 %fusion.84 = bf16[1152,1024]{1,0:T(8,128)(2,1)} fusion(bf16[1152,4096]{1,0:T(8,128)(2,1)} %fusion.54, bf16[1,1024,4096]{2,1,0:T(8,128)(2,1)} %param.22), kind=kOutput, calls=%fused_computation.110 | convolution fusion | flops 9664856064 | bytes 20185088 | tf_op jit(solution)/shard_map/dot_general | solution.py:27
  332.3 4.4 all-to-all-start.3
  340.7 50.7 %all-to-all-done.3 = bf16[8,144,1024]{2,1,0:T(8,128)(2,1)} async-done(((bf16[8,144,1024]{2,1,0:T(8,128)(2,1)}), bf16[8,144,1024]{2,1,0:T(8,128)(2,1)}, u32[]{:S(2)}, u32[]{:S(2)}) %all-to-all-start.3) | async-done | bytes 2359328 | tf_op jit(solution)/shard_map/all_to_all | solution.py:183
  391.4 8.0 gather_fusion.1
  418.4 6.4 reshape.372
  424.8 5.6 copy.80
  430.4 229.0 %while.46 = (s32[]{:T(128)}, f32[1024,16,64]{0,2,1:T(8,128)}, f32[1024,16,64]{0,2,1:T(8,128)}, bf16[2,512,16,64]{1,3,2,0:T(8,128)(2,1)}, s32[2]{0:T(128)S(1)}, /...) while((s32[]{:T(128)}, f32[1024,16,64]{0,2,1:T(8,128)}, ...), condition=%wide.region_14.16_spmd.clone.clone, body=%wide.region_12.15_spmd.clone.clone.sunk | while | flops 5501870592 | bytes 283366272 | solution.py:232
  433.1 14.4 fusion.158
  451.4 25.9 %multiply_reduce_fusion.3 = (f32[16,512]{1,0:T(8,128)S(1)}, f32[16,512,1024]{2,1,0:T(8,128)}) fusion(f32[16,512,1024]{2,1,0:T(8,128)} %fusion.158, f32[16,512]{1,0:T(8,128)S(1)} %dynamic-slice_bitcast_fusion.2, pred[512,1024]{1,0:T(8,128)(4,1)S(1)} %compare_and_fusion.6, bf16[1,1024,16,64]{1,3,2,0:T(8,128)(2,1)} %get-tuple-element.830, ...), kind=kOutput, calls=%fused_computation.26.clone.1 | convolution fusion | flops 1115676672 | bytes 70844416 | tf_op jit(solution)/shard_map/while/body/eval_jaxpr/while/body/eval_jaxpr/qhd,khd->hqk/dot_general | solution.py:213
  477.4 27.8 %multiply_convert_fusion.4 = bf16[16,512,1024]{2,1,0:T(8,128)(2,1)} fusion(f32[16,512,1024]{2,1,0:T(8,128)} %get-tuple-element.741, f32[16,512,1024]{2,1,0:T(8,128)} %fusion.158, f32[16,512]{1,0:T(8,128)S(1)} %get-tuple-element.742, f32[16,512]{1,0:T(8,128)S(1)} %dynamic-slice_bitcast_fusion.2, pred[512,1024]{1,0:T(8,128)(4,1)S(1)} %compare_and_fusion.6), kind=kLoop, calls=%fused_computation.25.clone.1 | loop fusion | flops 50331648 | bytes 84475904 | tf_op jit(solution)/shard_map/while/body/eval_jaxpr/while/body/eval_jaxpr/convert_element_type | solution.py:218
  505.2 11.2 bitcast_add_fusion.4
  516.3 9.7 bitcast_dynamic-update-slice_fusion.5
  526.1 17.5 %bitcast_add_fusion.5 = f32[1024,16,64]{0,2,1:T(8,128)} fusion(f32[1024,16,64]{0,2,1:T(8,128)} %get-tuple-element.804, f32[16,512,1024]{2,1,0:T(8,128)} %fusion.158, f32[16,512]{1,0:T(8,128)S(1)} %dynamic-slice_bitcast_fusion.2, pred[512,1024]{1,0:T(8,128)(4,1)S(1)} %compare_and_fusion.6, pred[]{:T(512)S(6)} %compare.10, ...), kind=kOutput, calls=%fused_computation.31.clone.1 | convolution fusion | flops 1109393408 | bytes 43548676 | tf_op jit(solution)/shard_map/while/body/eval_jaxpr/while/body/eval_jaxpr/hqk,qhd->khd/dot_general | solution.py:210
  546.1 14.4 fusion.158
  564.4 25.9 %multiply_reduce_fusion.3 = (f32[16,512]{1,0:T(8,128)S(1)}, f32[16,512,1024]{2,1,0:T(8,128)}) fusion(f32[16,512,1024]{2,1,0:T(8,128)} %fusion.158, f32[16,512]{1,0:T(8,128)S(1)} %dynamic-slice_bitcast_fusion.2, pred[512,1024]{1,0:T(8,128)(4,1)S(1)} %compare_and_fusion.6, bf16[1,1024,16,64]{1,3,2,0:T(8,128)(2,1)} %get-tuple-element.830, ...), kind=kOutput, calls=%fused_computation.26.clone.1 | convolution fusion | flops 1115676672 | bytes 70844416 | tf_op jit(solution)/shard_map/while/body/eval_jaxpr/while/body/eval_jaxpr/qhd,khd->hqk/dot_general | solution.py:213
  590.3 27.8 %multiply_convert_fusion.4 = bf16[16,512,1024]{2,1,0:T(8,128)(2,1)} fusion(f32[16,512,1024]{2,1,0:T(8,128)} %get-tuple-element.741, f32[16,512,1024]{2,1,0:T(8,128)} %fusion.158, f32[16,512]{1,0:T(8,128)S(1)} %get-tuple-element.742, f32[16,512]{1,0:T(8,128)S(1)} %dynamic-slice_bitcast_fusion.2, pred[512,1024]{1,0:T(8,128)(4,1)S(1)} %compare_and_fusion.6), kind=kLoop, calls=%fused_computation.25.clone.1 | loop fusion | flops 50331648 | bytes 84475904 | tf_op jit(solution)/shard_map/while/body/eval_jaxpr/while/body/eval_jaxpr/convert_element_type | solution.py:218
  618.1 12.4 bitcast_add_fusion.4
  630.5 9.8 bitcast_dynamic-update-slice_fusion.5
  640.3 18.7 %bitcast_add_fusion.5 = f32[1024,16,64]{0,2,1:T(8,128)} fusion(f32[1024,16,64]{0,2,1:T(8,128)} %get-tuple-element.804, f32[16,512,1024]{2,1,0:T(8,128)} %fusion.158, f32[16,512]{1,0:T(8,128)S(1)} %dynamic-slice_bitcast_fusion.2, pred[512,1024]{1,0:T(8,128)(4,1)S(1)} %compare_and_fusion.6, pred[]{:T(512)S(6)} %compare.10, ...), kind=kOutput, calls=%fused_computation.31.clone.1 | convolution fusion | flops 1109393408 | bytes 43548676 | tf_op jit(solution)/shard_map/while/body/eval_jaxpr/while/body/eval_jaxpr/hqk,qhd->khd/dot_general | solution.py:210
  670.2 8.4 fusion.116
  679.8 5.5 copy.82
  693.1 6.6 fusion.117
  699.7 20.8 %fusion.87 = bf16[1152,1024]{1,0:T(8,128)(2,1)} fusion(bf16[1,4096,1024]{2,1,0:T(8,128)(2,1)} %param.23, f32[1152,4096]{1,0:T(8,128)} %fusion.67), kind=kOutput, calls=%fused_computation.111 | convolution fusion | flops 9707323392 | bytes 29622272 | tf_op jit(solution)/shard_map/dot_general | solution.py:117
  720.5 4.4 all-to-all-start.1
  724.9 41.6 %copy.84 = bf16[1,1152,4096]{1,0,2:T(2,128)(2,1)} copy(bf16[1,1152,4096]{2,1,0:T(8,128)(2,1)} %bitcast.221) | data formatting | bytes 18874368 | tf_op jit(solution)/shard_map/stack | solution.py:168
  767.0 201.4 %reduce = bf16[4096,1152]{1,0:T(8,128)(2,1)} reduce(bf16[4096,1,1152]{2,1,0:T(2,128)(2,1)} %bitcast.217, bf16[]{:T(256)} %broadcast.353), dimensions={1}, to_apply=%bitcast.137.reduce_sub_computation | reduce | bytes 18874370
  968.4 8.5 reshape.381
  976.9 5.8 all-to-all-start.4
  983.0 14.4 fusion.91
  997.4 14.2 fusion.111
  1011.6 41.4 %copy.86 = bf16[1,1152,4096]{1,0,2:T(2,128)(2,1)} copy(bf16[1,1152,4096]{2,1,0:T(8,128)(2,1)} %fusion.111) | data formatting | bytes 18874368 | tf_op jit(solution)/shard_map/stack | solution.py:167
  1053.0 201.3 %reduce.1 = bf16[4096,1152]{1,0:T(8,128)(2,1)} reduce(bf16[4096,1,1152]{2,1,0:T(2,128)(2,1)} %bitcast.218, bf16[]{:T(256)} %broadcast.353), dimensions={1}, to_apply=%bitcast.139.reduce_sub_computation | reduce | bytes 18874370
  1254.3 8.5 reshape.383
  1262.8 5.9 all-to-all-start.5
  1268.7 8.0 gather_fusion
  1276.7 4.0 copy.76
  1280.8 8.9 add_add_fusion.2
  1289.6 5.5 copy.89
  1300.4 23.2 %reshape.382 = bf16[4096,1,1152]{2,1,0:T(2,128)(2,1)} reshape(bf16[4,2,589824]{2,1,0:T(2,128)(2,1)} %all-to-all-done.4) | data formatting | bytes 18874368
  1323.6 14.1 copy.96
  1337.7 12.7 copy.85
  1350.4 22.7 %all-to-all-done.5 = bf16[4,2,589824]{2,1,0:T(2,128)(2,1)} async-done(((bf16[4,2,589824]{2,1,0:T(2,128)(2,1)}), bf16[4,2,589824]{2,1,0:T(2,128)(2,1)}, u32[]{:S(2)}, u32[]{:S(2)}) %all-to-all-start.5) | async-done | bytes 9437216 | tf_op jit(solution)/shard_map/all_to_all | solution.py:171
  1373.1 23.2 %reshape.384 = bf16[4096,1,1152]{2,1,0:T(2,128)(2,1)} reshape(bf16[4,2,589824]{2,1,0:T(2,128)(2,1)} %all-to-all-done.5) | data formatting | bytes 18874368
  1396.4 14.3 copy.97
  1410.7 12.7 copy.87
  1423.4 16.0 %fusion.93 = f32[1,1024,1024]{2,1,0:T(8,128)} fusion(bf16[4608,1024]{1,0:T(8,128)(2,1)} %bitcast.222, bf16[1,4608,1024]{2,1,0:T(8,128)(2,1)} %all-gather.3.cloned.1.call-done), kind=kOutput, calls=%fused_computation.115 | convolution fusion | flops 9663676416 | bytes 23068672 | tf_op jit(solution)/shard_map/dot_general | solution.py:21
  1439.4 16.2 %fusion.96 = f32[1,1024,1024]{2,1,0:T(8,128)} fusion(bf16[4608,1024]{1,0:T(8,128)(2,1)} %bitcast.223, bf16[1,4608,1024]{2,1,0:T(8,128)(2,1)} %all-gather.5.cloned.1.call-done), kind=kOutput, calls=%fused_computation.116 | convolution fusion | flops 9663676416 | bytes 23068672 | tf_op jit(solution)/shard_map/dot_general | solution.py:21
  (199 shorter events, 97.2 us)
Async XLA Ops:
  8.0 142.3 %copy-start = (bf16[1024,1024]{1,0:T(8,128)(2,1)S(1)}, bf16[1024,1024]{1,0:T(8,128)(2,1)}, u32[]{:S(2)}) copy-start(bf16[1024,1024]{1,0:T(8,128)(2,1)} %param.21) | copy-start | bytes 6291460
  8.0 8.5 copy-start.45
  8.0 9.1 copy-start.46
  12.2 6.2 copy-start.7
  14.3 3.5 copy-start.26
  16.5 1.2 copy-start.34
  16.5 1.2 copy-start.38
  17.1 0.6 copy-start.30
  63.6 15.7 %copy-start.4 = (bf16[1,1024,16,64]{1,3,2,0:T(8,128)(2,1)S(1)}, bf16[1,1024,16,64]{1,3,2,0:T(8,128)(2,1)}, u32[]{:S(2)}) copy-start(bf16[1,1024,16,64]{1,3,2,0:T(8,128)(2,1)} %get-tuple-element.779) | copy-start | bytes 6291460 | tf_op jit(solution)/shard_map/while
  114.5 15.7 %copy-start.4 = (bf16[1,1024,16,64]{1,3,2,0:T(8,128)(2,1)S(1)}, bf16[1,1024,16,64]{1,3,2,0:T(8,128)(2,1)}, u32[]{:S(2)}) copy-start(bf16[1,1024,16,64]{1,3,2,0:T(8,128)(2,1)} %get-tuple-element.779) | copy-start | bytes 6291460 | tf_op jit(solution)/shard_map/while
  145.8 4.5 copy-start.8
  150.3 2.6 copy-start.18
  152.9 2.0 copy-start.5
  152.9 2.0 copy-start.22
  152.9 2.0 copy-start.44
  153.0 258.2 %copy-start.20 = (f32[1024]{0:T(1024)}, f32[1024]{0:T(1024)S(1)}, u32[]{:S(2)}) copy-start(f32[1024]{0:T(1024)S(1)} %broadcast_multiply_fusion) | copy-start | bytes 12292
  153.5 257.7 %copy-start.24 = (f32[1024]{0:T(1024)}, f32[1024]{0:T(1024)S(1)}, u32[]{:S(2)}) copy-start(f32[1024]{0:T(1024)S(1)} %fusion.105) | copy-start | bytes 12292
  154.9 5.9 copy-start.47
  154.9 5.9 copy-start.48
  160.9 250.3 %copy-start.40 = (pred[1024]{0:T(1024)(128)(4,1)}, pred[1024]{0:T(1024)(128)(4,1)S(1)}, u32[]{:S(2)}) copy-start(pred[1024]{0:T(1024)(128)(4,1)S(1)} %get-tuple-element.588) | copy-start | bytes 3076
  168.5 61.3 %all-to-all-start = ((bf16[8,144,1024]{2,1,0:T(8,128)(2,1)}), bf16[8,144,1024]{2,1,0:T(8,128)(2,1)}, u32[]{:S(2)}, u32[]{:S(2)}) async-start(bf16[8,144,1024]{2,1,0:T(8,128)(2,1)} %bitcast.225), calls=%async_computation | async-start | bytes 4718592 | tf_op jit(solution)/shard_map/all_to_all | solution.py:110
  229.8 59.1 %all-to-all-start.2 = ((bf16[8,144,1024]{2,1,0:T(8,128)(2,1)}), bf16[8,144,1024]{2,1,0:T(8,128)(2,1)}, u32[]{:S(2)}, u32[]{:S(2)}) async-start(bf16[8,144,1024]{2,1,0:T(8,128)(2,1)} %bitcast.224), calls=%async_computation.2 | async-start | bytes 4718592 | tf_op jit(solution)/shard_map/all_to_all | solution.py:140
  332.3 59.1 %all-to-all-start.3 = ((bf16[8,144,1024]{2,1,0:T(8,128)(2,1)}), bf16[8,144,1024]{2,1,0:T(8,128)(2,1)}, u32[]{:S(2)}, u32[]{:S(2)}) async-start(bf16[8,144,1024]{2,1,0:T(8,128)(2,1)} %bitcast.228), calls=%async_computation.3 | async-start | bytes 4718592 | tf_op jit(solution)/shard_map/all_to_all | solution.py:183
  336.7 961.0 %reduce-scatter.15.cloned.1.call-start = ((), (), s32[]{:S(2)}) async-start(), calls=%async_computation.15 | async-start | bytes 540672
  340.7 58.7 %copy-start.32 = (s32[1024]{0:T(1024)}, s32[1024]{0:T(1024)S(1)}, u32[]{:S(2)}) copy-start(s32[1024]{0:T(1024)S(1)} %broadcast_clamp_fusion) | copy-start | bytes 12292
  403.3 4.1 copy-start.6
  403.3 4.7 copy-start.11
  407.2 3.9 copy-start.12
  408.0 5.4 copy-start.28
  411.2 2.2 copy-start.36
  413.4 1.3 copy-start.15
  424.8 5.6 copy-start.2
  659.4 4.5 copy-start.3
  663.9 4.1 copy-start.19
  663.9 3.7 copy-start.14
  664.2 14.4 copy-start.16
  664.2 6.0 copy-start.51
  667.9 10.7 copy-start.17
  670.2 8.4 copy-start.43
  679.7 619.3 %reduce-scatter.13.cloned.1.call-start = ((), (), s32[]{:S(2)}) async-start(), calls=%async_computation.14 | async-start | bytes 540672
  679.7 5.5 copy-start.9
  679.7 5.5 copy-start.27
  679.7 5.5 copy-start.31
  685.3 3.1 copy-start.35
  685.3 3.5 copy-start.10
  685.3 3.4 copy-start.39
  688.4 2.5 copy-start.42
  691.9 731.4 %all-gather.3.cloned.1.call-start = ((), (), s32[]{:S(2)}) async-start(), calls=%async_computation.12 | async-start | bytes 11796480 | tf_op jit(solution)/shard_map/all_gather | solution.py:174
  692.5 746.9 %all-gather.5.cloned.1.call-start = ((), (), s32[]{:S(2)}) async-start(), calls=%async_computation.13 | async-start | bytes 11796480 | tf_op jit(solution)/shard_map/all_gather | solution.py:175
  693.1 762.5 %reduce-scatter.11.cloned.1.call-start = ((), (), s32[]{:S(2)}) async-start(), calls=%async_computation.11 | async-start | bytes 4325376 | tf_op jit(solution)/shard_map/reduce_scatter | solution.py:258
  720.5 256.4 %all-to-all-start.1 = ((bf16[8,144,1024]{2,1,0:T(8,128)(2,1)}), bf16[8,144,1024]{2,1,0:T(8,128)(2,1)}, u32[]{:S(2)}, u32[]{:S(2)}) async-start(bf16[8,144,1024]{2,1,0:T(8,128)(2,1)} %bitcast.229), calls=%async_computation.1 | async-start | bytes 4718592 | tf_op jit(solution)/shard_map/all_to_all | solution.py:123
  976.9 6.1 copy-start.50
  976.9 285.9 %all-to-all-start.4 = ((bf16[4,2,589824]{2,1,0:T(2,128)(2,1)}), bf16[4,2,589824]{2,1,0:T(2,128)(2,1)}, u32[]{:S(2)}, u32[]{:S(2)}) async-start(bf16[4,2,589824]{2,1,0:T(2,128)(2,1)} %reshape.381), calls=%async_computation.6 | async-start | bytes 18874368 | tf_op jit(solution)/shard_map/all_to_all | solution.py:172
  982.7 472.8 %reduce-scatter.9.cloned.1.call-start = ((), (), s32[]{:S(2)}) async-start(), calls=%async_computation.10 | async-start | bytes 12976128 | tf_op jit(solution)/shard_map/reduce_scatter | solution.py:257
  1262.8 5.9 copy-start.33
  1262.8 110.4 %all-to-all-start.5 = ((bf16[4,2,589824]{2,1,0:T(2,128)(2,1)}), bf16[4,2,589824]{2,1,0:T(2,128)(2,1)}, u32[]{:S(2)}, u32[]{:S(2)}) async-start(bf16[4,2,589824]{2,1,0:T(2,128)(2,1)} %reshape.383), calls=%async_computation.7 | async-start | bytes 18874368 | tf_op jit(solution)/shard_map/all_to_all | solution.py:171
  1276.7 4.0 copy-start.21
  1276.7 4.0 copy-start.23
  1276.7 4.0 copy-start.25
  1276.7 4.0 copy-start.29
  1276.7 4.0 copy-start.37
  1276.7 4.0 copy-start.41
  1289.6 5.5 copy-start.13
  1439.4 16.2 %copy-start.1 = (bf16[1024,1024]{1,0:T(8,128)(2,1)S(1)}, bf16[1024,1024]{1,0:T(8,128)(2,1)}, u32[]{:S(2)}) copy-start(bf16[1024,1024]{1,0:T(8,128)(2,1)} %param.21) | copy-start | bytes 6291460
  (1 other events, 0.6 us)
Sparse Core Ops, SparseCore 0:
  679.8 136.3 reduce-scatter.14
  818.5 131.9 reduce-scatter.12
  953.4 140.9 reduce-scatter.10
  1100.8 151.3 reduce-scatter.8
Sparse Core Ops, SparseCore 1:
  694.4 96.7 all-gather.2
  793.0 97.5 all-gather.4
where the time goes:
time: 1470 us; the launch traced here: 1460 us
  other arithmetic  539 us (37%)
  matrix products  381 us (26%)
  local copies, waits for them, and re-layouts  324 us (22%)
  waiting for transfers between devices  160 us (11%)
  starting transfers between devices  32 us (2%)
  between operations  16.1 us (1%)
    unnamed x4, other arithmetic  403 us
    unnamed x120, local copies, waits for them, and re-layouts  130 us
    dot_general x4, matrix products, block_scores(): jnp.einsum('qhd,khd->hqk', query_block, key_seq, preferred_element_type=j...  60.1 us
    convert_element_type x2, other arithmetic, attend_back(): score_grad = (prob_full * (prob_grad - jnp.sum(prob_full * prob_grad, axi...  55.6 us
    dot_general x4, matrix products, contract_cols(): lax.dot_general(first_mat, second_mat, (((1,), (1,)), ((), ())), preferre...  55.5 us
    dot_general x4, matrix products, contract_rows(): lax.dot_general(first_mat, second_mat, (((0,), (0,)), ((), ())), preferre...  53.1 us
    dot_general x2, matrix products, attend_back(): jnp.einsum('qhd,khd->hqk', head_grad, value_seq, preferred_element_type=j...  51.8 us
    all_to_all x1, waiting for transfers between devices, on_device(): lax.all_to_all(grad_rows, 'wide', split_axis=0, concat_axis=0, tiled=True)  50.7 us
  transfers between devices with their start and end apart: 12, of which 4 were waited for; matrix products, arithmetic and copies ran while one was open for 52% of the time, Pallas kernels for 0%

commit v1 on v0

v1 whole, which is shorter than its diff:
```python
import functools

import jax
import jax.numpy as jnp
from jax import lax
from jax.experimental import pallas as pl
from jax.experimental.pallas import tpu as pltpu
from jax.sharding import PartitionSpec as P

HEADS = 16
EPSILON = 1e-05
NEGATIVE = -1e30
CHUNKS = 2
BAND = 512
BLOCK = 256
F32 = jnp.float32
BF = jnp.bfloat16
VMEM_BYTES = 50 * 1024 * 1024


def mm(a, b):
    return lax.dot_general(a, b, (((1,), (0,)), ((), ())), preferred_element_type=F32)


def mm_nt(a, b):
    return lax.dot_general(a, b, (((1,), (1,)), ((), ())), preferred_element_type=F32)


def mm_tn(a, b):
    return lax.dot_general(a, b, (((0,), (0,)), ((), ())), preferred_element_type=F32)


def call(kernel, grid, in_specs, out_specs, out_shape, scratch=(), prefetch=0, flops=0, nbytes=0):
    return pl.pallas_call(
        kernel,
        grid_spec=pltpu.PrefetchScalarGridSpec(
            num_scalar_prefetch=prefetch,
            grid=grid,
            in_specs=in_specs,
            out_specs=out_specs,
            scratch_shapes=list(scratch),
        ),
        out_shape=out_shape,
        compiler_params=pltpu.CompilerParams(vmem_limit_bytes=VMEM_BYTES),
        cost_estimate=pl.CostEstimate(flops=flops, bytes_accessed=nbytes, transcendentals=0),
    )


def whole(shape):
    return pl.BlockSpec(shape, lambda *_: (0,) * len(shape))


def normalize(stream):
    average = jnp.mean(stream, axis=-1, keepdims=True)
    centered = stream - average
    inverse = lax.rsqrt(jnp.mean(centered * centered, axis=-1, keepdims=True) + EPSILON)
    return centered * inverse, inverse


def norm_back(unit, inverse, gain, grad):
    scaled = grad * gain
    first = jnp.mean(scaled, axis=-1, keepdims=True)
    second = jnp.mean(scaled * unit, axis=-1, keepdims=True)
    return inverse * (scaled - first - unit * second)


def qkv_kernel(x_ref, g_ref, b_ref, w_ref, n_ref, p_ref):
    rows = x_ref.shape[0]

    @pl.when(pl.program_id(0) == 0)
    def _():
        def step(i, _):
            at = pl.ds(i * 128, 128)
            unit, _inv = normalize(x_ref[at, :].astype(F32))
            n_ref[at, :] = (unit * g_ref[0:1, :] + b_ref[0:1, :]).astype(BF)
            return 0

        lax.fori_loop(0, rows // 128, step, 0)

    p_ref[...] = mm(n_ref[...], w_ref[...]).astype(BF)


def qkv(tokens, gains, biases, w_qkv):
    rows, dim = tokens.shape
    cols = w_qkv.shape[1]
    tile = 512
    return call(
        qkv_kernel,
        (cols // tile,),
        [whole((rows, dim)), whole(gains.shape), whole(biases.shape), pl.BlockSpec((dim, tile), lambda j: (0, j))],
        [whole((rows, dim)), pl.BlockSpec((rows, tile), lambda j: (0, j))],
        [jax.ShapeDtypeStruct((rows, dim), BF), jax.ShapeDtypeStruct((rows, cols), BF)],
        flops=2 * rows * dim * cols,
        nbytes=2 * (2 * rows * dim + dim * cols + rows * cols),
    )(tokens, gains, biases, w_qkv)


def spans(length):
    out = []
    for q_first in range(0, length, BLOCK):
        out.append((q_first, max(0, q_first - BAND)))
    return out


def fill_bias(bias_ref, doc_row, doc_col, length):
    at = 0
    for q_first, k_first in spans(length):
        keys = q_first + BLOCK - k_first
        key_pos = k_first + lax.broadcasted_iota(jnp.int32, (keys, BLOCK), 0)
        query_pos = q_first + lax.broadcasted_iota(jnp.int32, (keys, BLOCK), 1)
        same = doc_col[k_first : k_first + keys, :] == doc_row[:, q_first : q_first + BLOCK]
        bias_ref[at : at + keys, :] = jnp.where((key_pos <= query_pos) & same, 0.0, NEGATIVE).astype(F32)
        at += keys


def bias_rows(length):
    return sum(q + BLOCK - k for q, k in spans(length))


def head_lanes(block, head, head_dim):
    lane = lax.broadcasted_iota(jnp.int32, block.shape, 1)
    inside = (lane >= head * head_dim) & (lane < (head + 1) * head_dim)
    return jnp.where(inside, block, jnp.zeros_like(block))


def attn_fwd_kernel(head_dim, row_ref, col_ref, q_ref, k_ref, v_ref, o_ref, lse_ref, bias_ref):
    length = q_ref.shape[0]
    pair = q_ref.shape[1]
    scale = head_dim**-0.5

    @pl.when(pl.program_id(0) == 0)
    def _():
        fill_bias(bias_ref, row_ref[...], col_ref[...], length)

    value_t = v_ref[...].T
    at = 0
    for q_first, k_first in spans(length):
        keys = q_first + BLOCK - k_first
        q_at = slice(q_first, q_first + BLOCK)
        k_at = slice(k_first, k_first + keys)
        query = q_ref[q_at, :] * BF(scale)
        bias = bias_ref[at : at + keys, :]
        outs = []
        for head in range(pair // head_dim):
            scores = mm_nt(k_ref[k_at, :], head_lanes(query, head, head_dim)) + bias
            top = jnp.max(scores, axis=0, keepdims=True)
            exponent = jnp.exp(scores - top)
            total = jnp.sum(exponent, axis=0, keepdims=True)
            part = mm(value_t[head * head_dim : (head + 1) * head_dim, k_at], exponent.astype(BF))
            outs.append(part / total)
            lse_ref[0, head : head + 1, q_at] = top + jnp.log(total)
        o_ref[q_at, :] = jnp.concatenate(outs, axis=0).T.astype(BF)
        at += keys


def attn_fwd(projected, doc_row, doc_col, head_dim):
    length = projected.shape[0]
    width = projected.shape[1] // 3
    pair = 128
    pairs = width // pair
    per = pair // head_dim
    specs = [pl.BlockSpec((length, pair), functools.partial(lambda s, j: (0, s * pairs + j), s)) for s in range(3)]
    return call(
        functools.partial(attn_fwd_kernel, head_dim),
        (pairs,),
        [whole(doc_row.shape), whole(doc_col.shape)] + specs,
        [pl.BlockSpec((length, pair), lambda j: (0, j)), pl.BlockSpec((1, per, length), lambda j: (j, 0, 0))],
        [jax.ShapeDtypeStruct((length, width), BF), jax.ShapeDtypeStruct((pairs, per, length), F32)],
        scratch=[pltpu.VMEM((bias_rows(length), BLOCK), F32)],
        flops=8 * bias_rows(length) * BLOCK * width,
        nbytes=8 * length * width,
    )(doc_row, doc_col, projected, projected, projected)


def attn_bwd_kernel(head_dim, row_ref, col_ref, q_ref, k_ref, v_ref, do_ref, lse_ref, dq_ref, dk_ref, dv_ref, bias_ref, dk_sum, dv_sum):
    length = q_ref.shape[0]
    pair = q_ref.shape[1]
    scale = head_dim**-0.5

    @pl.when(pl.program_id(0) == 0)
    def _():
        fill_bias(bias_ref, row_ref[...], col_ref[...], length)

    key_t = (k_ref[...] * BF(scale)).T
    dk_sum[...] = jnp.zeros_like(dk_sum)
    dv_sum[...] = jnp.zeros_like(dv_sum)
    at = 0
    for q_first, k_first in spans(length):
        keys = q_first + BLOCK - k_first
        q_at = slice(q_first, q_first + BLOCK)
        k_at = slice(k_first, k_first + keys)
        query = q_ref[q_at, :] * BF(scale)
        grad = do_ref[q_at, :]
        bias = bias_ref[at : at + keys, :]
        dq_parts = []
        dk_part = None
        dv_part = None
        for head in range(pair // head_dim):
            query_one = head_lanes(query, head, head_dim)
            grad_one = head_lanes(grad, head, head_dim)
            scores = mm_nt(k_ref[k_at, :], query_one) + bias
            prob = jnp.exp(scores - lse_ref[0, head : head + 1, q_at])
            prob_grad = mm_nt(v_ref[k_at, :], grad_one)
            inner = jnp.sum(prob * prob_grad, axis=0, keepdims=True)
            score_grad = (prob * (prob_grad - inner)).astype(BF)
            dv_one = mm(prob.astype(BF), grad_one)
            dk_one = mm(score_grad, query_one)
            dv_part = dv_one if dv_part is None else dv_part + dv_one
            dk_part = dk_one if dk_part is None else dk_part + dk_one
            dq_parts.append(mm(key_t[head * head_dim : (head + 1) * head_dim, k_at], score_grad))
        dk_sum[k_at, :] += dk_part
        dv_sum[k_at, :] += dv_part
        dq_ref[q_at, :] = jnp.concatenate(dq_parts, axis=0).T.astype(BF)
        at += keys
    dk_ref[...] = dk_sum[...].astype(BF)
    dv_ref[...] = dv_sum[...].astype(BF)


def attn_bwd(projected, grad_heads, log_total, doc_row, doc_col, head_dim):
    length = projected.shape[0]
    width = projected.shape[1] // 3
    pair = 128
    pairs = width // pair
    per = pair // head_dim
    specs = [pl.BlockSpec((length, pair), functools.partial(lambda s, j: (0, s * pairs + j), s)) for s in range(3)]
    one = pl.BlockSpec((length, pair), lambda j: (0, j))
    return call(
        functools.partial(attn_bwd_kernel, head_dim),
        (pairs,),
        [whole(doc_row.shape), whole(doc_col.shape)]
        + specs
        + [one, pl.BlockSpec((1, per, length), lambda j: (j, 0, 0))],
        [one, one, one],
        [jax.ShapeDtypeStruct((length, width), BF)] * 3,
        scratch=[
            pltpu.VMEM((bias_rows(length), BLOCK), F32),
            pltpu.VMEM((length, pair), F32),
            pltpu.VMEM((length, pair), F32),
        ],
        flops=20 * bias_rows(length) * BLOCK * width,
        nbytes=14 * length * width,
    )(doc_row, doc_col, projected, projected, projected, grad_heads, log_total)


def middle_kernel(x_ref, h_ref, w_ref, g_ref, b_ref, m_ref, s_ref):
    middle = x_ref[...].astype(F32) + mm(h_ref[...], w_ref[...])
    m_ref[...] = middle
    unit, _inv = normalize(middle)
    s_ref[...] = (unit * g_ref[1:2, :] + b_ref[1:2, :]).astype(BF)


def make_middle(tokens, mixed_heads, w_attn_out, gains, biases):
    rows, dim = tokens.shape
    tile = 256
    block = pl.BlockSpec((tile, dim), lambda i: (i, 0))
    return call(
        middle_kernel,
        (rows // tile,),
        [block, block, whole(w_attn_out.shape), whole(gains.shape), whole(biases.shape)],
        [block, block],
        [jax.ShapeDtypeStruct((rows, dim), F32), jax.ShapeDtypeStruct((rows, dim), BF)],
        flops=2 * rows * dim * dim,
        nbytes=12 * rows * dim,
    )(tokens, mixed_heads, w_attn_out, gains, biases)


def dispatch_kernel(place_ref, x_ref, o_ref):
    tile = o_ref.shape[0]
    slot = pl.program_id(0) * tile + lax.broadcasted_iota(jnp.int32, (tile, place_ref.shape[1]), 0)
    pick = jnp.where(slot == place_ref[...], 1.0, 0.0).astype(BF)
    o_ref[...] = mm(pick, x_ref[...]).astype(BF)


def dispatch_rows(place_row, rows, count):
    dim = rows.shape[1]
    tile = 384
    return call(
        dispatch_kernel,
        (count // tile,),
        [whole(place_row.shape), whole(rows.shape)],
        pl.BlockSpec((tile, dim), lambda i: (i, 0)),
        jax.ShapeDtypeStruct((count, dim), BF),
        flops=2 * rows.shape[0] * count * dim,
        nbytes=2 * dim * (rows.shape[0] + count),
    )(place_row, rows)


def pick_rows(place, back):
    slot = lax.broadcasted_iota(jnp.int32, (place.shape[0], back.shape[0]), 1)
    return mm(jnp.where(slot == place, 1.0, 0.0).astype(BF), back)


def mixed_kernel(place_ref, m_ref, r_ref, o_ref):
    o_ref[...] = (m_ref[...] + pick_rows(place_ref[...], r_ref[...])).astype(BF)


def make_mixed(place_col, middle, back):
    rows, dim = middle.shape
    tile = 256
    block = pl.BlockSpec((tile, dim), lambda i: (i, 0))
    return call(
        mixed_kernel,
        (rows // tile,),
        [pl.BlockSpec((tile, 1), lambda i: (i, 0)), block, whole(back.shape)],
        block,
        jax.ShapeDtypeStruct((rows, dim), BF),
        flops=2 * rows * back.shape[0] * dim,
        nbytes=8 * rows * dim,
    )(place_col, middle, back)


def second_back_kernel(place_ref, m_ref, c_ref, r_ref, w_ref, g_ref, gm_ref, ga_ref, gh_ref, sums_ref):
    grad_sent = pick_rows(place_ref[...], r_ref[...])
    unit, inverse = normalize(m_ref[...])
    grad_middle = c_ref[...].astype(F32) + norm_back(unit, inverse, g_ref[1:2, :], grad_sent)
    gm_ref[...] = grad_middle
    grad_attn = grad_middle.astype(BF)
    ga_ref[...] = grad_attn
    gh_ref[...] = mm_nt(grad_attn, w_ref[...]).astype(BF)
    sums = jnp.concatenate(
        [jnp.sum(grad_sent * unit, axis=0, keepdims=True), jnp.sum(grad_sent, axis=0, keepdims=True)], axis=0
    )

    @pl.when(pl.program_id(0) == 0)
    def _():
        sums_ref[...] = sums

    @pl.when(pl.program_id(0) > 0)
    def _():
        sums_ref[...] += sums


def second_back(place_col, middle, cotangent, back, w_attn_out, gains):
    rows, dim = middle.shape
    tile = 256
    block = pl.BlockSpec((tile, dim), lambda i: (i, 0))
    return call(
        second_back_kernel,
        (rows // tile,),
        [
            pl.BlockSpec((tile, 1), lambda i: (i, 0)),
            block,
            block,
            whole(back.shape),
            whole(w_attn_out.shape),
            whole(gains.shape),
        ],
        [block, block, block, whole((2, dim))],
        [
            jax.ShapeDtypeStruct((rows, dim), F32),
            jax.ShapeDtypeStruct((rows, dim), BF),
            jax.ShapeDtypeStruct((rows, dim), BF),
            jax.ShapeDtypeStruct((2, dim), F32),
        ],
        flops=2 * rows * (back.shape[0] + dim) * dim,
        nbytes=16 * rows * dim,
    )(place_col, middle, cotangent, back, w_attn_out, gains)


def first_back_kernel(x_ref, gm_ref, dq_ref, dk_ref, dv_ref, w_ref, g_ref, dx_ref, sums_ref):
    dim = x_ref.shape[1]
    grad_normed = mm_nt(dq_ref[...], w_ref[:, :dim])
    grad_normed += mm_nt(dk_ref[...], w_ref[:, dim : 2 * dim])
    grad_normed += mm_nt(dv_ref[...], w_ref[:, 2 * dim :])
    unit, inverse = normalize(x_ref[...].astype(F32))
    dx_ref[...] = gm_ref[...] + norm_back(unit, inverse, g_ref[0:1, :], grad_normed)
    sums = jnp.concatenate(
        [jnp.sum(grad_normed * unit, axis=0, keepdims=True), jnp.sum(grad_normed, axis=0, keepdims=True)], axis=0
    )

    @pl.when(pl.program_id(0) == 0)
    def _():
        sums_ref[...] = sums

    @pl.when(pl.program_id(0) > 0)
    def _():
        sums_ref[...] += sums


def first_back(tokens, grad_middle, grads, w_qkv, gains):
    rows, dim = tokens.shape
    tile = 256
    block = pl.BlockSpec((tile, dim), lambda i: (i, 0))
    return call(
        first_back_kernel,
        (rows // tile,),
        [block, block, block, block, block, whole(w_qkv.shape), whole(gains.shape)],
        [block, whole((2, dim))],
        [jax.ShapeDtypeStruct((rows, dim), F32), jax.ShapeDtypeStruct((2, dim), F32)],
        flops=6 * rows * dim * dim,
        nbytes=22 * rows * dim,
    )(tokens, grad_middle, *grads, w_qkv, gains)


def expert_kernel(x_ref, c_ref, wi_ref, wo_ref, h_ref, gp_ref, out_ref, gr_ref, out_sum, gr_sum):
    step = pl.program_id(0)
    preact = mm(x_ref[...], wi_ref[...])
    grad_hidden = mm_nt(c_ref[...], wo_ref[...])
    slope = 0.7978845608028654
    square = preact * preact
    tanh = jnp.tanh(preact * (slope + (slope * 0.044715) * square))
    half = 0.5 + 0.5 * tanh
    hidden = preact * half
    gate = half + hidden * (1.0 - tanh) * (slope + (3.0 * slope * 0.044715) * square)
    hidden_low = hidden.astype(BF)
    grad_low = (gate * grad_hidden).astype(BF)
    h_ref[...] = hidden_low
    gp_ref[...] = grad_low
    out_part = mm(hidden_low, wo_ref[...])
    gr_part = mm_nt(grad_low, wi_ref[...])

    @pl.when(step == 0)
    def _():
        out_sum[...] = out_part
        gr_sum[...] = gr_part

    @pl.when(step > 0)
    def _():
        out_sum[...] += out_part
        gr_sum[...] += gr_part

    @pl.when(step == pl.num_programs(0) - 1)
    def _():
        out_ref[...] = out_sum[...].astype(BF)
        gr_ref[...] = gr_sum[...].astype(BF)


def expert(rows, grads, w_in, w_out):
    count, dim = rows.shape
    units = w_in.shape[1]
    tile = 512
    act = pl.BlockSpec((count, tile), lambda j: (0, j))
    return call(
        expert_kernel,
        (units // tile,),
        [
            whole(rows.shape),
            whole(grads.shape),
            pl.BlockSpec((dim, tile), lambda j: (0, j)),
            pl.BlockSpec((tile, dim), lambda j: (j, 0)),
        ],
        [act, act, whole(rows.shape), whole(rows.shape)],
        [
            jax.ShapeDtypeStruct((count, units), BF),
            jax.ShapeDtypeStruct((count, units), BF),
            jax.ShapeDtypeStruct((count, dim), BF),
            jax.ShapeDtypeStruct((count, dim), BF),
        ],
        scratch=[pltpu.VMEM((count, dim), F32), pltpu.VMEM((count, dim), F32)],
        flops=8 * count * dim * units,
        nbytes=4 * dim * units + 4 * count * units,
    )(rows, grads, w_in, w_out)


def outer_kernel(count, *refs):
    o_ref = refs[-1]
    total = mm_tn(refs[1][...], refs[1 + count][...])
    for i in range(1, count):
        total += mm_tn(refs[1 + i][...], refs[1 + count + i][...])
    o_ref[0] = total.astype(BF)


def outer(first, second, table, first_tile, second_tile, steps):
    count = len(first)
    first_cols = first_tile or first[0].shape[1]
    second_cols = second_tile or second[0].shape[1]
    return call(
        functools.partial(outer_kernel, count),
        (steps,),
        [pl.BlockSpec((a.shape[0], first_cols), lambda i, t: (0, t[0, i])) for a in first]
        + [pl.BlockSpec((a.shape[0], second_cols), lambda i, t: (0, t[1, i])) for a in second],
        pl.BlockSpec((1, first_cols, second_cols), lambda i, t: (i, 0, 0)),
        jax.ShapeDtypeStruct((steps, first_cols, second_cols), BF),
        prefetch=1,
        flops=2 * steps * first_cols * second_cols * sum(a.shape[0] for a in first),
        nbytes=2 * steps * first_cols * second_cols,
    )(table, *first, *second)


def swap(value, axis, mask):
    size = lax.axis_size(axis)
    return lax.ppermute(value, axis, [(i, i ^ mask) for i in range(size)])


def exchange(rows, axis):
    size = lax.axis_size(axis)
    blocks = rows.reshape(size, rows.shape[0] // size, rows.shape[1])
    parts = [blocks[0]] + [swap(blocks[p], axis, p) for p in range(1, size)]
    return jnp.concatenate(parts, axis=0)


def split_sum(value, dim, axis, mask):
    bit = jnp.where((lax.axis_index(axis) & mask) > 0, 1, 0)
    mine = lax.dynamic_index_in_dim(value, bit, dim, keepdims=False)
    other = lax.dynamic_index_in_dim(value, 1 - bit, dim, keepdims=False)
    return (mine.astype(F32) + swap(other, axis, mask).astype(F32)).astype(value.dtype)


def bits_of(size):
    return [1 << i for i in range(size.bit_length() - 1)]


def on_device(
    tokens,
    norm_gains,
    norm_biases,
    w_qkv,
    w_attn_out,
    w_in,
    w_out,
    segment_ids,
    expert_ids,
    slots,
    cotangent,
):
    tok, dim = tokens.shape
    head_dim = dim // HEADS
    wide = lax.axis_size("wide")
    narrow = lax.axis_size("narrow")
    units = w_in.shape[2]
    me_wide = lax.axis_index("wide")
    me_narrow = lax.axis_index("narrow")
    capacity = tok * 9 // (8 * wide)
    count = wide * capacity
    part_slots = capacity // CHUNKS
    part_rows = wide * part_slots
    w_in = w_in[0]
    w_out = w_out[0]

    place = (slots // part_slots) * part_rows + (expert_ids ^ me_wide) * part_slots + slots % part_slots
    place = jnp.where(slots < capacity, place, count).astype(jnp.int32)
    place_row = place[None, :]
    place_col = place[:, None]
    doc_row = segment_ids
    doc_col = segment_ids.reshape(tok, 1)

    sent_grads = dispatch_rows(place_row, cotangent, count)
    expert_grads = [exchange(sent_grads[c * part_rows : (c + 1) * part_rows], "wide") for c in range(CHUNKS)]

    normed, projected = qkv(tokens, norm_gains, norm_biases, w_qkv)
    mixed_heads, log_total = attn_fwd(projected, doc_row, doc_col, head_dim)
    middle, sent = make_middle(tokens, mixed_heads, w_attn_out, norm_gains, norm_biases)
    sent_rows = dispatch_rows(place_row, sent, count)
    expert_rows = [exchange(sent_rows[c * part_rows : (c + 1) * part_rows], "wide") for c in range(CHUNKS)]

    done = [expert(expert_rows[c], expert_grads[c], w_in, w_out) for c in range(CHUNKS)]
    hidden = [d[0] for d in done]
    grad_preact = [d[1] for d in done]
    back_grads = jnp.concatenate([exchange(d[3], "wide") for d in done], axis=0)
    back_rows = jnp.concatenate([exchange(d[2], "wide") for d in done], axis=0)

    quarter = units // narrow
    half = quarter // 2
    half_dim = dim // 2
    order = [0, 2, 1, 3]

    def place_table(firsts, seconds):
        return jnp.stack([jnp.stack(firsts), jnp.stack(seconds)]).astype(jnp.int32)

    zero = jnp.int32(0)

    def out_tiles(side, positions):
        table = place_table([2 * (me_narrow ^ p) + side for p in positions], [zero for _ in positions])
        return outer(hidden, expert_grads, table, half, None, len(positions))

    def in_tiles(side, positions):
        table = place_table([zero + side for _ in positions], [me_narrow ^ p for p in positions])
        return outer(expert_rows, grad_preact, table, half_dim, quarter, len(positions))

    def narrow_sum(tiles, side):
        masks = [1, 2] if side == 0 else [2, 1]
        first, second = masks
        send = tiles(side, [first, 3])
        keep = tiles(side, [0, second])
        got = swap(send, "narrow", first)
        again = (keep[1].astype(F32) + got[1].astype(F32)).astype(BF)
        last = swap(again, "narrow", second)
        return keep[0].astype(F32) + got[0].astype(F32) + last.astype(F32)

    d_w_out = jnp.concatenate([narrow_sum(out_tiles, 0), narrow_sum(out_tiles, 1)], axis=0)
    d_w_in = jnp.concatenate([narrow_sum(in_tiles, 0), narrow_sum(in_tiles, 1)], axis=0)

    mixed = make_mixed(place_col, middle, back_rows)
    grad_middle, grad_attn, grad_heads, sums_two = second_back(
        place_col, middle, cotangent, back_grads, w_attn_out, norm_gains
    )
    grads = attn_bwd(projected, grad_heads, log_total, doc_row, doc_col, head_dim)
    d_tokens, sums_one = first_back(tokens, grad_middle, grads, w_qkv, norm_gains)

    owners = narrow * wide

    def transposed(first, second):
        steps = first.shape[1] // 512
        table = place_table([jnp.int32(i) for i in range(steps)], [zero for _ in range(steps)])
        return outer([first], [second], table, 512, None, steps).reshape(first.shape[1], second.shape[1])

    d_qkv_t = jnp.concatenate([transposed(g, normed) for g in grads], axis=0)
    d_out_t = transposed(grad_attn, mixed_heads)
    own_qkv = 3 * dim // owners
    own_out = dim // owners
    joined = jnp.concatenate(
        [d_qkv_t.reshape(owners, own_qkv, dim), d_out_t.reshape(owners, own_out, dim)], axis=1
    )
    n_bits = bits_of(narrow)
    w_bits = bits_of(wide)
    shape = (2,) * (len(n_bits) + len(w_bits)) + (own_qkv + own_out, dim)
    value = joined.reshape(shape)
    names = [("narrow", b) for b in reversed(n_bits)] + [("wide", b) for b in reversed(w_bits)]
    steps = [("wide", 1), ("narrow", 1), ("narrow", 2)] + [("wide", b) for b in w_bits[1:]]
    for step in steps:
        dim_at = names.index(step)
        value = split_sum(value, dim_at, *step)
        names.pop(dim_at)
    d_w_qkv = value[:own_qkv].T.astype(F32)
    d_w_attn_out = value[own_qkv:].T.astype(F32)

    sums = jnp.concatenate([sums_one[0:1], sums_two[0:1], sums_one[1:2], sums_two[1:2]], axis=0)
    sums = lax.psum_scatter(sums, ("narrow", "wide"), scatter_dimension=1, tiled=True)
    return (mixed, d_tokens, sums[:2], sums[2:], d_w_qkv, d_w_attn_out, d_w_in[None], d_w_out[None])


def solution(mesh):
    placed = (
        P(("narrow", "wide"), None),
        P(),
        P(),
        P(),
        P(),
        P("wide", None, None),
        P("wide", None, None),
        P(("narrow", "wide"), None),
        P(("narrow", "wide")),
        P(("narrow", "wide")),
        P(("narrow", "wide"), None),
    )
    return jax.shard_map(
        on_device,
        mesh=mesh,
        in_specs=placed,
        out_specs=(
            P(("narrow", "wide"), None),
            P(("narrow", "wide"), None),
            P(None, ("narrow", "wide")),
            P(None, ("narrow", "wide")),
            P(None, ("narrow", "wide")),
            P(None, ("narrow", "wide")),
            P("wide", None, "narrow"),
            P("wide", "narrow", None),
        ),
        check_vma=False,
    )
```

time: 1470 us -> 727 us (0.49)
  other arithmetic: 539 us -> 42.9 us
  matrix products: 381 us -> 0 us
  local copies, waits for them, and re-layouts: 324 us -> 37.8 us
  Pallas kernels: 0 us -> 265 us
  starting transfers between devices: 32 us -> 121 us
  waiting for transfers between devices: 160 us -> 233 us
    unnamed x4 -> x1, other arithmetic: 403 us -> 0.01 us
    dot_general x26 -> x0, matrix products: 381 us -> none  [the longest x4 60.1 us: block_scores(): jnp.einsum('qhd,khd->hqk', query_block, key_seq, preferred_element_type=j...]
    pallas_call x0 -> x23, Pallas kernels: none -> 265 us  [the longest x12 74.8 us: outer(): call(functools.partial(outer_kernel, count), (steps,), [pl.BlockSpec((a.s...]
    all_to_all x6 -> x0, waiting for transfers between devices: 158 us -> none  [the longest x1 50.7 us: on_device(): lax.all_to_all(grad_rows, 'wide', split_axis=0, concat_axis=0, tiled=True)]
    ppermute x0 -> x69, waiting for transfers between devices: none -> 131 us  [swap(): return lax.ppermute(value, axis, [(i, i ^ mask) for i in range(size)])]
    ppermute x0 -> x69, starting transfers between devices: none -> 121 us  [swap(): return lax.ppermute(value, axis, [(i, i ^ mask) for i in range(size)])]
    unnamed x120 -> x157, local copies, waits for them, and re-layouts: 130 us -> 24.2 us
    unnamed x8 -> x2, waiting for transfers between devices: 1.12 us -> 102 us
  transfers between devices with their start and end apart: 12 -> 70, of which waited for: 4 -> 24; matrix products, arithmetic and copies ran while one was open for 52% -> 6% of each run, Pallas kernels for 0% -> 19%
where the time goes in v1:
time: 727 us; the launch traced here: 716 us
  Pallas kernels  265 us (36%)
  waiting for transfers between devices  233 us (32%)
  starting transfers between devices  121 us (17%)
  other arithmetic  42.9 us (6%)
  local copies, waits for them, and re-layouts  37.8 us (5%)
  between operations  15.6 us (2%)
    ppermute x69, waiting for transfers between devices, swap(): return lax.ppermute(value, axis, [(i, i ^ mask) for i in range(size)])  131 us
    ppermute x69, starting transfers between devices, swap(): return lax.ppermute(value, axis, [(i, i ^ mask) for i in range(size)])  121 us
    unnamed x2, waiting for transfers between devices  102 us
    pallas_call x12, Pallas kernels, outer(): call(functools.partial(outer_kernel, count), (steps,), [pl.BlockSpec((a.s...  74.8 us
    pallas_call x2, Pallas kernels, expert(): call(expert_kernel, (units // tile,), [whole(rows.shape), whole(grads.sha...  57.9 us
    pallas_call x1, Pallas kernels, attn_bwd(): call(functools.partial(attn_bwd_kernel, head_dim), (pairs,), [whole(doc_r...  39.5 us
    pallas_call x1, Pallas kernels, attn_fwd(): call(functools.partial(attn_fwd_kernel, head_dim), (pairs,), [whole(doc_r...  32 us
    unnamed x157, local copies, waits for them, and re-layouts  24.2 us
  transfers between devices with their start and end apart: 70, of which 24 were waited for; matrix products, arithmetic and copies ran while one was open for 6% of the time, Pallas kernels for 19%

profile of v1, /device:TPU:0, one launch (start us, length us, event | category | flops | bytes accessed | tf_op | source)
XLA Modules:
  0.0 715.6 jit_solution(13519621042680787995)
XLA Ops:
  9.6 13.5 %shard_map.170 = (bf16[1024,1024]{1,0:T(8,128)(2,1)S(1)}, bf16[1024,3072]{1,0:T(8,128)(2,1)}) custom-call(bf16[1024,1024]{1,0:T(8,128)(2,1)} %x_ref.7, f32[2,1024]{1,0:T(2,128)S(1)} %copy-done.32, f32[2,1024]{1,0:T(2,128)S(1)} %copy-done.30, bf16[1024,3072]{1,0:T(8,128)(2,1)} %w_ref.7), custom_call_target="tpu_custom_call" | custom-call | flops 6442450944 | bytes 16777216 | tf_op jit(solution)/shard_map/pallas_call | solution.py:87
  24.4 32.0 %shard_map.171 = (bf16[1024,1024]{1,0:T(8,128)(2,1)S(1)}, f32[8,2,1024]{2,1,0:T(2,128)S(1)}) custom-call(s32[1,1024]{1,0:T(1,128)S(1)} %copy-done.18, s32[1024,1]{1,0:T(8,128)S(1)} %copy.24.col_ref, bf16[1024,3072]{1,0:T(8,128)(2,1)} %get-tuple-element.31.q_ref.k_ref.v_ref, bf16[1024,3072]{1,0:T(8,128)(2,1)} %get-tuple-element.31.q_ref.k_ref.v_ref, ...), custom_call_target="tpu_custom_call" | custom-call | flops 4831838208 | bytes 8388608 | tf_op jit(solution)/shard_map/pallas_call | solution.py:163
  57.8 7.3 %shard_map.172 = (f32[1024,1024]{1,0:T(8,128)}, bf16[1024,1024]{1,0:T(8,128)(2,1)S(1)}) custom-call(bf16[1024,1024]{1,0:T(8,128)(2,1)} %x_ref.7, bf16[1024,1024]{1,0:T(8,128)(2,1)} %copy-done.27, bf16[1024,1024]{1,0:T(8,128)(2,1)} %w_ref.6, f32[2,1024]{1,0:T(2,128)S(1)} %copy-done.33, f32[2,1024]{1,0:T(2,128)S(1)} %copy-done.31), custom_call_target="tpu_custom_call" | custom-call | flops 2147483648 | bytes 12582912 | tf_op jit(solution)/shard_map/pallas_call | solution.py:256
  65.2 3.9 shard_map.173
  71.7 2.6 collective-permute-start.1
  74.4 2.8 collective-permute-start.3
  77.2 3.9 shard_map.174
  83.0 3.6 collective-permute-start.5
  88.4 8.9 %collective-permute-start.9 = (bf16[72,1024]{1,0:T(8,128)(2,1)S(1)}, bf16[72,1024]{1,0:T(8,128)(2,1)S(1)}, u32[]{:S(2)}, u32[]{:S(2)}) collective-permute-start(bf16[72,1024]{1,0:T(8,128)(2,1)S(1)} %get-tuple-element.66), channel_id=1, source_target_pairs={{0,3},{1,2},{2,1},{3,0},{4,7},{5,6},{6,5},{7,4},{8,11},{9,10},{10,... | collective-permute-start | bytes 442376 | tf_op jit(solution)/shard_map/ppermute | solution.py:482
  97.4 6.5 collective-permute-start.10
  103.9 7.3 %collective-permute-start.11 = (bf16[72,1024]{1,0:T(8,128)(2,1)S(1)}, bf16[72,1024]{1,0:T(8,128)(2,1)S(1)}, u32[]{:S(2)}, u32[]{:S(2)}) collective-permute-start(bf16[72,1024]{1,0:T(8,128)(2,1)S(1)} %get-tuple-element.64), channel_id=1, source_target_pairs={{0,5},{1,4},{2,7},{3,6},{4,1},{5,0},{6,3},{7,2},{8,13},{9,12},{10,... | collective-permute-start | bytes 442376 | tf_op jit(solution)/shard_map/ppermute | solution.py:482
  111.5 4.0 collective-permute-start.21
  116.3 4.5 collective-permute-start.22
  122.7 6.5 collective-permute-start.24
  129.2 7.3 %collective-permute-start.25 = (bf16[72,1024]{1,0:T(8,128)(2,1)S(1)}, bf16[72,1024]{1,0:T(8,128)(2,1)S(1)}, u32[]{:S(2)}, u32[]{:S(2)}) collective-permute-start(bf16[72,1024]{1,0:T(8,128)(2,1)S(1)} %get-tuple-element.72), channel_id=1, source_target_pairs={{0,5},{1,4},{2,7},{3,6},{4,1},{5,0},{6,3},{7,2},{8,13},{9,12},{10,... | collective-permute-start | bytes 442376 | tf_op jit(solution)/shard_map/ppermute | solution.py:482
  137.6 29.1 %shard_map.175 = (bf16[576,4096]{1,0:T(8,128)(2,1)}, bf16[576,4096]{1,0:T(8,128)(2,1)}, bf16[576,1024]{1,0:T(8,128)(2,1)S(1)}, bf16[576,1024]{1,0:T(8,128)(2,1)S(1)}) custom-call(bf16[576,1024]{1,0:T(8,128)(2,1)S(1)} %constant_dynamic-update-slice_fusion.x_ref.refs_1_, bf16[576,1024]{1,0:T(8,128)(2,1)} %copy-done.2, bf16[1024,4096]{1,0:T(8,128)(2,1)} %bitcast.106, ...), custom_call_target="tpu_custom_call" | custom-call | flops 19327352832 | bytes 26214400 | tf_op jit(solution)/shard_map/pallas_call | solution.py:433
  167.0 4.0 collective-permute-start.28
  172.6 2.8 collective-permute-done.26
  175.4 2.7 collective-permute-start.32
  180.4 3.9 collective-permute-done.29
  184.3 3.4 collective-permute-done.30
  188.1 7.7 %collective-permute-done.31 = bf16[72,1024]{1,0:T(8,128)(2,1)S(1)} collective-permute-done((bf16[72,1024]{1,0:T(8,128)(2,1)S(1)}, bf16[72,1024]{1,0:T(8,128)(2,1)S(1)}, u32[]{:S(2)}, u32[]{:S(2)}) %collective-permute-start.31) | collective-permute-done | bytes 147488 | tf_op jit(solution)/shard_map/ppermute | solution.py:482
  197.0 4.4 collective-permute-start.45
  204.7 28.8 %shard_map.176 = (bf16[576,4096]{1,0:T(8,128)(2,1)}, bf16[576,4096]{1,0:T(8,128)(2,1)}, bf16[576,1024]{1,0:T(8,128)(2,1)S(1)}, bf16[576,1024]{1,0:T(8,128)(2,1)S(1)}) custom-call(bf16[576,1024]{1,0:T(8,128)(2,1)S(1)} %constant_dynamic-update-slice_fusion.14.x_ref.refs_2_, bf16[576,1024]{1,0:T(8,128)(2,1)} %copy-done, bf16[1024,4096]{1,0:T(8,128)(2,1)} %bitcast.107, ...), custom_call_target="tpu_custom_call" | custom-call | flops 19327352832 | bytes 26214400 | tf_op jit(solution)/shard_map/pallas_call | solution.py:433
  233.5 2.5 collective-permute-start.47
  238.1 3.9 collective-permute-done.47
  242.0 3.3 collective-permute-done.48
  247.5 4.2 collective-permute-start.50
  257.2 4.1 collective-permute-done.50
  262.0 2.4 collective-permute-done.51
  265.7 8.3 %collective-permute-done.53 = bf16[72,1024]{1,0:T(8,128)(2,1)S(1)} collective-permute-done((bf16[72,1024]{1,0:T(8,128)(2,1)S(1)}, bf16[72,1024]{1,0:T(8,128)(2,1)S(1)}, u32[]{:S(2)}, u32[]{:S(2)}) %collective-permute-start.53) | collective-permute-done | bytes 147488 | tf_op jit(solution)/shard_map/ppermute | solution.py:482
  276.1 11.7 %shard_map.178 = (f32[1024,1024]{1,0:T(8,128)}, bf16[1024,1024]{1,0:T(8,128)(2,1)S(1)}, bf16[1024,1024]{1,0:T(8,128)(2,1)}, f32[2,1024]{1,0:T(2,128)S(1)}) custom-call(s32[1024,1]{1,0:T(8,128)S(1)} %copy.25.place_ref, f32[1024,1024]{1,0:T(8,128)} %get-tuple-element.33.m_ref, bf16[1024,1024]{1,0:T(8,128)(2,1)} %c_ref.1, ...), custom_call_target="tpu_custom_call" | custom-call | flops 4563402752 | bytes 16777216 | tf_op jit(solution)/shard_map/pallas_call | solution.py:337
  289.1 39.5 %shard_map.179 = (bf16[1024,1024]{1,0:T(8,128)(2,1)S(1)}, bf16[1024,1024]{1,0:T(8,128)(2,1)}, bf16[1024,1024]{1,0:T(8,128)(2,1)}) custom-call(s32[1,1024]{1,0:T(1,128)S(1)} %copy-done.18, s32[1024,1]{1,0:T(8,128)S(1)} %copy-done.13, bf16[1024,3072]{1,0:T(8,128)(2,1)} %get-tuple-element.31.q_ref.k_ref.v_ref, ...), custom_call_target="tpu_custom_call" | custom-call | flops 12079595520 | bytes 14680064 | tf_op jit(solution)/shard_map/pallas_call | solution.py:227
  329.9 5.3 shard_map.181
  335.2 5.1 shard_map.182
  340.3 5.1 shard_map.183
  345.4 5.1 shard_map.184
  350.5 12.0 %pad_maximum_fusion = bf16[3072,1024]{1,0:T(8,128)(2,1)S(1)} fusion(bf16[1024,1024]{1,0:T(8,128)(2,1)S(1)} %bitcast.95, bf16[1024,1024]{1,0:T(8,128)(2,1)S(1)} %bitcast.94, bf16[1024,1024]{1,0:T(8,128)(2,1)S(1)} %bitcast.93), kind=kLoop, calls=%fused_computation.6 | loop fusion | flops 18874368 | bytes 12582912 | tf_op jit(solution)/shard_map/concatenate | solution.py:597
  362.6 2.7 fusion.2
  372.5 6.5 shard_map.190
  380.5 6.5 shard_map.192
  388.8 4.9 collective-permute-start.15
  393.6 6.7 shard_map.189
  400.3 6.5 shard_map.191
  406.9 7.0 shard_map.185
  413.8 7.0 shard_map.186
  420.9 7.0 shard_map.187
  427.8 7.0 shard_map.188
  437.4 5.8 collective-permute-done.16
  447.1 8.7 %collective-permute-done.18 = bf16[72,1024]{1,0:T(8,128)(2,1)S(1)} collective-permute-done((bf16[72,1024]{1,0:T(8,128)(2,1)S(1)}, bf16[72,1024]{1,0:T(8,128)(2,1)S(1)}, u32[]{:S(2)}, u32[]{:S(2)}) %collective-permute-start.18) | collective-permute-done | bytes 147488 | tf_op jit(solution)/shard_map/ppermute | solution.py:482
  457.5 6.1 collective-permute-done.20
  466.8 14.4 %shard_map.180 = (f32[1024,1024]{1,0:T(8,128)}, f32[2,1024]{1,0:T(2,128)S(1)}) custom-call(bf16[1024,1024]{1,0:T(8,128)(2,1)S(1)} %copy-done.26, f32[1024,1024]{1,0:T(8,128)} %get-tuple-element.39.gm_ref, bf16[1024,1024]{1,0:T(8,128)(2,1)} %copy-done.38, bf16[1024,1024]{1,0:T(8,128)(2,1)} %get-tuple-element.43.dk_ref.refs_1_, ...), custom_call_target="tpu_custom_call" | custom-call | flops 6442450944 | bytes 23068672 | tf_op jit(solution)/shard_map/pallas_call | solution.py:384
  482.2 3.9 fusion
  493.0 9.9 %collective-permute-done.38 = bf16[72,1024]{1,0:T(8,128)(2,1)} collective-permute-done((bf16[72,1024]{1,0:T(8,128)(2,1)S(1)}, bf16[72,1024]{1,0:T(8,128)(2,1)}, u32[]{:S(2)}, u32[]{:S(2)}) %collective-permute-start.38) | collective-permute-done | bytes 147488 | tf_op jit(solution)/shard_map/ppermute | solution.py:482
  507.2 3.1 collective-permute-done.40
  512.5 4.8 collective-permute-done.41
  518.0 6.4 shard_map.177
  524.4 102.2 %reduce-scatter.4.cloned.1.call-done = f32[32,4]{1,0:T(8,128)} async-done(((f32[1024,4]{1,0:T(8,128)}), f32[32,4]{1,0:T(8,128)}) %reduce-scatter.4.cloned.1.call-update) | async-done | bytes 528
  633.0 2.6 fusion.5
  644.2 12.8 %collective-permute-done.66 = bf16[512,1024]{1,0:T(8,128)(2,1)S(1)} collective-permute-done((bf16[512,1024]{1,0:T(8,128)(2,1)S(1)}, bf16[512,1024]{1,0:T(8,128)(2,1)S(1)}, u32[]{:S(2)}, u32[]{:S(2)}) %collective-permute-start.66) | collective-permute-done | bytes 1048608 | tf_op jit(solution)/shard_map/ppermute | solution.py:482
  660.9 18.5 %collective-permute-done.58 = bf16[2,2,128,1024]{3,2,1,0:T(8,128)(2,1)S(1)} collective-permute-done((bf16[2,2,128,1024]{3,2,1,0:T(8,128)(2,1)S(1)}, bf16[2,2,128,1024]{3,2,1,0:T(8,128)(2,1)S(1)}, u32[]{:S(2)}, u32[]{:S(2)}) %collective-permute-start.58) | collective-permute-done | bytes 1048608 | tf_op jit(solution)/shard_map/ppermute | solution.py:482
  680.0 15.6 %collective-permute-done.62 = bf16[512,1024]{1,0:T(8,128)(2,1)S(1)} collective-permute-done((bf16[512,1024]{1,0:T(8,128)(2,1)S(1)}, bf16[512,1024]{1,0:T(8,128)(2,1)S(1)}, u32[]{:S(2)}, u32[]{:S(2)}) %collective-permute-start.62) | collective-permute-done | bytes 1048608 | tf_op jit(solution)/shard_map/ppermute | solution.py:482
  699.5 2.5 maximum_bitcast_fusion.1
  702.0 2.5 maximum_bitcast_fusion
  (311 shorter events, 104.6 us)
Async XLA Ops:
  7.2 619.4 %reduce-scatter.4.cloned.1.call-start = ((), (), s32[]{:S(2)}) async-start(), calls=%async_computation.1 | async-start | bytes 540672
  71.2 11.8 %collective-permute-start = (bf16[72,1024]{1,0:T(8,128)(2,1)S(1)}, bf16[72,1024]{1,0:T(8,128)(2,1)S(1)}, u32[]{:S(2)}, u32[]{:S(2)}) collective-permute-start(bf16[72,1024]{1,0:T(8,128)(2,1)S(1)} %get-tuple-element.84), channel_id=1, source_target_pairs={{0,1},{1,0},{2,3},{3,2},{4,5},{5,4},{6,7},{7,6},{8,9},{9,8},{10,11... | collective-permute-start | bytes 442376 | tf_op jit(solution)/shard_map/ppermute | solution.py:482
  71.7 15.0 %collective-permute-start.1 = (bf16[72,1024]{1,0:T(8,128)(2,1)S(1)}, bf16[72,1024]{1,0:T(8,128)(2,1)S(1)}, u32[]{:S(2)}, u32[]{:S(2)}) collective-permute-start(bf16[72,1024]{1,0:T(8,128)(2,1)S(1)} %get-tuple-element.83), channel_id=1, source_target_pairs={{0,2},{1,3},{2,0},{3,1},{4,6},{5,7},{6,4},{7,5},{8,10},{9,11},{10,... | collective-permute-start | bytes 442376 | tf_op jit(solution)/shard_map/ppermute | solution.py:482
  74.3 13.2 %collective-permute-start.2 = (bf16[72,1024]{1,0:T(8,128)(2,1)S(1)}, bf16[72,1024]{1,0:T(8,128)(2,1)S(1)}, u32[]{:S(2)}, u32[]{:S(2)}) collective-permute-start(bf16[72,1024]{1,0:T(8,128)(2,1)S(1)} %get-tuple-element.82), channel_id=1, source_target_pairs={{0,3},{1,2},{2,1},{3,0},{4,7},{5,6},{6,5},{7,4},{8,11},{9,10},{10,... | collective-permute-start | bytes 442376 | tf_op jit(solution)/shard_map/ppermute | solution.py:482
  74.4 13.3 %collective-permute-start.3 = (bf16[72,1024]{1,0:T(8,128)(2,1)S(1)}, bf16[72,1024]{1,0:T(8,128)(2,1)S(1)}, u32[]{:S(2)}, u32[]{:S(2)}) collective-permute-start(bf16[72,1024]{1,0:T(8,128)(2,1)S(1)} %get-tuple-element.81), channel_id=1, source_target_pairs={{0,4},{1,5},{2,6},{3,7},{4,0},{5,1},{6,2},{7,3},{8,12},{9,13},{10,... | collective-permute-start | bytes 442376 | tf_op jit(solution)/shard_map/ppermute | solution.py:482
  77.1 11.3 %collective-permute-start.4 = (bf16[72,1024]{1,0:T(8,128)(2,1)S(1)}, bf16[72,1024]{1,0:T(8,128)(2,1)S(1)}, u32[]{:S(2)}, u32[]{:S(2)}) collective-permute-start(bf16[72,1024]{1,0:T(8,128)(2,1)S(1)} %get-tuple-element.80), channel_id=1, source_target_pairs={{0,5},{1,4},{2,7},{3,6},{4,1},{5,0},{6,3},{7,2},{8,13},{9,12},{10,... | collective-permute-start | bytes 442376 | tf_op jit(solution)/shard_map/ppermute | solution.py:482
  83.0 14.4 %collective-permute-start.5 = (bf16[72,1024]{1,0:T(8,128)(2,1)S(1)}, bf16[72,1024]{1,0:T(8,128)(2,1)S(1)}, u32[]{:S(2)}, u32[]{:S(2)}) collective-permute-start(bf16[72,1024]{1,0:T(8,128)(2,1)S(1)} %get-tuple-element.79), channel_id=1, source_target_pairs={{0,6},{1,7},{2,4},{3,5},{4,2},{5,3},{6,0},{7,1},{8,14},{9,15},{10,... | collective-permute-start | bytes 442376 | tf_op jit(solution)/shard_map/ppermute | solution.py:482
  86.6 17.2 %collective-permute-start.6 = (bf16[72,1024]{1,0:T(8,128)(2,1)S(1)}, bf16[72,1024]{1,0:T(8,128)(2,1)S(1)}, u32[]{:S(2)}, u32[]{:S(2)}) collective-permute-start(bf16[72,1024]{1,0:T(8,128)(2,1)S(1)} %get-tuple-element.78), channel_id=1, source_target_pairs={{0,7},{1,6},{2,5},{3,4},{4,3},{5,2},{6,1},{7,0},{8,15},{9,14},{10,... | collective-permute-start | bytes 442376 | tf_op jit(solution)/shard_map/ppermute | solution.py:482
  87.5 23.7 %collective-permute-start.7 = (bf16[72,1024]{1,0:T(8,128)(2,1)S(1)}, bf16[72,1024]{1,0:T(8,128)(2,1)S(1)}, u32[]{:S(2)}, u32[]{:S(2)}) collective-permute-start(bf16[72,1024]{1,0:T(8,128)(2,1)S(1)} %get-tuple-element.68), channel_id=1, source_target_pairs={{0,1},{1,0},{2,3},{3,2},{4,5},{5,4},{6,7},{7,6},{8,9},{9,8},{10,11... | collective-permute-start | bytes 442376 | tf_op jit(solution)/shard_map/ppermute | solution.py:482
  87.7 23.7 %collective-permute-start.8 = (bf16[72,1024]{1,0:T(8,128)(2,1)S(1)}, bf16[72,1024]{1,0:T(8,128)(2,1)S(1)}, u32[]{:S(2)}, u32[]{:S(2)}) collective-permute-start(bf16[72,1024]{1,0:T(8,128)(2,1)S(1)} %get-tuple-element.67), channel_id=1, source_target_pairs={{0,2},{1,3},{2,0},{3,1},{4,6},{5,7},{6,4},{7,5},{8,10},{9,11},{10,... | collective-permute-start | bytes 442376 | tf_op jit(solution)/shard_map/ppermute | solution.py:482
  88.4 23.0 %collective-permute-start.9 = (bf16[72,1024]{1,0:T(8,128)(2,1)S(1)}, bf16[72,1024]{1,0:T(8,128)(2,1)S(1)}, u32[]{:S(2)}, u32[]{:S(2)}) collective-permute-start(bf16[72,1024]{1,0:T(8,128)(2,1)S(1)} %get-tuple-element.66), channel_id=1, source_target_pairs={{0,3},{1,2},{2,1},{3,0},{4,7},{5,6},{6,5},{7,4},{8,11},{9,10},{10,... | collective-permute-start | bytes 442376 | tf_op jit(solution)/shard_map/ppermute | solution.py:482
  97.4 18.9 %collective-permute-start.10 = (bf16[72,1024]{1,0:T(8,128)(2,1)S(1)}, bf16[72,1024]{1,0:T(8,128)(2,1)S(1)}, u32[]{:S(2)}, u32[]{:S(2)}) collective-permute-start(bf16[72,1024]{1,0:T(8,128)(2,1)S(1)} %get-tuple-element.65), channel_id=1, source_target_pairs={{0,4},{1,5},{2,6},{3,7},{4,0},{5,1},{6,2},{7,3},{8,12},{9,13},{10,... | collective-permute-start | bytes 442376 | tf_op jit(solution)/shard_map/ppermute | solution.py:482
  103.9 16.9 %collective-permute-start.11 = (bf16[72,1024]{1,0:T(8,128)(2,1)S(1)}, bf16[72,1024]{1,0:T(8,128)(2,1)S(1)}, u32[]{:S(2)}, u32[]{:S(2)}) collective-permute-start(bf16[72,1024]{1,0:T(8,128)(2,1)S(1)} %get-tuple-element.64), channel_id=1, source_target_pairs={{0,5},{1,4},{2,7},{3,6},{4,1},{5,0},{6,3},{7,2},{8,13},{9,12},{10,... | collective-permute-start | bytes 442376 | tf_op jit(solution)/shard_map/ppermute | solution.py:482
  111.2 11.5 %collective-permute-start.12 = (bf16[72,1024]{1,0:T(8,128)(2,1)S(1)}, bf16[72,1024]{1,0:T(8,128)(2,1)S(1)}, u32[]{:S(2)}, u32[]{:S(2)}) collective-permute-start(bf16[72,1024]{1,0:T(8,128)(2,1)S(1)} %get-tuple-element.63), channel_id=1, source_target_pairs={{0,6},{1,7},{2,4},{3,5},{4,2},{5,3},{6,0},{7,1},{8,14},{9,15},{10,... | collective-permute-start | bytes 442376 | tf_op jit(solution)/shard_map/ppermute | solution.py:482
  111.3 17.9 %collective-permute-start.13 = (bf16[72,1024]{1,0:T(8,128)(2,1)S(1)}, bf16[72,1024]{1,0:T(8,128)(2,1)S(1)}, u32[]{:S(2)}, u32[]{:S(2)}) collective-permute-start(bf16[72,1024]{1,0:T(8,128)(2,1)S(1)} %get-tuple-element.62), channel_id=1, source_target_pairs={{0,7},{1,6},{2,5},{3,4},{4,3},{5,2},{6,1},{7,0},{8,15},{9,14},{10,... | collective-permute-start | bytes 442376 | tf_op jit(solution)/shard_map/ppermute | solution.py:482
  111.5 55.4 %collective-permute-start.21 = (bf16[72,1024]{1,0:T(8,128)(2,1)S(1)}, bf16[72,1024]{1,0:T(8,128)(2,1)S(1)}, u32[]{:S(2)}, u32[]{:S(2)}) collective-permute-start(bf16[72,1024]{1,0:T(8,128)(2,1)S(1)} %get-tuple-element.76), channel_id=1, source_target_pairs={{0,1},{1,0},{2,3},{3,2},{4,5},{5,4},{6,7},{7,6},{8,9},{9,8},{10,11... | collective-permute-start | bytes 442376 | tf_op jit(solution)/shard_map/ppermute | solution.py:482
  116.3 50.6 %collective-permute-start.22 = (bf16[72,1024]{1,0:T(8,128)(2,1)S(1)}, bf16[72,1024]{1,0:T(8,128)(2,1)S(1)}, u32[]{:S(2)}, u32[]{:S(2)}) collective-permute-start(bf16[72,1024]{1,0:T(8,128)(2,1)S(1)} %get-tuple-element.75), channel_id=1, source_target_pairs={{0,2},{1,3},{2,0},{3,1},{4,6},{5,7},{6,4},{7,5},{8,10},{9,11},{10,... | collective-permute-start | bytes 442376 | tf_op jit(solution)/shard_map/ppermute | solution.py:482
  120.8 46.2 %collective-permute-start.23 = (bf16[72,1024]{1,0:T(8,128)(2,1)S(1)}, bf16[72,1024]{1,0:T(8,128)(2,1)S(1)}, u32[]{:S(2)}, u32[]{:S(2)}) collective-permute-start(bf16[72,1024]{1,0:T(8,128)(2,1)S(1)} %get-tuple-element.74), channel_id=1, source_target_pairs={{0,3},{1,2},{2,1},{3,0},{4,7},{5,6},{6,5},{7,4},{8,11},{9,10},{10,... | collective-permute-start | bytes 442376 | tf_op jit(solution)/shard_map/ppermute | solution.py:482
  122.7 48.3 %collective-permute-start.24 = (bf16[72,1024]{1,0:T(8,128)(2,1)S(1)}, bf16[72,1024]{1,0:T(8,128)(2,1)S(1)}, u32[]{:S(2)}, u32[]{:S(2)}) collective-permute-start(bf16[72,1024]{1,0:T(8,128)(2,1)S(1)} %get-tuple-element.73), channel_id=1, source_target_pairs={{0,4},{1,5},{2,6},{3,7},{4,0},{5,1},{6,2},{7,3},{8,12},{9,13},{10,... | collective-permute-start | bytes 442376 | tf_op jit(solution)/shard_map/ppermute | solution.py:482
  129.2 41.9 %collective-permute-start.25 = (bf16[72,1024]{1,0:T(8,128)(2,1)S(1)}, bf16[72,1024]{1,0:T(8,128)(2,1)S(1)}, u32[]{:S(2)}, u32[]{:S(2)}) collective-permute-start(bf16[72,1024]{1,0:T(8,128)(2,1)S(1)} %get-tuple-element.72), channel_id=1, source_target_pairs={{0,5},{1,4},{2,7},{3,6},{4,1},{5,0},{6,3},{7,2},{8,13},{9,12},{10,... | collective-permute-start | bytes 442376 | tf_op jit(solution)/shard_map/ppermute | solution.py:482
  166.8 8.6 %collective-permute-start.26 = (bf16[72,1024]{1,0:T(8,128)(2,1)S(1)}, bf16[72,1024]{1,0:T(8,128)(2,1)S(1)}, u32[]{:S(2)}, u32[]{:S(2)}) collective-permute-start(bf16[72,1024]{1,0:T(8,128)(2,1)S(1)} %get-tuple-element.71), channel_id=1, source_target_pairs={{0,6},{1,7},{2,4},{3,5},{4,2},{5,3},{6,0},{7,1},{8,14},{9,15},{10,... | collective-permute-start | bytes 442376 | tf_op jit(solution)/shard_map/ppermute | solution.py:482
  166.9 8.5 %collective-permute-start.27 = (bf16[72,1024]{1,0:T(8,128)(2,1)S(1)}, bf16[72,1024]{1,0:T(8,128)(2,1)S(1)}, u32[]{:S(2)}, u32[]{:S(2)}) collective-permute-start(bf16[72,1024]{1,0:T(8,128)(2,1)S(1)} %get-tuple-element.70), channel_id=1, source_target_pairs={{0,7},{1,6},{2,5},{3,4},{4,3},{5,2},{6,1},{7,0},{8,15},{9,14},{10,... | collective-permute-start | bytes 442376 | tf_op jit(solution)/shard_map/ppermute | solution.py:482
  167.0 11.1 %collective-permute-start.28 = (bf16[72,1024]{1,0:T(8,128)(2,1)S(1)}, bf16[72,1024]{1,0:T(8,128)(2,1)S(1)}, u32[]{:S(2)}, u32[]{:S(2)}) collective-permute-start(bf16[72,1024]{1,0:T(8,128)(2,1)S(1)} %get-tuple-element.60), channel_id=1, source_target_pairs={{0,1},{1,0},{2,3},{3,2},{4,5},{5,4},{6,7},{7,6},{8,9},{9,8},{10,11... | collective-permute-start | bytes 442376 | tf_op jit(solution)/shard_map/ppermute | solution.py:482
  171.0 13.3 %collective-permute-start.29 = (bf16[72,1024]{1,0:T(8,128)(2,1)S(1)}, bf16[72,1024]{1,0:T(8,128)(2,1)S(1)}, u32[]{:S(2)}, u32[]{:S(2)}) collective-permute-start(bf16[72,1024]{1,0:T(8,128)(2,1)S(1)} %get-tuple-element.59), channel_id=1, source_target_pairs={{0,2},{1,3},{2,0},{3,1},{4,6},{5,7},{6,4},{7,5},{8,10},{9,11},{10,... | collective-permute-start | bytes 442376 | tf_op jit(solution)/shard_map/ppermute | solution.py:482
  171.1 16.6 %collective-permute-start.30 = (bf16[72,1024]{1,0:T(8,128)(2,1)S(1)}, bf16[72,1024]{1,0:T(8,128)(2,1)S(1)}, u32[]{:S(2)}, u32[]{:S(2)}) collective-permute-start(bf16[72,1024]{1,0:T(8,128)(2,1)S(1)} %get-tuple-element.58), channel_id=1, source_target_pairs={{0,3},{1,2},{2,1},{3,0},{4,7},{5,6},{6,5},{7,4},{8,11},{9,10},{10,... | collective-permute-start | bytes 442376 | tf_op jit(solution)/shard_map/ppermute | solution.py:482
  175.4 20.4 %collective-permute-start.31 = (bf16[72,1024]{1,0:T(8,128)(2,1)S(1)}, bf16[72,1024]{1,0:T(8,128)(2,1)S(1)}, u32[]{:S(2)}, u32[]{:S(2)}) collective-permute-start(bf16[72,1024]{1,0:T(8,128)(2,1)S(1)} %get-tuple-element.57), channel_id=1, source_target_pairs={{0,4},{1,5},{2,6},{3,7},{4,0},{5,1},{6,2},{7,3},{8,12},{9,13},{10,... | collective-permute-start | bytes 442376 | tf_op jit(solution)/shard_map/ppermute | solution.py:482
  175.4 20.4 %collective-permute-start.32 = (bf16[72,1024]{1,0:T(8,128)(2,1)S(1)}, bf16[72,1024]{1,0:T(8,128)(2,1)S(1)}, u32[]{:S(2)}, u32[]{:S(2)}) collective-permute-start(bf16[72,1024]{1,0:T(8,128)(2,1)S(1)} %get-tuple-element.56), channel_id=1, source_target_pairs={{0,5},{1,4},{2,7},{3,6},{4,1},{5,0},{6,3},{7,2},{8,13},{9,12},{10,... | collective-permute-start | bytes 442376 | tf_op jit(solution)/shard_map/ppermute | solution.py:482
  178.2 18.9 %collective-permute-start.33 = (bf16[72,1024]{1,0:T(8,128)(2,1)S(1)}, bf16[72,1024]{1,0:T(8,128)(2,1)S(1)}, u32[]{:S(2)}, u32[]{:S(2)}) collective-permute-start(bf16[72,1024]{1,0:T(8,128)(2,1)S(1)} %get-tuple-element.55), channel_id=1, source_target_pairs={{0,6},{1,7},{2,4},{3,5},{4,2},{5,3},{6,0},{7,1},{8,14},{9,15},{10,... | collective-permute-start | bytes 442376 | tf_op jit(solution)/shard_map/ppermute | solution.py:482
  184.3 17.1 %collective-permute-start.34 = (bf16[72,1024]{1,0:T(8,128)(2,1)S(1)}, bf16[72,1024]{1,0:T(8,128)(2,1)S(1)}, u32[]{:S(2)}, u32[]{:S(2)}) collective-permute-start(bf16[72,1024]{1,0:T(8,128)(2,1)S(1)} %get-tuple-element.54), channel_id=1, source_target_pairs={{0,7},{1,6},{2,5},{3,4},{4,3},{5,2},{6,1},{7,0},{8,15},{9,14},{10,... | collective-permute-start | bytes 442376 | tf_op jit(solution)/shard_map/ppermute | solution.py:482
  187.8 45.7 %collective-permute-start.42 = (bf16[72,1024]{1,0:T(8,128)(2,1)S(1)}, bf16[72,1024]{1,0:T(8,128)(2,1)S(1)}, u32[]{:S(2)}, u32[]{:S(2)}) collective-permute-start(bf16[72,1024]{1,0:T(8,128)(2,1)S(1)} %get-tuple-element.100), channel_id=1, source_target_pairs={{0,1},{1,0},{2,3},{3,2},{4,5},{5,4},{6,7},{7,6},{8,9},{9,8},{10,11... | collective-permute-start | bytes 442376 | tf_op jit(solution)/shard_map/ppermute | solution.py:482
  195.8 40.3 %collective-permute-start.43 = (bf16[72,1024]{1,0:T(8,128)(2,1)S(1)}, bf16[72,1024]{1,0:T(8,128)(2,1)S(1)}, u32[]{:S(2)}, u32[]{:S(2)}) collective-permute-start(bf16[72,1024]{1,0:T(8,128)(2,1)S(1)} %get-tuple-element.99), channel_id=1, source_target_pairs={{0,2},{1,3},{2,0},{3,1},{4,6},{5,7},{6,4},{7,5},{8,10},{9,11},{10,... | collective-permute-start | bytes 442376 | tf_op jit(solution)/shard_map/ppermute | solution.py:482
  195.8 42.2 %collective-permute-start.44 = (bf16[72,1024]{1,0:T(8,128)(2,1)S(1)}, bf16[72,1024]{1,0:T(8,128)(2,1)S(1)}, u32[]{:S(2)}, u32[]{:S(2)}) collective-permute-start(bf16[72,1024]{1,0:T(8,128)(2,1)S(1)} %get-tuple-element.98), channel_id=1, source_target_pairs={{0,3},{1,2},{2,1},{3,0},{4,7},{5,6},{6,5},{7,4},{8,11},{9,10},{10,... | collective-permute-start | bytes 442376 | tf_op jit(solution)/shard_map/ppermute | solution.py:482
  197.0 41.0 %collective-permute-start.45 = (bf16[72,1024]{1,0:T(8,128)(2,1)S(1)}, bf16[72,1024]{1,0:T(8,128)(2,1)S(1)}, u32[]{:S(2)}, u32[]{:S(2)}) collective-permute-start(bf16[72,1024]{1,0:T(8,128)(2,1)S(1)} %get-tuple-element.97), channel_id=1, source_target_pairs={{0,4},{1,5},{2,6},{3,7},{4,0},{5,1},{6,2},{7,3},{8,12},{9,13},{10,... | collective-permute-start | bytes 442376 | tf_op jit(solution)/shard_map/ppermute | solution.py:482
  201.4 36.6 %collective-permute-start.46 = (bf16[72,1024]{1,0:T(8,128)(2,1)S(1)}, bf16[72,1024]{1,0:T(8,128)(2,1)S(1)}, u32[]{:S(2)}, u32[]{:S(2)}) collective-permute-start(bf16[72,1024]{1,0:T(8,128)(2,1)S(1)} %get-tuple-element.96), channel_id=1, source_target_pairs={{0,5},{1,4},{2,7},{3,6},{4,1},{5,0},{6,3},{7,2},{8,13},{9,12},{10,... | collective-permute-start | bytes 442376 | tf_op jit(solution)/shard_map/ppermute | solution.py:482
  233.5 8.5 %collective-permute-start.47 = (bf16[72,1024]{1,0:T(8,128)(2,1)S(1)}, bf16[72,1024]{1,0:T(8,128)(2,1)S(1)}, u32[]{:S(2)}, u32[]{:S(2)}) collective-permute-start(bf16[72,1024]{1,0:T(8,128)(2,1)S(1)} %get-tuple-element.95), channel_id=1, source_target_pairs={{0,6},{1,7},{2,4},{3,5},{4,2},{5,3},{6,0},{7,1},{8,14},{9,15},{10,... | collective-permute-start | bytes 442376 | tf_op jit(solution)/shard_map/ppermute | solution.py:482
  236.0 9.3 %collective-permute-start.48 = (bf16[72,1024]{1,0:T(8,128)(2,1)S(1)}, bf16[72,1024]{1,0:T(8,128)(2,1)S(1)}, u32[]{:S(2)}, u32[]{:S(2)}) collective-permute-start(bf16[72,1024]{1,0:T(8,128)(2,1)S(1)} %get-tuple-element.94), channel_id=1, source_target_pairs={{0,7},{1,6},{2,5},{3,4},{4,3},{5,2},{6,1},{7,0},{8,15},{9,14},{10,... | collective-permute-start | bytes 442376 | tf_op jit(solution)/shard_map/ppermute | solution.py:482
  247.5 13.8 %collective-permute-start.50 = (bf16[72,1024]{1,0:T(8,128)(2,1)S(1)}, bf16[72,1024]{1,0:T(8,128)(2,1)S(1)}, u32[]{:S(2)}, u32[]{:S(2)}) collective-permute-start(bf16[72,1024]{1,0:T(8,128)(2,1)S(1)} %get-tuple-element.91), channel_id=1, source_target_pairs={{0,2},{1,3},{2,0},{3,1},{4,6},{5,7},{6,4},{7,5},{8,10},{9,11},{10,... | collective-permute-start | bytes 442376 | tf_op jit(solution)/shard_map/ppermute | solution.py:482
  251.9 12.5 %collective-permute-start.51 = (bf16[72,1024]{1,0:T(8,128)(2,1)S(1)}, bf16[72,1024]{1,0:T(8,128)(2,1)S(1)}, u32[]{:S(2)}, u32[]{:S(2)}) collective-permute-start(bf16[72,1024]{1,0:T(8,128)(2,1)S(1)} %get-tuple-element.90), channel_id=1, source_target_pairs={{0,3},{1,2},{2,1},{3,0},{4,7},{5,6},{6,5},{7,4},{8,11},{9,10},{10,... | collective-permute-start | bytes 442376 | tf_op jit(solution)/shard_map/ppermute | solution.py:482
  252.1 13.0 %collective-permute-start.52 = (bf16[72,1024]{1,0:T(8,128)(2,1)S(1)}, bf16[72,1024]{1,0:T(8,128)(2,1)S(1)}, u32[]{:S(2)}, u32[]{:S(2)}) collective-permute-start(bf16[72,1024]{1,0:T(8,128)(2,1)S(1)} %get-tuple-element.89), channel_id=1, source_target_pairs={{0,4},{1,5},{2,6},{3,7},{4,0},{5,1},{6,2},{7,3},{8,12},{9,13},{10,... | collective-permute-start | bytes 442376 | tf_op jit(solution)/shard_map/ppermute | solution.py:482
  254.3 19.8 %collective-permute-start.53 = (bf16[72,1024]{1,0:T(8,128)(2,1)S(1)}, bf16[72,1024]{1,0:T(8,128)(2,1)S(1)}, u32[]{:S(2)}, u32[]{:S(2)}) collective-permute-start(bf16[72,1024]{1,0:T(8,128)(2,1)S(1)} %get-tuple-element.88), channel_id=1, source_target_pairs={{0,5},{1,4},{2,7},{3,6},{4,1},{5,0},{6,3},{7,2},{8,13},{9,12},{10,... | collective-permute-start | bytes 442376 | tf_op jit(solution)/shard_map/ppermute | solution.py:482
  254.5 20.2 %collective-permute-start.54 = (bf16[72,1024]{1,0:T(8,128)(2,1)S(1)}, bf16[72,1024]{1,0:T(8,128)(2,1)S(1)}, u32[]{:S(2)}, u32[]{:S(2)}) collective-permute-start(bf16[72,1024]{1,0:T(8,128)(2,1)S(1)} %get-tuple-element.87), channel_id=1, source_target_pairs={{0,6},{1,7},{2,4},{3,5},{4,2},{5,3},{6,0},{7,1},{8,14},{9,15},{10,... | collective-permute-start | bytes 442376 | tf_op jit(solution)/shard_map/ppermute | solution.py:482
  261.3 14.1 %collective-permute-start.55 = (bf16[72,1024]{1,0:T(8,128)(2,1)S(1)}, bf16[72,1024]{1,0:T(8,128)(2,1)S(1)}, u32[]{:S(2)}, u32[]{:S(2)}) collective-permute-start(bf16[72,1024]{1,0:T(8,128)(2,1)S(1)} %get-tuple-element.86), channel_id=1, source_target_pairs={{0,7},{1,6},{2,5},{3,4},{4,3},{5,2},{6,1},{7,0},{8,15},{9,14},{10,... | collective-permute-start | bytes 442376 | tf_op jit(solution)/shard_map/ppermute | solution.py:482
  366.8 114.3 %collective-permute-start.56 = (bf16[2,2,2,2,128,1024]{5,4,3,2,1,0:T(8,128)(2,1)}, bf16[2,2,2,2,128,1024]{5,4,3,2,1,0:T(8,128)(2,1)}, u32[]{:S(2)}, u32[]{:S(2)}) collective-permute-start(bf16[2,2,2,2,128,1024]{5,4,3,2,1,0:T(8,128)(2,1)} %fusion.2), channel_id=1, source_target_pairs={{0,1},{1,0},{2,3},{3,2},{4,5},{5,4},{6,7},{7,6},{8,9},{9,8},{10,11... | collective-permute-start | bytes 12582920 | tf_op jit(solution)/shard_map/ppermute | solution.py:482
  379.0 249.6 %collective-permute-start.65 = (bf16[2,512,1024]{2,1,0:T(8,128)(2,1)}, bf16[2,512,1024]{2,1,0:T(8,128)(2,1)}, u32[]{:S(2)}, u32[]{:S(2)}) collective-permute-start(bf16[2,512,1024]{2,1,0:T(8,128)(2,1)} %shard_map.190), channel_id=1, source_target_pairs={{0,8},{8,0},{16,24},{24,16},{1,9},{9,1},{17,25},{25,17},{2,10},{10... | collective-permute-start | bytes 6291464 | tf_op jit(solution)/shard_map/ppermute | solution.py:482
  387.1 244.2 %collective-permute-start.67 = (bf16[2,512,1024]{2,1,0:T(8,128)(2,1)}, bf16[2,512,1024]{2,1,0:T(8,128)(2,1)}, u32[]{:S(2)}, u32[]{:S(2)}) collective-permute-start(bf16[2,512,1024]{2,1,0:T(8,128)(2,1)} %shard_map.192), channel_id=1, source_target_pairs={{0,16},{8,24},{16,0},{24,8},{1,17},{9,25},{17,1},{25,9},{2,18},{10... | collective-permute-start | bytes 6291464 | tf_op jit(solution)/shard_map/ppermute | solution.py:482
  388.7 46.2 %collective-permute-start.14 = (bf16[72,1024]{1,0:T(8,128)(2,1)S(1)}, bf16[72,1024]{1,0:T(8,128)(2,1)S(1)}, u32[]{:S(2)}, u32[]{:S(2)}) collective-permute-start(bf16[72,1024]{1,0:T(8,128)(2,1)S(1)} %get-tuple-element.116), channel_id=1, source_target_pairs={{0,1},{1,0},{2,3},{3,2},{4,5},{5,4},{6,7},{7,6},{8,9},{9,8},{10,11... | collective-permute-start | bytes 442376 | tf_op jit(solution)/shard_map/ppermute | solution.py:482
  388.8 46.2 %collective-permute-start.15 = (bf16[72,1024]{1,0:T(8,128)(2,1)S(1)}, bf16[72,1024]{1,0:T(8,128)(2,1)S(1)}, u32[]{:S(2)}, u32[]{:S(2)}) collective-permute-start(bf16[72,1024]{1,0:T(8,128)(2,1)S(1)} %get-tuple-element.115), channel_id=1, source_target_pairs={{0,2},{1,3},{2,0},{3,1},{4,6},{5,7},{6,4},{7,5},{8,10},{9,11},{10,... | collective-permute-start | bytes 442376 | tf_op jit(solution)/shard_map/ppermute | solution.py:482
  435.0 10.1 %collective-permute-start.17 = (bf16[72,1024]{1,0:T(8,128)(2,1)S(1)}, bf16[72,1024]{1,0:T(8,128)(2,1)S(1)}, u32[]{:S(2)}, u32[]{:S(2)}) collective-permute-start(bf16[72,1024]{1,0:T(8,128)(2,1)S(1)} %get-tuple-element.113), channel_id=1, source_target_pairs={{0,4},{1,5},{2,6},{3,7},{4,0},{5,1},{6,2},{7,3},{8,12},{9,13},{10,... | collective-permute-start | bytes 442376 | tf_op jit(solution)/shard_map/ppermute | solution.py:482
  443.1 12.6 %collective-permute-start.18 = (bf16[72,1024]{1,0:T(8,128)(2,1)S(1)}, bf16[72,1024]{1,0:T(8,128)(2,1)S(1)}, u32[]{:S(2)}, u32[]{:S(2)}) collective-permute-start(bf16[72,1024]{1,0:T(8,128)(2,1)S(1)} %get-tuple-element.112), channel_id=1, source_target_pairs={{0,5},{1,4},{2,7},{3,6},{4,1},{5,0},{6,3},{7,2},{8,13},{9,12},{10,... | collective-permute-start | bytes 442376 | tf_op jit(solution)/shard_map/ppermute | solution.py:482
  445.1 12.4 %collective-permute-start.19 = (bf16[72,1024]{1,0:T(8,128)(2,1)S(1)}, bf16[72,1024]{1,0:T(8,128)(2,1)S(1)}, u32[]{:S(2)}, u32[]{:S(2)}) collective-permute-start(bf16[72,1024]{1,0:T(8,128)(2,1)S(1)} %get-tuple-element.111), channel_id=1, source_target_pairs={{0,6},{1,7},{2,4},{3,5},{4,2},{5,3},{6,0},{7,1},{8,14},{9,15},{10,... | collective-permute-start | bytes 442376 | tf_op jit(solution)/shard_map/ppermute | solution.py:482
  464.3 24.6 %collective-permute-start.35 = (bf16[72,1024]{1,0:T(8,128)(2,1)S(1)}, bf16[72,1024]{1,0:T(8,128)(2,1)}, u32[]{:S(2)}, u32[]{:S(2)}) collective-permute-start(bf16[72,1024]{1,0:T(8,128)(2,1)S(1)} %get-tuple-element.108), channel_id=1, source_target_pairs={{0,1},{1,0},{2,3},{3,2},{4,5},{5,4},{6,7},{7,6},{8,9},{9,8},{10,11... | collective-permute-start | bytes 442376 | tf_op jit(solution)/shard_map/ppermute | solution.py:482
  464.4 25.7 %collective-permute-start.36 = (bf16[72,1024]{1,0:T(8,128)(2,1)S(1)}, bf16[72,1024]{1,0:T(8,128)(2,1)}, u32[]{:S(2)}, u32[]{:S(2)}) collective-permute-start(bf16[72,1024]{1,0:T(8,128)(2,1)S(1)} %get-tuple-element.107), channel_id=1, source_target_pairs={{0,2},{1,3},{2,0},{3,1},{4,6},{5,7},{6,4},{7,5},{8,10},{9,11},{10,... | collective-permute-start | bytes 442376 | tf_op jit(solution)/shard_map/ppermute | solution.py:482
  481.1 10.6 %collective-permute-start.37 = (bf16[72,1024]{1,0:T(8,128)(2,1)}, bf16[72,1024]{1,0:T(8,128)(2,1)}, u32[]{:S(2)}, u32[]{:S(2)}) collective-permute-start(bf16[72,1024]{1,0:T(8,128)(2,1)} %get-tuple-element.106), channel_id=1, source_target_pairs={{0,3},{1,2},{2,1},{3,0},{4,7},{5,6},{6,5},{7,4},{8,11},{9,10},{10,... | collective-permute-start | bytes 442376 | tf_op jit(solution)/shard_map/ppermute | solution.py:482
  488.9 14.0 %collective-permute-start.38 = (bf16[72,1024]{1,0:T(8,128)(2,1)S(1)}, bf16[72,1024]{1,0:T(8,128)(2,1)}, u32[]{:S(2)}, u32[]{:S(2)}) collective-permute-start(bf16[72,1024]{1,0:T(8,128)(2,1)S(1)} %get-tuple-element.105), channel_id=1, source_target_pairs={{0,4},{1,5},{2,6},{3,7},{4,0},{5,1},{6,2},{7,3},{8,12},{9,13},{10,... | collective-permute-start | bytes 442376 | tf_op jit(solution)/shard_map/ppermute | solution.py:482
  490.1 142.9 %collective-permute-start.57 = (bf16[2,2,2,128,1024]{4,3,2,1,0:T(8,128)(2,1)}, bf16[2,2,2,128,1024]{4,3,2,1,0:T(8,128)(2,1)}, u32[]{:S(2)}, u32[]{:S(2)}) collective-permute-start(bf16[2,2,2,128,1024]{4,3,2,1,0:T(8,128)(2,1)} %dynamic-slice_bitcast_fusion), channel_id=1, source_target_pairs={{0,8},{8,0},{16,24},{24,16},{1,9},{9,1},{17,25},{25,17},{2,10},{10... | collective-permute-start | bytes 6291464 | tf_op jit(solution)/shard_map/ppermute | solution.py:482
  491.7 15.0 %collective-permute-start.39 = (bf16[72,1024]{1,0:T(8,128)(2,1)S(1)}, bf16[72,1024]{1,0:T(8,128)(2,1)S(1)}, u32[]{:S(2)}, u32[]{:S(2)}) collective-permute-start(bf16[72,1024]{1,0:T(8,128)(2,1)S(1)} %get-tuple-element.104), channel_id=1, source_target_pairs={{0,5},{1,4},{2,7},{3,6},{4,1},{5,0},{6,3},{7,2},{8,13},{9,12},{10,... | collective-permute-start | bytes 442376 | tf_op jit(solution)/shard_map/ppermute | solution.py:482
  506.7 130.7 %collective-permute-start.61 = (bf16[2,512,1024]{2,1,0:T(8,128)(2,1)}, bf16[2,512,1024]{2,1,0:T(8,128)(2,1)}, u32[]{:S(2)}, u32[]{:S(2)}) collective-permute-start(bf16[2,512,1024]{2,1,0:T(8,128)(2,1)} %shard_map.186), channel_id=1, source_target_pairs={{0,8},{8,0},{16,24},{24,16},{1,9},{9,1},{17,25},{25,17},{2,10},{10... | collective-permute-start | bytes 6291464 | tf_op jit(solution)/shard_map/ppermute | solution.py:482
  517.4 123.1 %collective-permute-start.63 = (bf16[2,512,1024]{2,1,0:T(8,128)(2,1)}, bf16[2,512,1024]{2,1,0:T(8,128)(2,1)}, u32[]{:S(2)}, u32[]{:S(2)}) collective-permute-start(bf16[2,512,1024]{2,1,0:T(8,128)(2,1)} %shard_map.188), channel_id=1, source_target_pairs={{0,16},{8,24},{16,0},{24,8},{1,17},{9,25},{17,1},{25,9},{2,18},{10... | collective-permute-start | bytes 6291464 | tf_op jit(solution)/shard_map/ppermute | solution.py:482
  630.8 26.2 %collective-permute-start.66 = (bf16[512,1024]{1,0:T(8,128)(2,1)S(1)}, bf16[512,1024]{1,0:T(8,128)(2,1)S(1)}, u32[]{:S(2)}, u32[]{:S(2)}) collective-permute-start(bf16[512,1024]{1,0:T(8,128)(2,1)S(1)} %fusion.9), channel_id=1, source_target_pairs={{0,16},{8,24},{16,0},{24,8},{1,17},{9,25},{17,1},{25,9},{2,18},{10... | collective-permute-start | bytes 3145736 | tf_op jit(solution)/shard_map/ppermute | solution.py:482
  632.9 26.2 %collective-permute-start.68 = (bf16[512,1024]{1,0:T(8,128)(2,1)S(1)}, bf16[512,1024]{1,0:T(8,128)(2,1)S(1)}, u32[]{:S(2)}, u32[]{:S(2)}) collective-permute-start(bf16[512,1024]{1,0:T(8,128)(2,1)S(1)} %fusion.10), channel_id=1, source_target_pairs={{0,8},{8,0},{16,24},{24,16},{1,9},{9,1},{17,25},{25,17},{2,10},{10... | collective-permute-start | bytes 3145736 | tf_op jit(solution)/shard_map/ppermute | solution.py:482
  635.7 43.7 %collective-permute-start.58 = (bf16[2,2,128,1024]{3,2,1,0:T(8,128)(2,1)S(1)}, bf16[2,2,128,1024]{3,2,1,0:T(8,128)(2,1)S(1)}, u32[]{:S(2)}, u32[]{:S(2)}) collective-permute-start(bf16[2,2,128,1024]{3,2,1,0:T(8,128)(2,1)S(1)} %dynamic-slice_bitcast_fusion.1), channel_id=1, source_target_pairs={{0,16},{8,24},{16,0},{24,8},{1,17},{9,25},{17,1},{25,9},{2,18},{10... | collective-permute-start | bytes 3145736 | tf_op jit(solution)/shard_map/ppermute | solution.py:482
  639.0 56.5 %collective-permute-start.62 = (bf16[512,1024]{1,0:T(8,128)(2,1)S(1)}, bf16[512,1024]{1,0:T(8,128)(2,1)S(1)}, u32[]{:S(2)}, u32[]{:S(2)}) collective-permute-start(bf16[512,1024]{1,0:T(8,128)(2,1)S(1)} %fusion.7), channel_id=1, source_target_pairs={{0,16},{8,24},{16,0},{24,8},{1,17},{9,25},{17,1},{25,9},{2,18},{10... | collective-permute-start | bytes 3145736 | tf_op jit(solution)/shard_map/ppermute | solution.py:482
  642.1 55.2 %collective-permute-start.64 = (bf16[512,1024]{1,0:T(8,128)(2,1)S(1)}, bf16[512,1024]{1,0:T(8,128)(2,1)S(1)}, u32[]{:S(2)}, u32[]{:S(2)}) collective-permute-start(bf16[512,1024]{1,0:T(8,128)(2,1)S(1)} %fusion.8), channel_id=1, source_target_pairs={{0,8},{8,0},{16,24},{24,16},{1,9},{9,1},{17,25},{25,17},{2,10},{10... | collective-permute-start | bytes 3145736 | tf_op jit(solution)/shard_map/ppermute | solution.py:482
  679.9 19.3 %collective-permute-start.59 = (bf16[2,128,1024]{2,1,0:T(8,128)(2,1)S(1)}, bf16[2,128,1024]{2,1,0:T(8,128)(2,1)S(1)}, u32[]{:S(2)}, u32[]{:S(2)}) collective-permute-start(bf16[2,128,1024]{2,1,0:T(8,128)(2,1)S(1)} %dynamic-slice_bitcast_fusion.2), channel_id=1, source_target_pairs={{0,2},{1,3},{2,0},{3,1},{4,6},{5,7},{6,4},{7,5},{8,10},{9,11},{10,... | collective-permute-start | bytes 1572872 | tf_op jit(solution)/shard_map/ppermute | solution.py:482
  (58 other events, 810.8 us)
Sparse Core Ops, SparseCore 0:
  491.8 134.6 reduce-scatter.3

commit v2 on v1

v2 whole, which is shorter than its diff:
```python
import functools

import jax
import jax.numpy as jnp
from jax import lax
from jax.experimental import pallas as pl
from jax.experimental.pallas import tpu as pltpu
from jax.sharding import PartitionSpec as P

HEADS = 16
EPSILON = 1e-05
NEGATIVE = -1e30
BAND = 512
BLOCK = 256
SUB = 256
F32 = jnp.float32
BF = jnp.bfloat16
VMEM_BYTES = 60 * 1024 * 1024


def mm(a, b):
    return lax.dot_general(a, b, (((1,), (0,)), ((), ())), preferred_element_type=F32)


def mm_nt(a, b):
    return lax.dot_general(a, b, (((1,), (1,)), ((), ())), preferred_element_type=F32)


def mm_tn(a, b):
    return lax.dot_general(a, b, (((0,), (0,)), ((), ())), preferred_element_type=F32)


def call(kernel, grid, in_specs, out_specs, out_shape, scratch=(), prefetch=0, aliases=None, after=(), cost=0):
    count = prefetch + len(in_specs)
    extra = len(after)

    def body(*refs):
        kernel(*refs[:count], *refs[count + extra :])

    run = pl.pallas_call(
        body,
        grid_spec=pltpu.PrefetchScalarGridSpec(
            num_scalar_prefetch=prefetch,
            grid=grid,
            in_specs=list(in_specs) + [pl.BlockSpec(memory_space=pl.ANY)] * extra,
            out_specs=out_specs,
            scratch_shapes=list(scratch),
        ),
        out_shape=out_shape,
        input_output_aliases=aliases or {},
        compiler_params=pltpu.CompilerParams(vmem_limit_bytes=VMEM_BYTES),
        cost_estimate=pl.CostEstimate(flops=1 + int(cost * 1.15e9), bytes_accessed=0, transcendentals=0),
    )
    return lambda *args: run(*args, *after)


def whole(shape):
    return pl.BlockSpec(shape, lambda *_: (0,) * len(shape))


def normalize(stream):
    average = jnp.mean(stream, axis=-1, keepdims=True)
    centered = stream - average
    inverse = lax.rsqrt(jnp.mean(centered * centered, axis=-1, keepdims=True) + EPSILON)
    return centered * inverse, inverse


def norm_back(unit, inverse, gain, grad):
    scaled = grad * gain
    first = jnp.mean(scaled, axis=-1, keepdims=True)
    second = jnp.mean(scaled * unit, axis=-1, keepdims=True)
    return inverse * (scaled - first - unit * second)


def first_norm_kernel(x_ref, g_ref, b_ref, n_ref):
    unit, _inverse = normalize(x_ref[...].astype(F32))
    n_ref[...] = (unit * g_ref[0:1, :] + b_ref[0:1, :]).astype(BF)


def first_norm(tokens, gains, biases, after=(), cost=0):
    rows, dim = tokens.shape
    block = pl.BlockSpec((256, dim), lambda i: (i, 0))
    return call(
        first_norm_kernel,
        (rows // 256,),
        [block, whole(gains.shape), whole(biases.shape)],
        block,
        jax.ShapeDtypeStruct((rows, dim), BF),
        after=after,
        cost=cost,
    )(tokens, gains, biases)


def project_kernel(n_ref, w_ref, p_ref):
    p_ref[...] = mm(n_ref[...], w_ref[...]).astype(BF)


def project(normed, w_qkv, after=(), cost=0):
    rows, dim = normed.shape
    cols = w_qkv.shape[1]
    tile = 768
    return call(
        project_kernel,
        (cols // tile,),
        [whole((rows, dim)), pl.BlockSpec((dim, tile), lambda j: (0, j))],
        pl.BlockSpec((rows, tile), lambda j: (0, j)),
        jax.ShapeDtypeStruct((rows, cols), BF),
        after=after,
        cost=cost,
    )(normed, w_qkv)


def spans(length):
    out = []
    for q_first in range(0, length, BLOCK):
        out.append((q_first, max(0, q_first - BAND)))
    return out


def fill_bias(bias_ref, doc_row, doc_col, length):
    at = 0
    for q_first, k_first in spans(length):
        keys = q_first + BLOCK - k_first
        key_pos = k_first + lax.broadcasted_iota(jnp.int32, (keys, BLOCK), 0)
        query_pos = q_first + lax.broadcasted_iota(jnp.int32, (keys, BLOCK), 1)
        same = doc_col[k_first : k_first + keys, :] == doc_row[:, q_first : q_first + BLOCK]
        bias_ref[at : at + keys, :] = jnp.where((key_pos <= query_pos) & same, 0.0, NEGATIVE).astype(F32)
        at += keys


def bias_rows(length):
    return sum(q + BLOCK - k for q, k in spans(length))


def head_lanes(block, head, head_dim):
    lane = lax.broadcasted_iota(jnp.int32, block.shape, 1)
    inside = (lane >= head * head_dim) & (lane < (head + 1) * head_dim)
    return jnp.where(inside, block, jnp.zeros_like(block))


def attn_fwd_kernel(head_dim, row_ref, col_ref, q_ref, k_ref, v_ref, o_ref, lse_ref, bias_ref):
    length = q_ref.shape[0]
    pair = q_ref.shape[1]
    scale = head_dim**-0.5

    @pl.when(pl.program_id(0) == 0)
    def _():
        fill_bias(bias_ref, row_ref[...], col_ref[...], length)

    value_t = v_ref[...].T
    at = 0
    for q_first, k_first in spans(length):
        keys = q_first + BLOCK - k_first
        q_at = slice(q_first, q_first + BLOCK)
        k_at = slice(k_first, k_first + keys)
        query = q_ref[q_at, :] * BF(scale)
        bias = bias_ref[at : at + keys, :]
        outs = []
        for head in range(pair // head_dim):
            scores = mm_nt(k_ref[k_at, :], head_lanes(query, head, head_dim)) + bias
            top = jnp.max(scores, axis=0, keepdims=True)
            exponent = jnp.exp(scores - top)
            total = jnp.sum(exponent, axis=0, keepdims=True)
            part = mm(value_t[head * head_dim : (head + 1) * head_dim, k_at], exponent.astype(BF))
            outs.append(part / total)
            lse_ref[0, head : head + 1, q_at] = top + jnp.log(total)
        o_ref[q_at, :] = jnp.concatenate(outs, axis=0).T.astype(BF)
        at += keys


def attn_fwd(projected, doc_row, doc_col, head_dim, cost=0):
    length = projected.shape[0]
    width = projected.shape[1] // 3
    pair = 128
    pairs = width // pair
    per = pair // head_dim
    specs = [pl.BlockSpec((length, pair), functools.partial(lambda s, j: (0, s * pairs + j), s)) for s in range(3)]
    return call(
        functools.partial(attn_fwd_kernel, head_dim),
        (pairs,),
        [whole(doc_row.shape), whole(doc_col.shape)] + specs,
        [pl.BlockSpec((length, pair), lambda j: (0, j)), pl.BlockSpec((1, per, length), lambda j: (j, 0, 0))],
        [jax.ShapeDtypeStruct((length, width), BF), jax.ShapeDtypeStruct((pairs, per, length), F32)],
        scratch=[pltpu.VMEM((bias_rows(length), BLOCK), F32)],
        cost=cost,
    )(doc_row, doc_col, projected, projected, projected)


def attn_bwd_kernel(head_dim, row_ref, col_ref, q_ref, k_ref, v_ref, do_ref, lse_ref, g_ref, gt_ref, bias_ref, dk_sum, dv_sum):
    length = q_ref.shape[0]
    pair = q_ref.shape[1]
    scale = head_dim**-0.5

    @pl.when(pl.program_id(0) == 0)
    def _():
        fill_bias(bias_ref, row_ref[...], col_ref[...], length)

    key_t = (k_ref[...] * BF(scale)).T
    dk_sum[...] = jnp.zeros_like(dk_sum)
    dv_sum[...] = jnp.zeros_like(dv_sum)
    at = 0
    for q_first, k_first in spans(length):
        keys = q_first + BLOCK - k_first
        q_at = slice(q_first, q_first + BLOCK)
        k_at = slice(k_first, k_first + keys)
        query = q_ref[q_at, :] * BF(scale)
        grad = do_ref[q_at, :]
        bias = bias_ref[at : at + keys, :]
        dq_parts = []
        dk_part = None
        dv_part = None
        for head in range(pair // head_dim):
            query_one = head_lanes(query, head, head_dim)
            grad_one = head_lanes(grad, head, head_dim)
            scores = mm_nt(k_ref[k_at, :], query_one) + bias
            prob = jnp.exp(scores - lse_ref[0, head : head + 1, q_at])
            prob_grad = mm_nt(v_ref[k_at, :], grad_one)
            inner = jnp.sum(prob * prob_grad, axis=0, keepdims=True)
            score_grad = (prob * (prob_grad - inner)).astype(BF)
            dv_one = mm(prob.astype(BF), grad_one)
            dk_one = mm(score_grad, query_one)
            dv_part = dv_one if dv_part is None else dv_part + dv_one
            dk_part = dk_one if dk_part is None else dk_part + dk_one
            dq_parts.append(mm(key_t[head * head_dim : (head + 1) * head_dim, k_at], score_grad))
        dk_sum[k_at, :] += dk_part
        dv_sum[k_at, :] += dv_part
        dq_t = jnp.concatenate(dq_parts, axis=0)
        gt_ref[0, :, q_at] = dq_t.astype(BF)
        g_ref[0, q_at, :] = dq_t.T.astype(BF)
        at += keys
    for i, ref in ((1, dk_sum), (2, dv_sum)):
        low = ref[...].astype(BF)
        g_ref[i] = low
        gt_ref[i] = low.T


def attn_bwd(projected, grad_heads, log_total, doc_row, doc_col, head_dim, part, parts, held=(), after=(), cost=0):
    length = projected.shape[0]
    width = projected.shape[1] // 3
    pair = 128
    pairs = width // pair
    steps = pairs // parts
    first = part * steps
    per = pair // head_dim
    specs = [
        pl.BlockSpec((length, pair), functools.partial(lambda s, j: (0, s * pairs + first + j), s)) for s in range(3)
    ]
    held = list(held)
    count = len(held)
    kernel = functools.partial(attn_bwd_kernel, head_dim)
    return call(
        lambda *refs: kernel(*refs[:7], *refs[7 + count :]),
        (steps,),
        [whole(doc_row.shape), whole(doc_col.shape)]
        + specs
        + [
            pl.BlockSpec((length, pair), lambda j: (0, first + j)),
            pl.BlockSpec((1, per, length), lambda j: (first + j, 0, 0)),
        ]
        + [pl.BlockSpec(memory_space=pl.ANY)] * count,
        [
            pl.BlockSpec((3, length, pair), lambda j: (0, 0, first + j)),
            pl.BlockSpec((3, pair, length), lambda j: (0, first + j, 0)),
        ],
        [jax.ShapeDtypeStruct((3, length, width), BF), jax.ShapeDtypeStruct((3, width, length), BF)],
        scratch=[
            pltpu.VMEM((bias_rows(length), BLOCK), F32),
            pltpu.VMEM((length, pair), F32),
            pltpu.VMEM((length, pair), F32),
        ],
        aliases={7 + i: i for i in range(count)},
        after=after,
        cost=cost,
    )(doc_row, doc_col, projected, projected, projected, grad_heads, log_total, *held)


def middle_kernel(x_ref, h_ref, w_ref, g_ref, b_ref, *refs):
    m_ref, s_ref = refs[-2:]
    middle = x_ref[...].astype(F32) + mm(h_ref[...], w_ref[...])
    m_ref[...] = middle
    unit, _inverse = normalize(middle)
    s_ref[...] = (unit * g_ref[1:2, :] + b_ref[1:2, :]).astype(BF)


def make_middle(tokens, mixed_heads, w_attn_out, gains, biases, part, parts, held=(), after=(), cost=0):
    rows, dim = tokens.shape
    tile = 256
    steps = rows // tile // parts
    block = pl.BlockSpec((tile, dim), lambda i: (part * steps + i, 0))
    held = list(held)
    return call(
        middle_kernel,
        (steps,),
        [block, block, whole(w_attn_out.shape), whole(gains.shape), whole(biases.shape)]
        + [pl.BlockSpec(memory_space=pl.ANY)] * len(held),
        [block, pl.BlockSpec((tile, dim), lambda i: (i, 0))],
        [jax.ShapeDtypeStruct((rows, dim), F32), jax.ShapeDtypeStruct((rows // parts, dim), BF)],
        aliases={5: 0} if held else None,
        after=after,
        cost=cost,
    )(tokens, mixed_heads, w_attn_out, gains, biases, *held)


def dispatch_kernel(parts, slots, *refs):
    places = refs[:2]
    rows = [refs[2 : 2 + parts], refs[2 + parts : 2 + 2 * parts]]
    o_refs = refs[2 + 2 * parts :]
    count = slots * (o_refs[0].shape[0] // (2 * slots)) * len(o_refs)
    for side in range(2):
        total = None
        at = 0
        for ref in rows[side]:
            slot = lax.broadcasted_iota(jnp.int32, (count, ref.shape[0]), 0)
            pick = jnp.where(slot == places[side][:, at : at + ref.shape[0]], 1.0, 0.0).astype(BF)
            part = mm(pick, ref[...])
            total = part if total is None else total + part
            at += ref.shape[0]
        low = total.astype(BF)
        if len(o_refs) == 1:
            o_refs[0][side * count : (side + 1) * count, :] = low
        else:
            for i, ref in enumerate(o_refs):
                ref[side * slots : (side + 1) * slots, :] = low[i * slots : (i + 1) * slots]


def dispatch_rows(places, rows, positions, slots, after=(), cost=0):
    dim = rows[0][0].shape[1]
    parts = len(rows[0])
    apart = slots % 16 == 0
    count = positions if apart else 1
    shape = (2 * slots * (positions // count), dim)
    out = call(
        functools.partial(dispatch_kernel, parts, slots),
        (1,),
        [whole(p.shape) for p in places] + [whole(r.shape) for side in rows for r in side],
        [whole(shape)] * count,
        [jax.ShapeDtypeStruct(shape, BF)] * count,
        after=after,
        cost=cost,
    )(*places, *rows[0], *rows[1])
    if apart:
        return out
    sides = out[0].reshape(2, positions, slots, dim)
    return [sides[:, p].reshape(2 * slots, dim) for p in range(positions)]


def fill(joined_ref, block_refs):
    at = 0
    for ref in block_refs:
        joined_ref[at : at + ref.shape[0], :] = ref[...]
        at += ref.shape[0]


def pick_rows(place, back):
    slot = lax.broadcasted_iota(jnp.int32, (place.shape[0], back.shape[0]), 1)
    return mm(jnp.where(slot == place, 1.0, 0.0).astype(BF), back)


def mixed_kernel(count, place_ref, m_ref, *refs):
    o_ref, joined_ref = refs[count:]

    @pl.when(pl.program_id(0) == 0)
    def _():
        fill(joined_ref, refs[:count])

    o_ref[...] = (m_ref[...] + pick_rows(place_ref[...], joined_ref[...])).astype(BF)


def make_mixed(place_col, middle, back, after=(), cost=0):
    rows, dim = middle.shape
    tile = 256
    total = sum(n for _, n in back)
    block = pl.BlockSpec((tile, dim), lambda i: (i, 0))
    return call(
        functools.partial(mixed_kernel, len(back)),
        (rows // tile,),
        [pl.BlockSpec((tile, 1), lambda i: (i, 0)), block] + [whole((n, dim)) for _, n in back],
        block,
        jax.ShapeDtypeStruct((rows, dim), BF),
        scratch=[pltpu.VMEM((total, dim), BF)],
        after=after,
        cost=cost,
    )(place_col, middle, *[b for b, _ in back])


def second_back_kernel(count, place_ref, m_ref, c_ref, w_ref, g_ref, *refs):
    gm_ref, gat_ref, gh_ref, sums_ref, joined_ref = refs[count:]

    @pl.when(pl.program_id(0) == 0)
    def _():
        fill(joined_ref, refs[:count])

    grad_sent = pick_rows(place_ref[...], joined_ref[...])
    unit, inverse = normalize(m_ref[...])
    grad_middle = c_ref[...].astype(F32) + norm_back(unit, inverse, g_ref[1:2, :], grad_sent)
    gm_ref[...] = grad_middle
    grad_attn = grad_middle.astype(BF)
    gat_ref[...] = grad_attn.T
    gh_ref[...] = mm_nt(grad_attn, w_ref[...]).astype(BF)
    sums = jnp.concatenate(
        [jnp.sum(grad_sent * unit, axis=0, keepdims=True), jnp.sum(grad_sent, axis=0, keepdims=True)], axis=0
    )

    @pl.when(pl.program_id(0) == 0)
    def _():
        sums_ref[...] = sums

    @pl.when(pl.program_id(0) > 0)
    def _():
        sums_ref[...] += sums


def second_back(place_col, middle, cotangent, back, w_attn_out, gains, after=(), cost=0):
    rows, dim = middle.shape
    tile = 256
    total = sum(n for _, n in back)
    block = pl.BlockSpec((tile, dim), lambda i: (i, 0))
    return call(
        functools.partial(second_back_kernel, len(back)),
        (rows // tile,),
        [pl.BlockSpec((tile, 1), lambda i: (i, 0)), block, block, whole(w_attn_out.shape), whole(gains.shape)]
        + [whole((n, dim)) for _, n in back],
        [block, pl.BlockSpec((dim, tile), lambda i: (0, i)), block, whole((2, dim))],
        [
            jax.ShapeDtypeStruct((rows, dim), F32),
            jax.ShapeDtypeStruct((dim, rows), BF),
            jax.ShapeDtypeStruct((rows, dim), BF),
            jax.ShapeDtypeStruct((2, dim), F32),
        ],
        scratch=[pltpu.VMEM((total, dim), BF)],
        after=after,
        cost=cost,
    )(place_col, middle, cotangent, w_attn_out, gains, *[b for b, _ in back])


def first_back_kernel(x_ref, gm_ref, d_ref, w_ref, g_ref, dx_ref, sums_ref):
    dim = x_ref.shape[1]
    grad_normed = mm_nt(d_ref[0], w_ref[:, :dim])
    grad_normed += mm_nt(d_ref[1], w_ref[:, dim : 2 * dim])
    grad_normed += mm_nt(d_ref[2], w_ref[:, 2 * dim :])
    unit, inverse = normalize(x_ref[...].astype(F32))
    dx_ref[...] = gm_ref[...] + norm_back(unit, inverse, g_ref[0:1, :], grad_normed)
    sums = jnp.concatenate(
        [jnp.sum(grad_normed * unit, axis=0, keepdims=True), jnp.sum(grad_normed, axis=0, keepdims=True)], axis=0
    )

    @pl.when(pl.program_id(0) == 0)
    def _():
        sums_ref[...] = sums

    @pl.when(pl.program_id(0) > 0)
    def _():
        sums_ref[...] += sums


def first_back(tokens, grad_middle, grads, w_qkv, gains, after=(), cost=0):
    rows, dim = tokens.shape
    tile = 256
    block = pl.BlockSpec((tile, dim), lambda i: (i, 0))
    return call(
        first_back_kernel,
        (rows // tile,),
        [
            block,
            block,
            pl.BlockSpec((3, tile, dim), lambda i: (0, i, 0)),
            whole(w_qkv.shape),
            whole(gains.shape),
        ],
        [block, whole((2, dim))],
        [jax.ShapeDtypeStruct((rows, dim), F32), jax.ShapeDtypeStruct((2, dim), F32)],
        after=after,
        cost=cost,
    )(tokens, grad_middle, grads, w_qkv, gains)


def grad_hidden_kernel(count, wo_ref, *refs):
    gh_ref, turned_ref, joined_ref = refs[count:]

    @pl.when(pl.program_id(0) == 0)
    def _():
        fill(joined_ref, refs[:count])
        turned_ref[...] = joined_ref[...].T

    gh_ref[...] = mm_nt(joined_ref[...], wo_ref[...]).astype(BF)


def grad_hidden(grads, w_out, after=(), cost=0):
    total = sum(g.shape[0] for g in grads)
    units, dim = w_out.shape
    tile = 512
    return call(
        functools.partial(grad_hidden_kernel, len(grads)),
        (units // tile,),
        [pl.BlockSpec((tile, dim), lambda j: (j, 0))] + [whole(g.shape) for g in grads],
        [pl.BlockSpec((total, tile), lambda j: (0, j)), whole((dim, total))],
        [jax.ShapeDtypeStruct((total, units), BF), jax.ShapeDtypeStruct((dim, total), BF)],
        scratch=[pltpu.VMEM((total, dim), BF)],
        after=after,
        cost=cost,
    )(w_out, *grads)


def expert_kernel(count, aliased, wi_ref, gh_ref, *refs):
    blocks = refs[:count]
    outs = refs[count + aliased :]
    h_ref, gp_ref = outs[:2]
    gr_refs = outs[2:-2]
    joined_ref, gr_sum = outs[-2:]
    step = pl.program_id(0)

    @pl.when(step == 0)
    def _():
        fill(joined_ref, blocks)
        gr_sum[...] = jnp.zeros_like(gr_sum)

    slope = 0.7978845608028654
    for first in range(0, wi_ref.shape[1], SUB):
        cols = slice(first, first + SUB)
        preact = mm(joined_ref[...], wi_ref[:, cols])
        square = preact * preact
        tanh = jnp.tanh(preact * (slope + (slope * 0.044715) * square))
        half = 0.5 + 0.5 * tanh
        hidden = preact * half
        gate = half + hidden * (1.0 - tanh) * (slope + (3.0 * slope * 0.044715) * square)
        h_ref[:, cols] = hidden.astype(BF)
        grad_low = (gate * gh_ref[:, cols].astype(F32)).astype(BF)
        gp_ref[:, cols] = grad_low
        gr_sum[...] += mm_nt(grad_low, wi_ref[:, cols])

    @pl.when(step == pl.num_programs(0) - 1)
    def _():
        at = 0
        for ref in gr_refs:
            ref[...] = gr_sum[at : at + ref.shape[0], :].astype(BF)
            at += ref.shape[0]


def expert(blocks, gh, w_in, first, held=(), out_rows=None, after=(), cost=0):
    count = sum(b.shape[0] for b in blocks)
    dim, units = w_in.shape
    tile = 1024
    at = first // count
    act = pl.BlockSpec((count, tile), lambda j: (at, j))
    shape = jax.ShapeDtypeStruct(gh.shape, BF)
    held = list(held)
    pieces = out_rows or [b.shape[0] for b in blocks]
    return call(
        functools.partial(expert_kernel, len(blocks), len(held)),
        (units // tile,),
        [pl.BlockSpec((dim, tile), lambda j: (0, j)), act]
        + [whole(b.shape) for b in blocks]
        + [pl.BlockSpec(memory_space=pl.ANY)] * len(held),
        [act, act] + [whole((n, dim)) for n in pieces],
        [shape, shape] + [jax.ShapeDtypeStruct((n, dim), BF) for n in pieces],
        scratch=[pltpu.VMEM((count, dim), BF), pltpu.VMEM((count, dim), F32)],
        aliases={2 + len(blocks) + i: i for i in range(len(held))},
        after=after,
        cost=cost,
    )(w_in, gh, *blocks, *held)


def turn_kernel(count, *refs):
    o_ref, joined_ref = refs[count:]
    fill(joined_ref, refs[:count])
    o_ref[...] = joined_ref[...].T


def turned(blocks, after=(), cost=0):
    total = sum(b.shape[0] for b in blocks)
    dim = blocks[0].shape[1]
    return call(
        functools.partial(turn_kernel, len(blocks)),
        (1,),
        [whole(b.shape) for b in blocks],
        whole((dim, total)),
        jax.ShapeDtypeStruct((dim, total), BF),
        scratch=[pltpu.VMEM((total, dim), BF)],
        after=after,
        cost=cost,
    )(*blocks)


def produced_kernel(h_ref, wo_ref, *refs):
    o_refs, total_ref = refs[:-1], refs[-1]
    step = pl.program_id(0)
    part = mm(h_ref[...], wo_ref[...])

    @pl.when(step == 0)
    def _():
        total_ref[...] = part

    @pl.when(step > 0)
    def _():
        total_ref[...] += part

    @pl.when(step == pl.num_programs(0) - 1)
    def _():
        at = 0
        for ref in o_refs:
            ref[...] = total_ref[at : at + ref.shape[0], :].astype(BF)
            at += ref.shape[0]


def make_produced(hidden, w_out, pieces, after=(), cost=0):
    rows, units = hidden.shape
    dim = w_out.shape[1]
    tile = 512
    return call(
        produced_kernel,
        (units // tile,),
        [pl.BlockSpec((rows, tile), lambda j: (0, j)), pl.BlockSpec((tile, dim), lambda j: (j, 0))],
        [whole((n, dim)) for n in pieces],
        [jax.ShapeDtypeStruct((n, dim), BF) for n in pieces],
        scratch=[pltpu.VMEM((rows, dim), F32)],
        after=after,
        cost=cost,
    )(hidden, w_out)


def halves_kernel(count, slots, *refs):
    o_ref = refs[-1]
    for i in range(count):
        o_ref[i * slots : (i + 1) * slots, :] = refs[i][...]


def second_halves(blocks, slots, after=(), cost=0):
    dim = blocks[0].shape[1]
    count = len(blocks)
    return call(
        functools.partial(halves_kernel, count, slots),
        (1,),
        [pl.BlockSpec((slots, dim), lambda i: (1, 0))] * count,
        whole((count * slots, dim)),
        jax.ShapeDtypeStruct((count * slots, dim), BF),
        after=after,
        cost=cost,
    )(*blocks)


def add_kernel(k_ref, g_ref, o_ref):
    o_ref[...] = (k_ref[...].astype(F32) + g_ref[...].astype(F32)).astype(BF)


def add_second(keep, got, after=(), cost=0):
    _, rows, cols = keep.shape
    tile = 256
    block = pl.BlockSpec((1, tile, cols), lambda i: (1, i, 0))
    return call(
        add_kernel,
        (rows // tile,),
        [block, block],
        pl.BlockSpec((1, tile, cols), lambda i: (0, i, 0)),
        jax.ShapeDtypeStruct((1, rows, cols), BF),
        after=after,
        cost=cost,
    )(keep, got)


def stack_kernel(a_ref, b_ref, o_ref):
    o_ref[0:1, :] = a_ref[0:1, :]
    o_ref[1:2, :] = b_ref[0:1, :]
    o_ref[2:3, :] = a_ref[1:2, :]
    o_ref[3:4, :] = b_ref[1:2, :]


def stack_sums(first, second, after=(), cost=0):
    _, dim = first.shape
    return call(
        stack_kernel,
        (1,),
        [whole(first.shape), whole(second.shape)],
        whole((4, dim)),
        jax.ShapeDtypeStruct((4, dim), F32),
        after=after,
        cost=cost,
    )(first, second)


def tiles_kernel(_, a_ref, b_ref, o_ref):
    o_ref[0] = mm(a_ref[...], b_ref[...]).astype(BF)


def weight_tiles(first, second, table, first_tile, second_tile, after=(), cost=0):
    steps = table.shape[1]
    depth = first.shape[1]
    return call(
        tiles_kernel,
        (steps,),
        [
            pl.BlockSpec((first_tile, depth), lambda i, t: (t[0, i], 0)),
            pl.BlockSpec((depth, second_tile), lambda i, t: (0, t[1, i])),
        ],
        pl.BlockSpec((1, first_tile, second_tile), lambda i, t: (i, 0, 0)),
        jax.ShapeDtypeStruct((steps, first_tile, second_tile), BF),
        prefetch=1,
        after=after,
        cost=cost,
    )(table, first, second)


def joint_kernel(g_ref, ga_ref, n_ref, h_ref, o_ref):
    own = o_ref.shape[0]
    dim = o_ref.shape[2]
    qkv_part = mm(g_ref[...], n_ref[...]).reshape(own, g_ref.shape[0] // own, dim)
    out_part = mm(ga_ref[...], h_ref[...]).reshape(own, ga_ref.shape[0] // own, dim)
    o_ref[...] = jnp.concatenate([qkv_part, out_part], axis=1).astype(BF)


def joint(grads_t, grad_attn_t, normed, mixed_heads, owners, part, parts, after=(), cost=0):
    rows, dim = normed.shape
    steps = 8
    cols = dim // parts
    own = owners // steps
    qkv_rows = grads_t.shape[0] // steps
    out_rows = grad_attn_t.shape[0] // steps
    right = pl.BlockSpec((rows, cols), lambda i: (0, part))
    each = (qkv_rows + out_rows) // own
    return call(
        joint_kernel,
        (steps,),
        [
            pl.BlockSpec((qkv_rows, rows), lambda i: (i, 0)),
            pl.BlockSpec((out_rows, rows), lambda i: (i, 0)),
            right,
            right,
        ],
        pl.BlockSpec((own, each, cols), lambda i: (i, 0, 0)),
        jax.ShapeDtypeStruct((owners, each, cols), BF),
        after=after,
        cost=cost,
    )(grads_t, grad_attn_t, normed, mixed_heads)


def finish_kernel(turn, *refs):
    o_ref = refs[-1]
    total = refs[0][0].astype(F32) + refs[1][0].astype(F32) + refs[2][0].astype(F32)
    o_ref[...] = total.T if turn else total


def finish(keep, got, last, turn, side, held=None, after=(), cost=0):
    _, rows, cols = keep.shape
    tile = 256
    block = pl.BlockSpec((1, tile, cols), lambda i: (0, i, 0))
    steps = rows // tile
    shape = (cols, 2 * rows) if turn else (2 * rows, cols)
    out = (
        pl.BlockSpec((cols, tile), lambda i: (0, side * steps + i))
        if turn
        else pl.BlockSpec((tile, cols), lambda i: (side * steps + i, 0))
    )
    more = [] if held is None else [held]
    count = len(more)

    def body(*refs):
        finish_kernel(turn, *refs[:3], refs[3 + count])

    return call(
        body,
        (steps,),
        [block] * 3 + [pl.BlockSpec(memory_space=pl.ANY)] * count,
        out,
        jax.ShapeDtypeStruct(shape, F32),
        aliases={3: 0} if more else None,
        after=after,
        cost=cost,
    )(keep, got, last, *more)


def swap(value, axis, mask):
    size = lax.axis_size(axis)
    return lax.ppermute(value, axis, [(i, i ^ mask) for i in range(size)])


def split_sum(value, dim, axis, mask):
    bit = jnp.where((lax.axis_index(axis) & mask) > 0, 1, 0)
    mine = lax.dynamic_index_in_dim(value, bit, dim, keepdims=False)
    other = lax.dynamic_index_in_dim(value, 1 - bit, dim, keepdims=False)
    return (mine.astype(F32) + swap(other, axis, mask).astype(F32)).astype(value.dtype)


def bits_of(size):
    return [1 << i for i in range(size.bit_length() - 1)]


def on_device(
    tokens,
    norm_gains,
    norm_biases,
    w_qkv,
    w_attn_out,
    w_in,
    w_out,
    segment_ids,
    expert_ids,
    slots,
    cotangent,
):
    tok, dim = tokens.shape
    head_dim = dim // HEADS
    wide = lax.axis_size("wide")
    narrow = lax.axis_size("narrow")
    units = w_in.shape[2]
    me_wide = lax.axis_index("wide")
    me_narrow = lax.axis_index("narrow")
    capacity = tok * 9 // (8 * wide)
    w_in = w_in[0]
    w_out = w_out[0]
    zs = wide // 2
    slots_all = zs * capacity
    groups = [list(range(zs // 2)), list(range(zs // 2, 3 * zs // 4)), list(range(3 * zs // 4, zs))]
    apart = capacity % 16 == 0

    def joinable(blocks):
        return blocks if apart else [jnp.concatenate(blocks, axis=0)]

    def by_position(pieces):
        return list(pieces) if apart else [q for p in pieces for q in jnp.split(p, p.shape[0] // (2 * capacity))]

    def piece_rows(group):
        return [2 * capacity] * len(group) if apart else [2 * capacity * len(group)]

    away = expert_ids ^ me_wide
    kept = slots < capacity
    base = (away >> 1) * capacity + slots
    core = away & 1
    nowhere = 2 * slots_all
    place_own = jnp.where(kept & (core == 0), base, nowhere).astype(jnp.int32)[None, :]
    place_sent = jnp.where(kept & (core == 1), base, nowhere).astype(jnp.int32)[None, :]
    places = [place_own, swap(place_sent, "wide", 1)]
    place_col = jnp.where(kept, core * slots_all + base, nowhere).astype(jnp.int32)[:, None]
    doc_row = segment_ids
    doc_col = segment_ids.reshape(tok, 1)

    def exchange(blocks, positions):
        return [swap(blocks[z], "wide", 2 * z) if z else blocks[z] for z in positions]

    def bring_back(blocks, after):
        if not apart:
            theirs = jnp.concatenate([b[capacity:] for b in blocks], axis=0)
            ours = swap(theirs, "wide", 1)
            return [(jnp.concatenate([b[:capacity] for b in blocks], axis=0), slots_all), (ours, slots_all)]
        ours = swap(second_halves(blocks, capacity, after), "wide", 1)
        return [(b, capacity) for b in blocks] + [(ours, slots_all)]

    cotangent_other = swap(cotangent, "wide", 1)
    normed = first_norm(tokens, norm_gains, norm_biases)
    sent_grads = dispatch_rows(places, [[cotangent], [cotangent_other]], zs, capacity, after=[normed])
    expert_grads = exchange(sent_grads, range(zs))

    projected = project(normed, w_qkv, after=[sent_grads[0]])
    mixed_heads, log_total = attn_fwd(projected, doc_row, doc_col, head_dim)
    middle, sent_first = make_middle(tokens, mixed_heads, w_attn_out, norm_gains, norm_biases, 0, 2)
    other_first = swap(sent_first, "wide", 1)
    middle, sent_last = make_middle(
        tokens, mixed_heads, w_attn_out, norm_gains, norm_biases, 1, 2, [middle], after=expert_grads
    )
    other_last = swap(sent_last, "wide", 1)
    sent_rows = dispatch_rows(places, [[sent_first, sent_last], [other_first, other_last]], zs, capacity)
    expert_rows = exchange(sent_rows, range(zs))

    gh, grads_t = grad_hidden(joinable(expert_grads), w_out, after=[sent_rows[0]])
    held = ()
    back_grads = []
    before = [gh]
    for group in groups:
        blocks = joinable([expert_rows[z] for z in group])
        outs = expert(blocks, gh, w_in, 2 * group[0] * capacity, held, piece_rows(group), after=before)
        held = outs[:2]
        before = [outs[2]]
        pieces = by_position(outs[2:])
        back_grads += exchange({z: pieces[i] for i, z in enumerate(group)}, group)
    hidden, grad_preact = held

    quarter = units // narrow
    half_dim = dim // 2

    def tiles(turned_rows, right, side, positions, after):
        table = jnp.stack(
            [jnp.full((len(positions),), side, jnp.int32), jnp.stack([me_narrow ^ p for p in positions]).astype(jnp.int32)]
        )
        return weight_tiles(turned_rows, right, table, half_dim, quarter, after=after)

    masks = [(1, 2), (2, 1)]
    sides = range(2)

    def send(turned_rows, right, after):
        out = [tiles(turned_rows, right, side, [masks[side][0], 3], after) for side in sides]
        return out, [swap(out[side], "narrow", masks[side][0]) for side in sides]

    def keep(turned_rows, right, after):
        return [tiles(turned_rows, right, side, [0, masks[side][1]], after) for side in sides]

    def second_step(kept, got, after):
        again = [add_second(kept[side], got[side], after) for side in sides]
        return again, [swap(again[side], "narrow", masks[side][1]) for side in sides]

    send_out, got_out = send(grads_t, hidden, before)
    rows_t = turned(joinable(expert_rows), after=send_out)
    keep_out = keep(grads_t, hidden, [rows_t])
    produced = make_produced(hidden, w_out, piece_rows(range(zs)), after=keep_out)
    back_rows = exchange(by_position(produced), range(zs))
    back_grads = bring_back(back_grads, [produced[0]])
    send_in, got_in = send(rows_t, grad_preact, [back_grads[0][0], produced[0]])
    grad_middle, grad_attn_t, grad_heads, sums_two = second_back(
        place_col, middle, cotangent, back_grads, w_attn_out, norm_gains, after=send_in + got_out
    )
    attn = functools.partial(attn_bwd, projected, grad_heads, log_total, doc_row, doc_col, head_dim)
    held = attn(0, 2)
    back_rows = bring_back(back_rows, [held[0]])
    again_out, last_out = second_step(keep_out, got_out, [held[0]])
    grads, grads_all_t = attn(1, 2, held, after=again_out)
    grads_all_t = grads_all_t.reshape(3 * dim, tok)

    owners = narrow * wide
    own_qkv = 3 * dim // owners
    n_bits = bits_of(narrow)
    w_bits = bits_of(wide)
    joints = []
    for side in sides:
        joints.append(joint(grads_all_t, grad_attn_t, normed, mixed_heads, owners, side, 2, after=joints))
    keep_in = keep(rows_t, grad_preact, joints)
    again_in, last_in = second_step(keep_in, got_in, keep_in)
    values = []
    for side in sides:
        value = joints[side].reshape((2,) * (len(n_bits) + len(w_bits)) + joints[side].shape[1:])
        names = [("narrow", b) for b in reversed(n_bits)] + [("wide", b) for b in reversed(w_bits)]
        steps = [("wide", 1)] + [("narrow", b) for b in masks[side]] + [("wide", b) for b in w_bits[1:]]
        for step in steps:
            at = names.index(step)
            value = split_sum(value, at, *step)
            names.pop(at)
        values.append(value)
    d_tokens, sums_one = first_back(tokens, grad_middle, grads, w_qkv, norm_gains, after=again_in)
    mixed = make_mixed(place_col, middle, back_rows, after=[sums_one])
    value = jnp.concatenate(values, axis=1)
    d_w_qkv = value[:own_qkv].T.astype(F32)
    d_w_attn_out = value[own_qkv:].T.astype(F32)

    d_w_out = finish(keep_out[0], got_out[0], last_out[0], True, 0, after=[mixed])
    d_w_out = finish(keep_out[1], got_out[1], last_out[1], True, 1, d_w_out)
    d_w_in = finish(keep_in[0], got_in[0], last_in[0], False, 0, after=[d_w_out])
    d_w_in = finish(keep_in[1], got_in[1], last_in[1], False, 1, d_w_in)

    sums = stack_sums(sums_one, sums_two, after=[d_w_in])
    for axis, bits in (("narrow", n_bits), ("wide", w_bits)):
        for bit in bits:
            sums = sums + swap(sums, axis, bit)
    own = dim // owners
    sums = lax.dynamic_slice_in_dim(sums, (me_narrow * wide + me_wide) * own, own, 1)
    return (mixed, d_tokens, sums[:2], sums[2:], d_w_qkv, d_w_attn_out, d_w_in[None], d_w_out[None])


def solution(mesh):
    placed = (
        P(("narrow", "wide"), None),
        P(),
        P(),
        P(),
        P(),
        P("wide", None, None),
        P("wide", None, None),
        P(("narrow", "wide"), None),
        P(("narrow", "wide")),
        P(("narrow", "wide")),
        P(("narrow", "wide"), None),
    )
    return jax.shard_map(
        on_device,
        mesh=mesh,
        in_specs=placed,
        out_specs=(
            P(("narrow", "wide"), None),
            P(("narrow", "wide"), None),
            P(None, ("narrow", "wide")),
            P(None, ("narrow", "wide")),
            P(None, ("narrow", "wide")),
            P(None, ("narrow", "wide")),
            P("wide", None, "narrow"),
            P("wide", "narrow", None),
        ),
        check_vma=False,
    )
```

time: 727 us -> 498 us (0.69)
  waiting for transfers between devices: 233 us -> 77.5 us
  starting transfers between devices: 121 us -> 35 us
  Pallas kernels: 265 us -> 336 us
  other arithmetic: 42.9 us -> 12.7 us
  between operations: 15.6 us -> 1.44 us
  local copies, waits for them, and re-layouts: 37.8 us -> 25.6 us
    unnamed x2 -> x0, waiting for transfers between devices: 102 us -> none
    ppermute x69 -> x41, starting transfers between devices: 121 us -> 35 us  [swap(): return lax.ppermute(value, axis, [(i, i ^ mask) for i in range(size)])]
    pallas_call x23 -> x39, Pallas kernels: 265 us -> 336 us  [call(): return lambda *args: run(*args, *after)]
    ppermute x69 -> x41, waiting for transfers between devices: 131 us -> 77.5 us  [swap(): return lax.ppermute(value, axis, [(i, i ^ mask) for i in range(size)])]
    unnamed x157 -> x44, local copies, waits for them, and re-layouts: 24.2 us -> 10.9 us
    concatenate x2 -> x0, other arithmetic: 12.1 us -> none  [the longest x1 12 us: on_device(): d_qkv_t = jnp.concatenate([transposed(g, normed) for g in grads], axis=0)]
  transfers between devices with their start and end apart: 70 -> 41, of which waited for: 24 -> 15; matrix products, arithmetic and copies ran while one was open for 6% -> 5% of each run, Pallas kernels for 19% -> 66%
where the time goes in v2:
time: 498 us; the launch traced here: 488 us
  Pallas kernels  336 us (67%)
  waiting for transfers between devices  77.5 us (16%)
  starting transfers between devices  35 us (7%)
  local copies, waits for them, and re-layouts  25.6 us (5%)
  other arithmetic  12.7 us (3%)
    pallas_call x39, Pallas kernels, call(): return lambda *args: run(*args, *after)  336 us
    ppermute x41, waiting for transfers between devices, swap(): return lax.ppermute(value, axis, [(i, i ^ mask) for i in range(size)])  77.5 us
    ppermute x41, starting transfers between devices, swap(): return lax.ppermute(value, axis, [(i, i ^ mask) for i in range(size)])  35 us
    unnamed x44, local copies, waits for them, and re-layouts  10.9 us
  transfers between devices with their start and end apart: 41, of which 15 were waited for; matrix products, arithmetic and copies ran while one was open for 5% of the time, Pallas kernels for 66%

profile of v2, /device:TPU:0, one launch (start us, length us, event | category | flops | bytes accessed | tf_op | source)
XLA Modules:
  0.0 488.3 jit_solution(6175563788827849301)
XLA Ops:
  2.5 4.5 shard_map.170.refs_4_.refs_0_.refs_2_
  8.3 6.1 %shard_map.171 = (bf16[288,1024]{1,0:T(8,128)(2,1)}, bf16[288,1024]{1,0:T(8,128)(2,1)}, bf16[288,1024]{1,0:T(8,128)(2,1)}, bf16[288,1024]{1,0:T(8,128)(2,1)}) custom-call(s32[1,1024]{1,0:T(1,128)} %bitcast.95, s32[1,1024]{1,0:T(1,128)} %copy-done.21, bf16[1024,1024]{1,0:T(8,128)(2,1)} %refs_2_.9, bf16[1024,1024]{1,0:T(8,128)(2,1)} %copy-done.17, ...), custom_call_target="tpu_custom_call" | custom-call | flops 1 | tf_op jit(solution)/shard_map/pallas_call | solution.py:54
  14.5 3.0 collective-permute-start.2
  17.5 2.6 collective-permute-start.3
  21.1 10.8 %shard_map.172.refs_2_.refs_3_.refs_4_ = bf16[1024,3072]{1,0:T(8,128)(2,1)} custom-call(bf16[1024,1024]{1,0:T(8,128)(2,1)} %shard_map.170.refs_4_.refs_0_.refs_2_, bf16[1024,3072]{1,0:T(8,128)(2,1)} %refs_3_.7, bf16[288,1024]{1,0:T(8,128)(2,1)} %get-tuple-element.48.refs_2_.refs_6_.refs_1_), custom_call_target="tpu_custom_call" | custom-call | flops 1 | tf_op jit(solution)/shard_map/pallas_call | solution.py:54
  31.9 32.8 %shard_map.173 = (bf16[1024,1024]{1,0:T(8,128)(2,1)}, f32[8,2,1024]{2,1,0:T(2,128)}) custom-call(s32[1,1024]{1,0:T(1,128)} %refs_0_.12, s32[1024,1]{1,0:T(8,128)} %copy.32.refs_1_, bf16[1024,3072]{1,0:T(8,128)(2,1)} %shard_map.172.refs_2_.refs_3_.refs_4_, bf16[1024,3072]{1,0:T(8,128)(2,1)} %shard_map.172.refs_2_.refs_3_.refs_4_, ...), custom_call_target="tpu_custom_call" | custom-call | flops 1 | tf_op jit(solution)/shard_map/pallas_call | solution.py:54
  64.7 4.9 shard_map.174
  70.9 4.9 shard_map.175
  76.3 2.5 collective-permute-done.6.refs_5_
  79.8 6.1 %shard_map.176 = (bf16[288,1024]{1,0:T(8,128)(2,1)}, bf16[288,1024]{1,0:T(8,128)(2,1)}, bf16[288,1024]{1,0:T(8,128)(2,1)}, bf16[288,1024]{1,0:T(8,128)(2,1)}) custom-call(s32[1,1024]{1,0:T(1,128)} %bitcast.96, s32[1,1024]{1,0:T(1,128)} %copy-done.21, bf16[512,1024]{1,0:T(8,128)(2,1)} %get-tuple-element.55.refs_2_, ...), custom_call_target="tpu_custom_call" | custom-call | flops 1 | tf_op jit(solution)/shard_map/pallas_call | solution.py:54
  85.9 1.9 collective-permute-start.9
  87.8 2.5 collective-permute-start.8
  90.3 16.5 %shard_map.177 = (bf16[1152,4096]{1,0:T(8,128)(2,1)}, bf16[1024,1152]{1,0:T(8,128)(2,1)}) custom-call(bf16[4096,1024]{1,0:T(8,128)(2,1)} %bitcast.92, bf16[288,1024]{1,0:T(8,128)(2,1)} %get-tuple-element.48.refs_2_.refs_6_.refs_1_, bf16[288,1024]{1,0:T(8,128)(2,1)} %copy-done.10, bf16[288,1024]{1,0:T(8,128)(2,1)} %copy-done.11, ...), custom_call_target="tpu_custom_call" | custom-call | flops 1 | tf_op jit(solution)/shard_map/pallas_call | solution.py:54
  106.8 7.0 %collective-permute-done.9.refs_3_.refs_1_ = bf16[288,1024]{1,0:T(8,128)(2,1)S(1)} collective-permute-done((bf16[288,1024]{1,0:T(8,128)(2,1)}, bf16[288,1024]{1,0:T(8,128)(2,1)S(1)}, u32[]{:S(2)}, u32[]{:S(2)}) %collective-permute-start.9) | collective-permute-done | bytes 589856 | tf_op jit(solution)/shard_map/ppermute | solution.py:772
  114.6 20.6 %shard_map.178 = (bf16[1152,4096]{1,0:T(8,128)(2,1)}, bf16[1152,4096]{1,0:T(8,128)(2,1)}, bf16[288,1024]{1,0:T(8,128)(2,1)}, bf16[288,1024]{1,0:T(8,128)(2,1)}) custom-call(bf16[1024,4096]{1,0:T(8,128)(2,1)} %bitcast.84, bf16[1152,4096]{1,0:T(8,128)(2,1)} %get-tuple-element.58.refs_1_.refs_4_, bf16[288,1024]{1,0:T(8,128)(2,1)} %get-tuple-element.57.refs_5_.refs_2_.refs_0_, ...), custom_call_target="tpu_custom_call" | custom-call | flops 1 | tf_op jit(solution)/shard_map/pallas_call | solution.py:54
  136.1 12.7 %shard_map.179 = (bf16[1152,4096]{1,0:T(8,128)(2,1)}, bf16[1152,4096]{1,0:T(8,128)(2,1)}, bf16[288,1024]{1,0:T(8,128)(2,1)}) custom-call(bf16[1024,4096]{1,0:T(8,128)(2,1)} %bitcast.85, bf16[1152,4096]{1,0:T(8,128)(2,1)} %get-tuple-element.58.refs_1_.refs_4_, bf16[288,1024]{1,0:T(8,128)(2,1)} %copy-done.15, ...), custom_call_target="tpu_custom_call", output_to_operand_aliasing={{0}: (3, {}), {1}: (4, {})} | custom-call | flops 1 | tf_op jit(solution)/shard_map/pallas_call | solution.py:54
  151.0 12.5 %shard_map.180 = (bf16[1152,4096]{1,0:T(8,128)(2,1)}, bf16[1152,4096]{1,0:T(8,128)(2,1)}, bf16[288,1024]{1,0:T(8,128)(2,1)}) custom-call(bf16[1024,4096]{1,0:T(8,128)(2,1)} %bitcast.86, bf16[1152,4096]{1,0:T(8,128)(2,1)} %get-tuple-element.58.refs_1_.refs_4_, bf16[288,1024]{1,0:T(8,128)(2,1)} %copy-done.16, ...), custom_call_target="tpu_custom_call", output_to_operand_aliasing={{0}: (3, {}), {1}: (4, {})} | custom-call | flops 1 | tf_op jit(solution)/shard_map/pallas_call | solution.py:54
  163.5 1.9 collective-permute-start.15
  167.2 6.8 %shard_map.182.refs_5_ = bf16[2,512,1024]{2,1,0:T(8,128)(2,1)} custom-call(s32[2,2]{1,0:T(2,128)} %stack.84.refs_0_, bf16[1024,1152]{1,0:T(8,128)(2,1)} %get-tuple-element.69.refs_1_, bf16[1152,4096]{1,0:T(8,128)(2,1)} %get-tuple-element.68.refs_2_.refs_0_, bf16[288,1024]{1,0:T(8,128)(2,1)} %get-tuple-element.70.refs_3_), custom_call_target="tpu_custom_call" | custom-call | flops 1 | tf_op jit(solution)/shard_map/pallas_call | solution.py:54
  175.5 6.9 %shard_map.181.refs_4_ = bf16[2,512,1024]{2,1,0:T(8,128)(2,1)} custom-call(s32[2,2]{1,0:T(2,128)} %stack.81.refs_0_, bf16[1024,1152]{1,0:T(8,128)(2,1)} %get-tuple-element.69.refs_1_, bf16[1152,4096]{1,0:T(8,128)(2,1)} %get-tuple-element.68.refs_2_.refs_0_, bf16[288,1024]{1,0:T(8,128)(2,1)} %get-tuple-element.70.refs_3_), custom_call_target="tpu_custom_call" | custom-call | flops 1 | tf_op jit(solution)/shard_map/pallas_call | solution.py:54
  182.5 1.6 collective-permute-start.17
  184.7 3.7 shard_map.183.refs_3_.refs_1_
  189.0 6.8 %shard_map.185.refs_3_.refs_0_ = bf16[2,512,1024]{2,1,0:T(8,128)(2,1)} custom-call(s32[2,2]{1,0:T(2,128)} %stack.87.refs_0_, bf16[1024,1152]{1,0:T(8,128)(2,1)} %get-tuple-element.69.refs_1_, bf16[1152,4096]{1,0:T(8,128)(2,1)} %get-tuple-element.68.refs_2_.refs_0_, bf16[1024,1152]{1,0:T(8,128)(2,1)} %shard_map.183.refs_3_.refs_1_), custom_call_target="tpu_custom_call" | custom-call | flops 1 | tf_op jit(solution)/shard_map/pallas_call | solution.py:54
  195.8 6.8 %shard_map.184.refs_2_.refs_0_ = bf16[2,512,1024]{2,1,0:T(8,128)(2,1)} custom-call(s32[2,2]{1,0:T(2,128)} %stack.36.refs_0_, bf16[1024,1152]{1,0:T(8,128)(2,1)} %get-tuple-element.69.refs_1_, bf16[1152,4096]{1,0:T(8,128)(2,1)} %get-tuple-element.68.refs_2_.refs_0_, bf16[1024,1152]{1,0:T(8,128)(2,1)} %shard_map.183.refs_3_.refs_1_), custom_call_target="tpu_custom_call" | custom-call | flops 1 | tf_op jit(solution)/shard_map/pallas_call | solution.py:54
  202.6 18.1 %shard_map.186 = (bf16[288,1024]{1,0:T(8,128)(2,1)}, bf16[288,1024]{1,0:T(8,128)(2,1)}, bf16[288,1024]{1,0:T(8,128)(2,1)}, bf16[288,1024]{1,0:T(8,128)(2,1)}) custom-call(bf16[1152,4096]{1,0:T(8,128)(2,1)} %get-tuple-element.68.refs_2_.refs_0_, bf16[4096,1024]{1,0:T(8,128)(2,1)} %bitcast.93, bf16[2,512,1024]{2,1,0:T(8,128)(2,1)} %shard_map.184.refs_2_.refs_0_, ...), custom_call_target="tpu_custom_call" | custom-call | flops 1 | tf_op jit(solution)/shard_map/pallas_call | solution.py:54
  221.8 2.3 shard_map.187
  225.5 2.0 collective-permute-start.11
  227.5 2.6 collective-permute-start.12
  231.1 6.8 %shard_map.189.refs_11_ = bf16[2,512,1024]{2,1,0:T(8,128)(2,1)} custom-call(s32[2,2]{1,0:T(2,128)} %stack.84.refs_0_, bf16[1024,1152]{1,0:T(8,128)(2,1)} %shard_map.183.refs_3_.refs_1_, bf16[1152,4096]{1,0:T(8,128)(2,1)} %get-tuple-element.76.refs_2_, bf16[288,1024]{1,0:T(8,128)(2,1)} %get-tuple-element.64.refs_5_.refs_0_.refs_3_, ...), custom_call_target="tpu_custom_call" | custom-call | flops 1 | tf_op jit(solution)/shard_map/pallas_call | solution.py:54
  237.9 6.8 %shard_map.188.refs_10_ = bf16[2,512,1024]{2,1,0:T(8,128)(2,1)} custom-call(s32[2,2]{1,0:T(2,128)} %stack.81.refs_0_, bf16[1024,1152]{1,0:T(8,128)(2,1)} %shard_map.183.refs_3_.refs_1_, bf16[1152,4096]{1,0:T(8,128)(2,1)} %get-tuple-element.76.refs_2_, bf16[288,1024]{1,0:T(8,128)(2,1)} %get-tuple-element.64.refs_5_.refs_0_.refs_3_, ...), custom_call_target="tpu_custom_call" | custom-call | flops 1 | tf_op jit(solution)/shard_map/pallas_call | solution.py:54
  246.1 12.8 %shard_map.190 = (f32[1024,1024]{1,0:T(8,128)}, bf16[1024,1024]{1,0:T(8,128)(2,1)}, bf16[1024,1024]{1,0:T(8,128)(2,1)}, f32[2,1024]{1,0:T(2,128)}) custom-call(s32[1024,1]{1,0:T(8,128)} %copy.36.refs_0_, f32[1024,1024]{1,0:T(8,128)} %get-tuple-element.54.refs_1_, bf16[1024,1024]{1,0:T(8,128)(2,1)} %refs_2_.9, bf16[1024,1024]{1,0:T(8,128)(2,1)} %refs_3_.6, ...), custom_call_target="tpu_custom_call" | custom-call | flops 1 | tf_op jit(solution)/shard_map/pallas_call | solution.py:54
  258.9 21.9 %shard_map.191 = (bf16[3,1024,1024]{2,1,0:T(8,128)(2,1)}, bf16[3,1024,1024]{2,1,0:T(8,128)(2,1)}) custom-call(s32[1,1024]{1,0:T(1,128)} %refs_0_.12, s32[1024,1]{1,0:T(8,128)} %copy.32.refs_1_, bf16[1024,3072]{1,0:T(8,128)(2,1)} %shard_map.172.refs_2_.refs_3_.refs_4_, bf16[1024,3072]{1,0:T(8,128)(2,1)} %shard_map.172.refs_2_.refs_3_.refs_4_, ...), custom_call_target="tpu_custom_call" | custom-call | flops 1 | tf_op jit(solution)/shard_map/pallas_call | solution.py:54
  280.7 2.5 shard_map.194.refs_10_
  283.2 2.4 shard_map.193.refs_9_
  286.7 2.3 shard_map.192
  289.0 21.6 %shard_map.195 = (bf16[3,1024,1024]{2,1,0:T(8,128)(2,1)}, bf16[3,1024,1024]{2,1,0:T(8,128)(2,1)}) custom-call(s32[1,1024]{1,0:T(1,128)} %refs_0_.12, s32[1024,1]{1,0:T(8,128)} %copy.32.refs_1_, bf16[1024,3072]{1,0:T(8,128)(2,1)} %shard_map.172.refs_2_.refs_3_.refs_4_, ...), custom_call_target="tpu_custom_call", output_to_operand_aliasing={{0}: (7, {}), {1}: (8, {})} | custom-call | flops 1 | tf_op jit(solution)/shard_map/pallas_call | solution.py:54
  310.7 10.6 %shard_map.196.refs_4_.refs_3_ = bf16[32,128,512]{2,1,0:T(8,128)(2,1)} custom-call(bf16[3072,1024]{1,0:T(8,128)(2,1)} %bitcast.88, bf16[1024,1024]{1,0:T(8,128)(2,1)} %get-tuple-element.84.refs_1_, bf16[1024,1024]{1,0:T(8,128)(2,1)} %shard_map.170.refs_4_.refs_0_.refs_2_, bf16[1024,1024]{1,0:T(8,128)(2,1)} %get-tuple-element.49.refs_1_.refs_3_), custom_call_target="tpu_custom_call" | custom-call | flops 1 | tf_op jit(solution)/shard_map/pallas_call | solution.py:54
  321.8 10.6 %shard_map.197.refs_4_ = bf16[32,128,512]{2,1,0:T(8,128)(2,1)} custom-call(bf16[3072,1024]{1,0:T(8,128)(2,1)} %bitcast.89, bf16[1024,1024]{1,0:T(8,128)(2,1)} %get-tuple-element.84.refs_1_, bf16[1024,1024]{1,0:T(8,128)(2,1)} %shard_map.170.refs_4_.refs_0_.refs_2_, bf16[1024,1024]{1,0:T(8,128)(2,1)} %get-tuple-element.49.refs_1_.refs_3_, ...), custom_call_target="tpu_custom_call" | custom-call | flops 1 | tf_op jit(solution)/shard_map/pallas_call | solution.py:54
  332.4 3.9 constant_dynamic-slice_fusion.2
  336.3 1.6 copy.51
  342.0 6.8 %shard_map.199.refs_3_.refs_0_ = bf16[2,512,1024]{2,1,0:T(8,128)(2,1)} custom-call(s32[2,2]{1,0:T(2,128)} %stack.87.refs_0_, bf16[1024,1152]{1,0:T(8,128)(2,1)} %shard_map.183.refs_3_.refs_1_, bf16[1152,4096]{1,0:T(8,128)(2,1)} %get-tuple-element.76.refs_2_, bf16[32,128,512]{2,1,0:T(8,128)(2,1)} %shard_map.196.refs_4_.refs_3_, ...), custom_call_target="tpu_custom_call" | custom-call | flops 1 | tf_op jit(solution)/shard_map/pallas_call | solution.py:54
  348.8 7.1 %shard_map.198.refs_0_.refs_2_ = bf16[2,512,1024]{2,1,0:T(8,128)(2,1)} custom-call(s32[2,2]{1,0:T(2,128)} %stack.36.refs_0_, bf16[1024,1152]{1,0:T(8,128)(2,1)} %shard_map.183.refs_3_.refs_1_, bf16[1152,4096]{1,0:T(8,128)(2,1)} %get-tuple-element.76.refs_2_, bf16[32,128,512]{2,1,0:T(8,128)(2,1)} %shard_map.196.refs_4_.refs_3_, ...), custom_call_target="tpu_custom_call" | custom-call | flops 1 | tf_op jit(solution)/shard_map/pallas_call | solution.py:54
  355.9 2.4 shard_map.201.refs_6_
  358.3 10.7 %collective-permute-done.20.refs_1_ = bf16[2,512,1024]{2,1,0:T(8,128)(2,1)} collective-permute-done((bf16[2,512,1024]{2,1,0:T(8,128)(2,1)}, bf16[2,512,1024]{2,1,0:T(8,128)(2,1)}, u32[]{:S(2)}, u32[]{:S(2)}) %collective-permute-start.20) | collective-permute-done | bytes 2097184 | tf_op jit(solution)/shard_map/ppermute | solution.py:772
  369.5 2.4 shard_map.200.refs_5_
  372.5 3.0 fusion
  379.7 2.2 fusion.1
  384.2 14.2 %shard_map.202 = (f32[1024,1024]{1,0:T(8,128)}, f32[2,1024]{1,0:T(2,128)}) custom-call(bf16[1024,1024]{1,0:T(8,128)(2,1)} %refs_0_.13, f32[1024,1024]{1,0:T(8,128)} %get-tuple-element.80.refs_1_, bf16[3,1024,1024]{2,1,0:T(8,128)(2,1)} %get-tuple-element.82.refs_2_, bf16[1024,3072]{1,0:T(8,128)(2,1)} %refs_3_.7, f32[2,1024]{1,0:T(2,128)} %refs_4_.7, ...), custom_call_target="tpu_custom_call" | custom-call | flops 1 | tf_op jit(solution)/shard_map/pallas_call | solution.py:54
  398.4 7.3 %shard_map.203.refs_3_ = bf16[1024,1024]{1,0:T(8,128)(2,1)} custom-call(s32[1024,1]{1,0:T(8,128)} %copy.36.refs_0_, f32[1024,1024]{1,0:T(8,128)} %get-tuple-element.54.refs_1_, bf16[288,1024]{1,0:T(8,128)(2,1)} %get-tuple-element.71.refs_4_.refs_0_.refs_2_, bf16[288,1024]{1,0:T(8,128)(2,1)} %copy-done.8, bf16[288,1024]{1,0:T(8,128)(2,1)} %copy-done.9, ...), custom_call_target="tpu_custom_call" | custom-call | flops 1 | tf_op jit(solution)/shard_map/pallas_call | solution.py:54
  405.8 3.1 shard_map.204.refs_3_
  408.9 3.2 shard_map.205.refs_3_
  412.1 3.0 shard_map.206.refs_3_
  415.1 2.8 collective-permute-done.22.refs_2_
  417.9 3.0 shard_map.207.refs_2_
  422.8 15.7 %collective-permute-done.26 = f32[4,1024]{1,0:T(4,128)S(1)} collective-permute-done((f32[4,1024]{1,0:T(4,128)}, f32[4,1024]{1,0:T(4,128)S(1)}, u32[]{:S(2)}, u32[]{:S(2)}) %collective-permute-start.26) | collective-permute-done | bytes 16416 | tf_op jit(solution)/shard_map/ppermute | solution.py:772
  439.5 3.5 collective-permute-done.27
  444.2 3.7 collective-permute-done.29
  448.0 4.6 collective-permute-done.30
  452.7 1.7 fusion.2
  457.4 8.7 %collective-permute-done.38 = bf16[2,2,128,512]{3,2,0,1:T(8,128)(2,1)S(1)} collective-permute-done((bf16[2,2,128,512]{3,2,0,1:T(8,128)(2,1)S(1)}, bf16[2,2,128,512]{3,2,0,1:T(8,128)(2,1)S(1)}, u32[]{:S(2)}, u32[]{:S(2)}) %collective-permute-start.38) | collective-permute-done | bytes 524320 | tf_op jit(solution)/shard_map/ppermute | solution.py:772
  468.7 7.1 %collective-permute-done.39 = bf16[2,128,512]{2,1,0:T(8,128)(2,1)S(1)} collective-permute-done((bf16[2,128,512]{2,1,0:T(8,128)(2,1)S(1)}, bf16[2,128,512]{2,1,0:T(8,128)(2,1)S(1)}, u32[]{:S(2)}, u32[]{:S(2)}) %collective-permute-start.39) | collective-permute-done | bytes 262176 | tf_op jit(solution)/shard_map/ppermute | solution.py:772
  476.1 2.8 collective-permute-done.34
  480.5 2.8 collective-permute-done.40
  483.4 2.9 collective-permute-done.35
  (140 shorter events, 46.9 us)
Async XLA Ops:
  0.6 6.4 %collective-permute-start.1 = (bf16[1024,1024]{1,0:T(8,128)(2,1)}, bf16[1024,1024]{1,0:T(8,128)(2,1)S(1)}, u32[]{:S(2)}, u32[]{:S(2)}) collective-permute-start(bf16[1024,1024]{1,0:T(8,128)(2,1)} %refs_2_.9), channel_id=1, source_target_pairs={{0,1},{1,0},{2,3},{3,2},{4,5},{5,4},{6,7},{7,6},{8,9},{9,8},{10,11... | collective-permute-start | bytes 6291464 | tf_op jit(solution)/shard_map/ppermute | solution.py:772
  2.5 4.5 collective-permute-start
  7.0 0.6 copy-start.21
  7.0 1.3 copy-start.17
  8.3 11.8 %copy-start.20 = (s32[1,1024]{1,0:T(1,128)S(1)}, s32[1,1024]{1,0:T(1,128)}, u32[]{:S(2)}) copy-start(s32[1,1024]{1,0:T(1,128)} %refs_0_.12) | copy-start | bytes 12292
  14.5 55.1 %collective-permute-start.2 = (bf16[288,1024]{1,0:T(8,128)(2,1)}, bf16[288,1024]{1,0:T(8,128)(2,1)S(1)}, u32[]{:S(2)}, u32[]{:S(2)}) collective-permute-start(bf16[288,1024]{1,0:T(8,128)(2,1)} %get-tuple-element.51), channel_id=1, source_target_pairs={{0,2},{1,3},{2,0},{3,1},{4,6},{5,7},{6,4},{7,5},{8,10},{9,11},{10,... | collective-permute-start | bytes 1769480 | tf_op jit(solution)/shard_map/ppermute | solution.py:772
  17.5 52.1 %collective-permute-start.3 = (bf16[288,1024]{1,0:T(8,128)(2,1)}, bf16[288,1024]{1,0:T(8,128)(2,1)S(1)}, u32[]{:S(2)}, u32[]{:S(2)}) collective-permute-start(bf16[288,1024]{1,0:T(8,128)(2,1)} %get-tuple-element.52), channel_id=1, source_target_pairs={{0,4},{1,5},{2,6},{3,7},{4,0},{5,1},{6,2},{7,3},{8,12},{9,13},{10,... | collective-permute-start | bytes 1769480 | tf_op jit(solution)/shard_map/ppermute | solution.py:772
  20.1 49.5 %collective-permute-start.4 = (bf16[288,1024]{1,0:T(8,128)(2,1)}, bf16[288,1024]{1,0:T(8,128)(2,1)S(1)}, u32[]{:S(2)}, u32[]{:S(2)}) collective-permute-start(bf16[288,1024]{1,0:T(8,128)(2,1)} %get-tuple-element.53), channel_id=1, source_target_pairs={{0,6},{1,7},{2,4},{3,5},{4,2},{5,3},{6,0},{7,1},{8,14},{9,15},{10,... | collective-permute-start | bytes 1769480 | tf_op jit(solution)/shard_map/ppermute | solution.py:772
  69.5 6.7 %collective-permute-start.5 = (bf16[512,1024]{1,0:T(8,128)(2,1)}, bf16[512,1024]{1,0:T(8,128)(2,1)S(1)}, u32[]{:S(2)}, u32[]{:S(2)}) collective-permute-start(bf16[512,1024]{1,0:T(8,128)(2,1)} %get-tuple-element.55.refs_2_), channel_id=1, source_target_pairs={{0,1},{1,0},{2,3},{3,2},{4,5},{5,4},{6,7},{7,6},{8,9},{9,8},{10,11... | collective-permute-start | bytes 3145736 | tf_op jit(solution)/shard_map/ppermute | solution.py:772
  69.6 0.8 copy-start.10
  69.6 1.0 copy-start.11
  69.6 1.3 copy-start.12
  75.8 3.0 collective-permute-start.6
  76.3 2.5 copy-start.18
  78.8 1.0 copy-start.19
  85.9 27.9 %collective-permute-start.9 = (bf16[288,1024]{1,0:T(8,128)(2,1)}, bf16[288,1024]{1,0:T(8,128)(2,1)S(1)}, u32[]{:S(2)}, u32[]{:S(2)}) collective-permute-start(bf16[288,1024]{1,0:T(8,128)(2,1)} %get-tuple-element.61), channel_id=1, source_target_pairs={{0,2},{1,3},{2,0},{3,1},{4,6},{5,7},{6,4},{7,5},{8,10},{9,11},{10,... | collective-permute-start | bytes 1769480 | tf_op jit(solution)/shard_map/ppermute | solution.py:772
  87.8 47.4 %collective-permute-start.8 = (bf16[288,1024]{1,0:T(8,128)(2,1)}, bf16[288,1024]{1,0:T(8,128)(2,1)S(1)}, u32[]{:S(2)}, u32[]{:S(2)}) collective-permute-start(bf16[288,1024]{1,0:T(8,128)(2,1)} %get-tuple-element.60), channel_id=1, source_target_pairs={{0,4},{1,5},{2,6},{3,7},{4,0},{5,1},{6,2},{7,3},{8,12},{9,13},{10,... | collective-permute-start | bytes 1769480 | tf_op jit(solution)/shard_map/ppermute | solution.py:772
  90.3 59.8 %collective-permute-start.7 = (bf16[288,1024]{1,0:T(8,128)(2,1)}, bf16[288,1024]{1,0:T(8,128)(2,1)S(1)}, u32[]{:S(2)}, u32[]{:S(2)}) collective-permute-start(bf16[288,1024]{1,0:T(8,128)(2,1)} %get-tuple-element.59), channel_id=1, source_target_pairs={{0,6},{1,7},{2,4},{3,5},{4,2},{5,3},{6,0},{7,1},{8,14},{9,15},{10,... | collective-permute-start | bytes 1769480 | tf_op jit(solution)/shard_map/ppermute | solution.py:772
  113.8 0.8 copy-start.7
  135.2 0.9 copy-start.15
  148.7 72.0 %collective-permute-start.14 = (bf16[288,1024]{1,0:T(8,128)(2,1)}, bf16[288,1024]{1,0:T(8,128)(2,1)S(1)}, u32[]{:S(2)}, u32[]{:S(2)}) collective-permute-start(bf16[288,1024]{1,0:T(8,128)(2,1)} %get-tuple-element.67.refs_5_), channel_id=1, source_target_pairs={{0,4},{1,5},{2,6},{3,7},{4,0},{5,1},{6,2},{7,3},{8,12},{9,13},{10,... | collective-permute-start | bytes 1769480 | tf_op jit(solution)/shard_map/ppermute | solution.py:772
  150.2 0.8 copy-start.16
  163.5 57.2 %collective-permute-start.15 = (bf16[288,1024]{1,0:T(8,128)(2,1)}, bf16[288,1024]{1,0:T(8,128)(2,1)S(1)}, u32[]{:S(2)}, u32[]{:S(2)}) collective-permute-start(bf16[288,1024]{1,0:T(8,128)(2,1)} %get-tuple-element.70.refs_3_), channel_id=1, source_target_pairs={{0,6},{1,7},{2,4},{3,5},{4,2},{5,3},{6,0},{7,1},{8,14},{9,15},{10,... | collective-permute-start | bytes 1769480 | tf_op jit(solution)/shard_map/ppermute | solution.py:772
  165.4 55.3 %collective-permute-start.13 = (bf16[288,1024]{1,0:T(8,128)(2,1)}, bf16[288,1024]{1,0:T(8,128)(2,1)}, u32[]{:S(2)}, u32[]{:S(2)}) collective-permute-start(bf16[288,1024]{1,0:T(8,128)(2,1)} %get-tuple-element.75), channel_id=1, source_target_pairs={{0,2},{1,3},{2,0},{3,1},{4,6},{5,7},{6,4},{7,5},{8,10},{9,11},{10,... | collective-permute-start | bytes 1769480 | tf_op jit(solution)/shard_map/ppermute | solution.py:772
  174.0 70.7 %collective-permute-start.18 = (bf16[2,512,1024]{2,1,0:T(8,128)(2,1)}, bf16[2,512,1024]{2,1,0:T(8,128)(2,1)S(1)}, u32[]{:S(2)}, u32[]{:S(2)}) collective-permute-start(bf16[2,512,1024]{2,1,0:T(8,128)(2,1)} %shard_map.182.refs_5_), channel_id=1, source_target_pairs={{0,16},{8,24},{16,0},{24,8},{1,17},{9,25},{17,1},{25,9},{2,18},{10... | collective-permute-start | bytes 6291464 | tf_op jit(solution)/shard_map/ppermute | solution.py:772
  182.5 62.8 %collective-permute-start.17 = (bf16[2,512,1024]{2,1,0:T(8,128)(2,1)}, bf16[2,512,1024]{2,1,0:T(8,128)(2,1)}, u32[]{:S(2)}, u32[]{:S(2)}) collective-permute-start(bf16[2,512,1024]{2,1,0:T(8,128)(2,1)} %shard_map.181.refs_4_), channel_id=1, source_target_pairs={{0,8},{8,0},{16,24},{24,16},{1,9},{9,1},{17,25},{25,17},{2,10},{10... | collective-permute-start | bytes 6291464 | tf_op jit(solution)/shard_map/ppermute | solution.py:772
  220.7 0.8 copy-start.14
  220.7 1.0 copy-start.13
  224.1 3.4 collective-permute-start.16
  224.1 61.6 %collective-permute-start.10 = (bf16[288,1024]{1,0:T(8,128)(2,1)}, bf16[288,1024]{1,0:T(8,128)(2,1)S(1)}, u32[]{:S(2)}, u32[]{:S(2)}) collective-permute-start(bf16[288,1024]{1,0:T(8,128)(2,1)} %get-tuple-element.72), channel_id=1, source_target_pairs={{0,2},{1,3},{2,0},{3,1},{4,6},{5,7},{6,4},{7,5},{8,10},{9,11},{10,... | collective-permute-start | bytes 1769480 | tf_op jit(solution)/shard_map/ppermute | solution.py:772
  225.5 60.2 %collective-permute-start.11 = (bf16[288,1024]{1,0:T(8,128)(2,1)}, bf16[288,1024]{1,0:T(8,128)(2,1)S(1)}, u32[]{:S(2)}, u32[]{:S(2)}) collective-permute-start(bf16[288,1024]{1,0:T(8,128)(2,1)} %get-tuple-element.73), channel_id=1, source_target_pairs={{0,4},{1,5},{2,6},{3,7},{4,0},{5,1},{6,2},{7,3},{8,12},{9,13},{10,... | collective-permute-start | bytes 1769480 | tf_op jit(solution)/shard_map/ppermute | solution.py:772
  227.5 58.2 %collective-permute-start.12 = (bf16[288,1024]{1,0:T(8,128)(2,1)}, bf16[288,1024]{1,0:T(8,128)(2,1)}, u32[]{:S(2)}, u32[]{:S(2)}) collective-permute-start(bf16[288,1024]{1,0:T(8,128)(2,1)} %get-tuple-element.74), channel_id=1, source_target_pairs={{0,6},{1,7},{2,4},{3,5},{4,2},{5,3},{6,0},{7,1},{8,14},{9,15},{10,... | collective-permute-start | bytes 1769480 | tf_op jit(solution)/shard_map/ppermute | solution.py:772
  244.7 1.4 copy-start.1
  244.7 97.0 %collective-permute-start.21 = (bf16[2,512,1024]{2,1,0:T(8,128)(2,1)}, bf16[2,512,1024]{2,1,0:T(8,128)(2,1)}, u32[]{:S(2)}, u32[]{:S(2)}) collective-permute-start(bf16[2,512,1024]{2,1,0:T(8,128)(2,1)} %shard_map.189.refs_11_), channel_id=1, source_target_pairs={{0,16},{8,24},{16,0},{24,8},{1,17},{9,25},{17,1},{25,9},{2,18},{10... | collective-permute-start | bytes 6291464 | tf_op jit(solution)/shard_map/ppermute | solution.py:772
  285.7 0.8 copy-start.8
  285.7 1.1 copy-start.9
  321.3 47.7 %collective-permute-start.20 = (bf16[2,512,1024]{2,1,0:T(8,128)(2,1)}, bf16[2,512,1024]{2,1,0:T(8,128)(2,1)}, u32[]{:S(2)}, u32[]{:S(2)}) collective-permute-start(bf16[2,512,1024]{2,1,0:T(8,128)(2,1)} %shard_map.188.refs_10_), channel_id=1, source_target_pairs={{0,8},{8,0},{16,24},{24,16},{1,9},{9,1},{17,25},{25,17},{2,10},{10... | collective-permute-start | bytes 6291464 | tf_op jit(solution)/shard_map/ppermute | solution.py:772
  336.3 2.9 copy-start
  337.9 34.1 %collective-permute-start.36 = (bf16[2,2,2,2,128,512]{5,4,2,3,1,0:T(8,128)(2,1)}, bf16[2,2,2,2,128,512]{5,4,2,3,1,0:T(8,128)(2,1)}, u32[]{:S(2)}, u32[]{:S(2)}) collective-permute-start(bf16[2,2,2,2,128,512]{5,4,2,3,1,0:T(8,128)(2,1)} %bitcast.81), channel_id=1, source_target_pairs={{0,1},{1,0},{2,3},{3,2},{4,5},{5,4},{6,7},{7,6},{8,9},{9,8},{10,11... | collective-permute-start | bytes 6291464 | tf_op jit(solution)/shard_map/ppermute | solution.py:772
  341.0 37.2 %collective-permute-start.31 = (bf16[2,2,2,2,128,512]{5,4,2,3,0,1:T(8,128)(2,1)}, bf16[2,2,2,2,128,512]{5,4,2,3,0,1:T(8,128)(2,1)}, u32[]{:S(2)}, u32[]{:S(2)}) collective-permute-start(bf16[2,2,2,2,128,512]{5,4,2,3,0,1:T(8,128)(2,1)} %bitcast.82), channel_id=1, source_target_pairs={{0,1},{1,0},{2,3},{3,2},{4,5},{5,4},{6,7},{7,6},{8,9},{9,8},{10,11... | collective-permute-start | bytes 6291464 | tf_op jit(solution)/shard_map/ppermute | solution.py:772
  341.0 34.5 %collective-permute-start.25 = (bf16[1,512,1024]{2,1,0:T(8,128)(2,1)}, bf16[1,512,1024]{2,1,0:T(8,128)(2,1)}, u32[]{:S(2)}, u32[]{:S(2)}) collective-permute-start(bf16[1,512,1024]{2,1,0:T(8,128)(2,1)} %shard_map.193.refs_9_), channel_id=1, source_target_pairs={{0,16},{8,24},{16,0},{24,8},{1,17},{9,25},{17,1},{25,9},{2,18},{10... | collective-permute-start | bytes 3145736 | tf_op jit(solution)/shard_map/ppermute | solution.py:772
  341.8 42.0 %collective-permute-start.19 = (bf16[576,1024]{1,0:T(8,128)(2,1)}, bf16[576,1024]{1,0:T(8,128)(2,1)}, u32[]{:S(2)}, u32[]{:S(2)}) collective-permute-start(bf16[576,1024]{1,0:T(8,128)(2,1)} %shard_map.192), channel_id=1, source_target_pairs={{0,1},{1,0},{2,3},{3,2},{4,5},{5,4},{6,7},{7,6},{8,9},{9,8},{10,11... | collective-permute-start | bytes 3538952 | tf_op jit(solution)/shard_map/ppermute | solution.py:772
  369.0 39.9 %collective-permute-start.24 = (bf16[1,512,1024]{2,1,0:T(8,128)(2,1)}, bf16[1,512,1024]{2,1,0:T(8,128)(2,1)}, u32[]{:S(2)}, u32[]{:S(2)}) collective-permute-start(bf16[1,512,1024]{2,1,0:T(8,128)(2,1)} %shard_map.194.refs_10_), channel_id=1, source_target_pairs={{0,8},{8,0},{16,24},{24,16},{1,9},{9,1},{17,25},{25,17},{2,10},{10... | collective-permute-start | bytes 3145736 | tf_op jit(solution)/shard_map/ppermute | solution.py:772
  372.0 40.1 %collective-permute-start.23 = (bf16[1,512,1024]{2,1,0:T(8,128)(2,1)}, bf16[1,512,1024]{2,1,0:T(8,128)(2,1)}, u32[]{:S(2)}, u32[]{:S(2)}) collective-permute-start(bf16[1,512,1024]{2,1,0:T(8,128)(2,1)} %shard_map.200.refs_5_), channel_id=1, source_target_pairs={{0,16},{8,24},{16,0},{24,8},{1,17},{9,25},{17,1},{25,9},{2,18},{10... | collective-permute-start | bytes 3145736 | tf_op jit(solution)/shard_map/ppermute | solution.py:772
  372.5 3.0 copy-start.6
  375.5 6.5 %copy-start.2 = (bf16[2,2,2,2,128,512]{5,4,2,3,1,0:T(8,128)(2,1)}, bf16[2,2,2,2,128,512]{5,4,2,3,1,0:T(8,128)(2,1)S(1)}, u32[]{:S(2)}) copy-start(bf16[2,2,2,2,128,512]{5,4,2,3,1,0:T(8,128)(2,1)S(1)} %fusion) | copy-start | bytes 6291460
  375.5 42.4 %collective-permute-start.22 = (bf16[1,512,1024]{2,1,0:T(8,128)(2,1)S(1)}, bf16[1,512,1024]{2,1,0:T(8,128)(2,1)}, u32[]{:S(2)}, u32[]{:S(2)}) collective-permute-start(bf16[1,512,1024]{2,1,0:T(8,128)(2,1)S(1)} %copy-done.6), channel_id=1, source_target_pairs={{0,8},{8,0},{16,24},{24,16},{1,9},{9,1},{17,25},{25,17},{2,10},{10... | collective-permute-start | bytes 3145736 | tf_op jit(solution)/shard_map/ppermute | solution.py:772
  378.2 74.5 %collective-permute-start.37 = (bf16[2,2,2,128,512]{4,3,1,2,0:T(8,128)(2,1)}, bf16[2,2,2,128,512]{4,3,1,2,0:T(8,128)(2,1)}, u32[]{:S(2)}, u32[]{:S(2)}) collective-permute-start(bf16[2,2,2,128,512]{4,3,1,2,0:T(8,128)(2,1)} %dynamic-slice_bitcast_fusion), channel_id=1, source_target_pairs={{0,16},{8,24},{16,0},{24,8},{1,17},{9,25},{17,1},{25,9},{2,18},{10... | collective-permute-start | bytes 3145736 | tf_op jit(solution)/shard_map/ppermute | solution.py:772
  382.0 1.8 copy-start.4
  383.7 71.2 %collective-permute-start.32 = (bf16[2,2,2,128,512]{4,3,1,2,0:T(8,128)(2,1)}, bf16[2,2,2,128,512]{4,3,1,2,0:T(8,128)(2,1)}, u32[]{:S(2)}, u32[]{:S(2)}) collective-permute-start(bf16[2,2,2,128,512]{4,3,1,2,0:T(8,128)(2,1)} %dynamic-slice_bitcast_fusion.1), channel_id=1, source_target_pairs={{0,8},{8,0},{16,24},{24,16},{1,9},{9,1},{17,25},{25,17},{2,10},{10... | collective-permute-start | bytes 3145736 | tf_op jit(solution)/shard_map/ppermute | solution.py:772
  420.8 31.8 %copy-start.3 = (bf16[2,2,2,2,128,512]{5,4,2,3,1,0:T(8,128)(2,1)S(1)}, bf16[2,2,2,2,128,512]{5,4,2,3,1,0:T(8,128)(2,1)}, u32[]{:S(2)}) copy-start(bf16[2,2,2,2,128,512]{5,4,2,3,1,0:T(8,128)(2,1)} %copy-done.2) | copy-start | bytes 6291460
  422.3 16.2 %collective-permute-start.26 = (f32[4,1024]{1,0:T(4,128)}, f32[4,1024]{1,0:T(4,128)S(1)}, u32[]{:S(2)}, u32[]{:S(2)}) collective-permute-start(f32[4,1024]{1,0:T(4,128)} %shard_map.208), channel_id=1, source_target_pairs={{0,8},{8,0},{16,24},{24,16},{1,9},{9,1},{17,25},{25,17},{2,10},{10... | collective-permute-start | bytes 49160 | tf_op jit(solution)/shard_map/ppermute | solution.py:772
  439.3 3.7 collective-permute-start.27
  443.0 1.2 collective-permute-start.28
  444.2 3.7 collective-permute-start.29
  447.9 4.6 collective-permute-start.30
  452.7 2.3 copy-start.5
  454.4 11.8 %collective-permute-start.38 = (bf16[2,2,128,512]{3,2,0,1:T(8,128)(2,1)S(1)}, bf16[2,2,128,512]{3,2,0,1:T(8,128)(2,1)S(1)}, u32[]{:S(2)}, u32[]{:S(2)}) collective-permute-start(bf16[2,2,128,512]{3,2,0,1:T(8,128)(2,1)S(1)} %dynamic-slice_bitcast_fusion.2), channel_id=1, source_target_pairs={{0,8},{8,0},{16,24},{24,16},{1,9},{9,1},{17,25},{25,17},{2,10},{10... | collective-permute-start | bytes 1572872 | tf_op jit(solution)/shard_map/ppermute | solution.py:772
  456.6 11.5 %collective-permute-start.33 = (bf16[2,2,128,512]{3,2,0,1:T(8,128)(2,1)S(1)}, bf16[2,2,128,512]{3,2,0,1:T(8,128)(2,1)S(1)}, u32[]{:S(2)}, u32[]{:S(2)}) collective-permute-start(bf16[2,2,128,512]{3,2,0,1:T(8,128)(2,1)S(1)} %dynamic-slice_bitcast_fusion.3), channel_id=1, source_target_pairs={{0,16},{8,24},{16,0},{24,8},{1,17},{9,25},{17,1},{25,9},{2,18},{10... | collective-permute-start | bytes 1572872 | tf_op jit(solution)/shard_map/ppermute | solution.py:772
  466.3 9.4 %collective-permute-start.39 = (bf16[2,128,512]{2,1,0:T(8,128)(2,1)S(1)}, bf16[2,128,512]{2,1,0:T(8,128)(2,1)S(1)}, u32[]{:S(2)}, u32[]{:S(2)}) collective-permute-start(bf16[2,128,512]{2,1,0:T(8,128)(2,1)S(1)} %dynamic-slice_bitcast_fusion.4), channel_id=1, source_target_pairs={{0,2},{1,3},{2,0},{3,1},{4,6},{5,7},{6,4},{7,5},{8,10},{9,11},{10,... | collective-permute-start | bytes 786440 | tf_op jit(solution)/shard_map/ppermute | solution.py:772
  468.2 10.7 %collective-permute-start.34 = (bf16[2,128,512]{2,1,0:T(8,128)(2,1)S(1)}, bf16[2,128,512]{2,1,0:T(8,128)(2,1)S(1)}, u32[]{:S(2)}, u32[]{:S(2)}) collective-permute-start(bf16[2,128,512]{2,1,0:T(8,128)(2,1)S(1)} %dynamic-slice_bitcast_fusion.5), channel_id=1, source_target_pairs={{0,2},{1,3},{2,0},{3,1},{4,6},{5,7},{6,4},{7,5},{8,10},{9,11},{10,... | collective-permute-start | bytes 786440 | tf_op jit(solution)/shard_map/ppermute | solution.py:772
  475.9 7.5 %collective-permute-start.40 = (bf16[128,512]{1,0:T(8,128)(2,1)S(1)}, bf16[128,512]{1,0:T(8,128)(2,1)S(1)}, u32[]{:S(2)}, u32[]{:S(2)}) collective-permute-start(bf16[128,512]{1,0:T(8,128)(2,1)S(1)} %dynamic-slice_bitcast_fusion.6), channel_id=1, source_target_pairs={{0,4},{1,5},{2,6},{3,7},{4,0},{5,1},{6,2},{7,3},{8,12},{9,13},{10,... | collective-permute-start | bytes 393224 | tf_op jit(solution)/shard_map/ppermute | solution.py:772
  479.0 7.3 %collective-permute-start.35 = (bf16[128,512]{1,0:T(8,128)(2,1)S(1)}, bf16[128,512]{1,0:T(8,128)(2,1)S(1)}, u32[]{:S(2)}, u32[]{:S(2)}) collective-permute-start(bf16[128,512]{1,0:T(8,128)(2,1)S(1)} %dynamic-slice_bitcast_fusion.7), channel_id=1, source_target_pairs={{0,4},{1,5},{2,6},{3,7},{4,0},{5,1},{6,2},{7,3},{8,12},{9,13},{10,... | collective-permute-start | bytes 393224 | tf_op jit(solution)/shard_map/ppermute | solution.py:772
